TPU v7x, 32 devices: a whole 2x2x4 slice. The times are simulated.
32 devices in a mesh: groups: 2 (over x), tile: 16 (over z, y, core).
Axes of the slice: x: 2, y: 2, z: 4, core: 2. Of those that a mesh axis runs over, the one named last changes fastest.
Arguments:
- features: bfloat16 [128, 256, 2048], P(('groups', 'tile')), parts along dimension 0, may hold values from -0.5 to 0.5
- gauge_offset: int32 [128, 384], P(('groups', 'tile')), parts along dimension 0, may hold values from 0 to 248
- gauge_count: int32 [128], P(('groups', 'tile')), parts along dimension 0, may hold values from 1 to 384, as said below
- gauge_resid: bfloat16 [128, 384], P(('groups', 'tile')), parts along dimension 0, may hold values from -6 to 6
- damping: float32 [4096], P('groups'), parts along dimension 0, may hold values from 0.5 to 2
Outputs:
- panel_factor: float32 [512, 256], P('groups'), parts along dimension 0
- lower_trail: float32 [3584, 256], P(('groups', 'tile')), parts along dimension 0
- schur: float32 [3584, 1792], P(('groups', 'tile')), parts along dimension 0
- panel_rhs: float32 [512], P('groups'), parts along dimension 0
- trail_rhs: float32 [3584], P(('groups', 'tile')), parts along dimension 0
There are 2 independent parts, one for each index of `groups`. A program takes and returns all parts, laid end to end along the dimension named above; each array names one. Nothing has to cross between parts.
Inputs may be any that keep to these rules, and one draw needn't show every extreme that they name: `gauge_count`: the counts of the 4 tiles of one device sum to at most 768; in every draw some device reaches that sum, and some tile has 384 live gauges.
All inputs are finite; a program needn't handle non-finite values.
Results may differ from a plain program's by a relative error of at most 0.0033.
Values sent between devices are 32-bit elements; how exact they have to be, the bound alone decides.
No kernel may reach another device: no remote copies, remote signals or barrier semaphores. Data moves between devices by JAX's collectives and lax.ppermute only.
A program may use at most 128 MiB of HBM per device.

v0:
```python
import jax
import jax.numpy as jnp
from jax import lax
from jax.sharding import PartitionSpec as P

LWIN = 8


def per_device(features, gauge_offset, gauge_count, gauge_resid, damping):
    tiles_here, samples, params = features.shape
    slots = gauge_offset.shape[1]
    panel = params // 8
    trail = params - panel
    rows_here = tiles_here * slots
    slot_ids = lax.broadcasted_iota(jnp.int32, (tiles_here, slots), 1)
    live = slot_ids < gauge_count[:, None]
    sample_ids = lax.broadcasted_iota(jnp.int32, (tiles_here, slots, samples), 2)
    starts = gauge_offset[:, :, None]
    inside = (sample_ids >= starts) & (sample_ids < starts + LWIN) & live[:, :, None]
    window = jnp.where(inside, 1.0 / LWIN, 0.0).astype(jnp.bfloat16)
    jac = jnp.einsum("tgw,twp->tgp", window, features, preferred_element_type=jnp.float32)
    jac = jac.astype(jnp.bfloat16).reshape(rows_here, params)
    resid = jnp.where(live, gauge_resid, jnp.zeros_like(gauge_resid)).reshape(rows_here)
    grad_local = jnp.dot(resid, jac, preferred_element_type=jnp.float32)
    width = lax.axis_size("tile")
    owned = params // width
    owned_trail = owned - owned // 8
    index = lax.axis_index("tile")
    gauges = jac.shape[0]
    jac_split = jac.reshape(gauges, panel, 8)
    jac_panel = jac_split[:, :, 0]
    jac_trail = jac_split[:, :, 1:].reshape(gauges, trail)
    panel_local = lax.dot_general(
        jac, jac_panel, (((0,), (0,)), ((), ())), preferred_element_type=jnp.float32
    )
    panel_all, grad = lax.psum((panel_local, grad_local), "tile")
    own_trail = lax.psum_scatter(
        lax.dot_general(
            jac_trail, jac_trail, (((0,), (0,)), ((), ())), preferred_element_type=jnp.float32
        ),
        "tile",
        scatter_dimension=0,
        tiled=True,
    )
    damp_split = damping.reshape(panel, 8)
    damp_trail = damp_split[:, 1:].reshape(trail)
    trail_ids = index * owned_trail + lax.broadcasted_iota(jnp.int32, (owned_trail, trail), 0)
    column_ids = lax.broadcasted_iota(jnp.int32, (owned_trail, trail), 1)
    own_trail = own_trail + jnp.where(trail_ids == column_ids, damp_trail[None, :], 0.0)
    panel_split = panel_all.reshape(panel, 8, panel)
    n11 = panel_split[:, 0, :] + jnp.diag(damp_split[:, 0])
    n21 = panel_split[:, 1:, :].reshape(trail, panel)
    panel_factor = jnp.linalg.cholesky(n11)
    lower_all = lax.linalg.triangular_solve(
        panel_factor, n21, left_side=False, lower=True, transpose_a=True
    )
    lower_own = lax.dynamic_slice_in_dim(lower_all, index * owned_trail, owned_trail, 0)
    schur = own_trail - jnp.dot(lower_own, lower_all.T, precision=lax.Precision.HIGHEST)
    grad_split = grad.reshape(panel, 8)
    first_part = grad_split[:, 0]
    second_part = grad_split[:, 1:].reshape(trail)
    panel_rhs = lax.linalg.triangular_solve(
        panel_factor, first_part[:, None], left_side=True, lower=True
    )[:, 0]
    second_own = lax.dynamic_slice_in_dim(second_part, index * owned_trail, owned_trail, 0)
    trail_rhs = second_own - jnp.dot(lower_own, panel_rhs, precision=lax.Precision.HIGHEST)
    return (panel_factor, lower_own, schur, panel_rhs, trail_rhs)


def solution(mesh):
    return jax.shard_map(
        per_device,
        mesh=mesh,
        in_specs=(
            P(("groups", "tile"), None, None),
            P(("groups", "tile"), None),
            P(("groups", "tile")),
            P(("groups", "tile"), None),
            P("groups"),
        ),
        out_specs=(
            P("groups", None),
            P(("groups", "tile"), None),
            P(("groups", "tile"), None),
            P("groups"),
            P(("groups", "tile")),
        ),
        check_vma=False,
    )
```

profile of v0, /device:TPU:1, one launch (start us, length us, event | category | flops | bytes accessed | tf_op | source)
XLA Modules:
  0.0 298.2 jit_solution(8102636046108234531)
XLA Ops:
  7.2 0.7 iota_compare_fusion.7
  8.6 6.2 %convolution_convert_fusion = bf16[4,384,2048]{2,1,0:T(8,128)(2,1)} fusion(bf16[4,256,2048]{2,1,0:T(8,128)(2,1)} %param.5, s32[4,384]{1,0:T(4,128)S(1)} %broadcast_add_fusion, s32[4,384]{1,0:T(4,128)} %param.6, pred[4,384]{1,0:T(4,128)(4,1)S(1)} %iota_compare_fusion.7), kind=kOutput, calls=%fused_computation.2 | convolution fusion | flops 1616117760 | bytes 10499584 | tf_op jit(solution)/shard_map/tgw,twp->tgp/dot_general | solution.py:21
  14.8 10.8 %copy.29 = bf16[4,384,2048]{1,0,2:T(4,128)(2,1)} copy(bf16[4,384,2048]{2,1,0:T(8,128)(2,1)} %convolution_convert_fusion) | data formatting | bytes 12582912 | tf_op jit(solution)/shard_map/convert_element_type | solution.py:22
  25.6 11.0 %reshape_reshape.3 = bf16[1536,256,8]{0,2,1:T(8,128)(2,1)} reshape(bf16[4,384,2048]{1,0,2:T(4,128)(2,1)} %copy.29) | data formatting | bytes 12582912 | tf_op jit(solution)/shard_map/reshape;reshape | solution.py:30
  36.6 3.6 %slice.94 = bf16[1536,256,1]{0,2,1:T(2,128)(2,1)S(1)} slice(bf16[1536,256,8]{0,2,1:T(8,128)(2,1)} %reshape_reshape.3), slice={[0:1536], [0:256], [0:1]} | slice | bytes 1572864 | tf_op jit(solution)/shard_map/slice | solution.py:31
  40.2 1.4 copy.30
  41.6 4.7 %convolution_bitcast_fusion = f32[256,8,256]{2,1,0:T(8,128)S(1)} fusion(bf16[1536,2048]{1,0:T(8,128)(2,1)} %bitcast.84, bf16[1536,256,1]{1,0,2:T(8,128)(2,1)S(1)} %copy.30), kind=kOutput, calls=%fused_computation.8 | convolution fusion | flops 1610612736 | bytes 9175040 | tf_op jit(solution)/shard_map/dot_general | solution.py:33
  46.2 1.8 copy.31
  48.1 6.9 %slice.98 = bf16[1536,256,7]{0,2,1:T(8,128)(2,1)} slice(bf16[1536,256,8]{0,2,1:T(8,128)(2,1)} %reshape_reshape.3), slice={[0:1536], [0:256], [1:8]} | slice | bytes 11010048 | tf_op jit(solution)/shard_map/slice | solution.py:32
  55.1 9.5 %reshape.91 = bf16[1536,1792]{0,1:T(8,128)(2,1)} reshape(bf16[1536,256,7]{0,2,1:T(8,128)(2,1)} %slice.98) | data formatting | bytes 11010048 | tf_op jit(solution)/shard_map/reshape | solution.py:32
  64.6 17.1 %fusion.31 = f32[1792,1792]{1,0:T(8,128)} fusion(bf16[1536,1792]{0,1:T(8,128)(2,1)} %reshape.91), kind=kOutput, calls=%fused_computation.73 | convolution fusion | flops 9865003008 | bytes 18350080 | tf_op jit(solution)/shard_map/dot_general | solution.py:38
  82.9 3.7 %fusion.23 = f32[1,2048,1]{1,0,2:T(1,128)S(1)} fusion(bf16[4,384,2048]{2,1,0:T(8,128)(2,1)} %convolution_convert_fusion, bf16[4,384,1]{1,0,2:T(4,128)(2,1)S(1)} %select_bitcast_fusion.1), kind=kOutput, calls=%fused_computation.55 | convolution fusion | flops 6291456 | bytes 6302720 | tf_op jit(solution)/shard_map/dot_general | solution.py:24
  86.7 59.6 %psum.15 = f32[256,8]{1,0:T(8,128)S(1)} all-reduce(f32[256,8]{1,0:T(8,128)S(1)} %reshape.92), channel_id=1, replica_groups=mesh['groups'=2,'tile'=16] {'tile'}, use_global_device_ids=true, to_apply=%region_6.7 | all-reduce | flops 2048 | bytes 16384 | tf_op jit(solution)/shard_map/psum | solution.py:36
  147.3 1.0 fusion.13
  148.4 1.0 fusion.14
  149.4 11.7 %cholesky.49 = f32[128,128]{1,0:T(8,128)S(1)} custom-call(f32[128,128]{1,0:T(8,128)S(1)} %cholesky.115), custom_call_target="Cholesky" | custom-call | tf_op jit(solution)/shard_map/jit(cholesky)/cholesky | solution.py:53
  161.3 9.8 %custom-call.16 = f32[1,128,128]{1,2,0:T(8,128)S(1)} custom-call(f32[1,128,128]{2,1,0:T(8,128)S(1)} %get-tuple-element.53), custom_call_target="InvertDiagBlocksLowerTriangular" | custom-call | tf_op jit(solution)/shard_map/jit(cholesky)/cholesky | solution.py:53
  171.7 11.7 %cholesky.103 = f32[128,128]{1,0:T(8,128)S(1)} custom-call(f32[128,128]{1,0:T(8,128)S(1)} %convolution_subtract_fusion.2), custom_call_target="Cholesky" | custom-call | tf_op jit(solution)/shard_map/jit(cholesky)/cholesky | solution.py:53
  185.6 0.8 copy.39
  186.5 4.2 %while.1 = (s32[]{:T(128)}, f32[256,256]{0,1:T(8,128)S(1)}, s32[2,2]{1,0:T(2,128)S(1)}, f32[2,128,128]{2,1,0:T(8,128)S(1)}, s32[]{:T(128)}) while((s32[]{:T(128)}, f32[256,256]{0,1:T(8,128)S(1)}, s32[2,2]{1,0:T(2,128)S(1)}, f32[2,128,128]{2,1,0:T(8,128)S(1)}, s32[]{:T(128)}) %tuple.32), condition=%wide.while_cond, body=%wide.while_body.sunk | while | flops 2 | bytes 393329 | solution.py:54
  187.1 1.4 dynamic-slice.7
  189.2 1.4 dynamic-slice.7
  190.8 19.9 %custom-call.17 = f32[2,128,128]{1,2,0:T(8,128)S(1)} custom-call(f32[2,128,128]{2,1,0:T(8,128)S(1)} %get-tuple-element.12), custom_call_target="InvertDiagBlocksLowerTriangular" | custom-call | tf_op jit(solution)/shard_map/triangular_solve | solution.py:54
  210.7 1.4 slice.97
  212.1 2.2 copy.36
  214.3 1.5 reshape.90
  215.8 2.3 fusion.5
  218.1 1.6 convolution_subtract_fusion
  219.7 0.9 fusion.20
  220.8 0.7 copy.40
  223.5 64.8 %reduce-scatter.2.cloned.1.call-done = f32[112,1792]{1,0:T(8,128)} async-done(((f32[1792,1792]{1,0:T(8,128)}), f32[112,1792]{1,0:T(8,128)}) %reduce-scatter.2.cloned.1.call-update) | async-done | bytes 802832 | tf_op jit(solution)/shard_map/reduce_scatter | solution.py:37
  288.3 3.1 %convolution_subtract_fusion.1 = f32[112,1792]{1,0:T(8,128)} fusion(f32[112,256]{0,1:T(8,128)S(1)} %fusion.16, f32[1792,128]{0,1:T(8,128)S(1)} %fusion.20, f32[1792,128]{0,1:T(8,128)S(1)} %fusion.5, f32[112,1792]{1,0:T(8,128)} %reduce-scatter.2.cloned.1.call-done, f32[1792]{0:T(1024)S(1)} %broadcast_in_dim.55, s32[112]{0:T(128)S(1)} %iota_add_fusion), kind=kOutput, calls=%fused_computation.4 | convolution fusion | flops 617824256 | bytes 3562944 | tf_op jit(solution)/shard_map/dot_general | solution.py:58
  (57 shorter events, 8.2 us)
Async XLA Ops:
  7.2 140.2 %all-reduce.3.cloned.1.call-start = ((), (), s32[]{:S(2)}) async-start(), calls=%async_computation.1 | async-start | bytes 4194304 | tf_op jit(solution)/shard_map/psum | solution.py:36
  48.1 240.2 %reduce-scatter.2.cloned.1.call-start = ((), (), s32[]{:S(2)}) async-start(), calls=%async_computation.2 | async-start | bytes 13647872 | tf_op jit(solution)/shard_map/reduce_scatter | solution.py:37
  81.7 0.7 copy-start.2
  81.7 1.1 copy-start.3
  81.7 1.1 copy-start.4
  183.5 27.2 %copy-start.1 = (f32[256,8,256]{0,2,1:T(8,128)S(1)}, f32[256,8,256]{0,2,1:T(8,128)}, u32[]{:S(2)}) copy-start(f32[256,8,256]{0,2,1:T(8,128)} %all-reduce.3.cloned.1.call-done) | copy-start | bytes 6291460
  215.8 2.3 copy-start
Sparse Core Ops, SparseCore 0:
  48.2 99.0 all-reduce.2
  151.9 136.2 reduce-scatter.1
where the time goes:
time: 301 us; the launch traced here: 298 us
  waiting for transfers between devices  65.2 us (22%)
  blocking collectives  59.6 us (20%)
  other arithmetic  58.1 us (19%)
  local copies, waits for them, and re-layouts  58 us (19%)
  matrix products  41.5 us (14%)
  between operations  15.6 us (5%)
    reduce_scatter x1, waiting for transfers between devices, per_device(): lax.psum_scatter(lax.dot_general(jac_trail, jac_trail, (((0,), (0,)), (()...  64.8 us
    psum x1, blocking collectives, per_device(): panel_all, grad = lax.psum((panel_local, grad_local), 'tile')  59.6 us
    another operation x6, other arithmetic, per_device(): panel_factor = jnp.linalg.cholesky(n11)  33.9 us
    another operation x4, other arithmetic, per_device(): lax.linalg.triangular_solve(panel_factor, n21, left_side=False, lower=Tru...  20.1 us
    dot_general x1, matrix products, per_device(): lax.dot_general(jac_trail, jac_trail, (((0,), (0,)), ((), ())), preferred...  17.1 us
    another operation x1, local copies, waits for them, and re-layouts, per_device(): jac_split = jac.reshape(gauges, panel, 8)  11 us
    convert_element_type x1, local copies, waits for them, and re-layouts, per_device(): jac = jac.astype(jnp.bfloat16).reshape(rows_here, params)  10.8 us
    reshape x1, local copies, waits for them, and re-layouts, per_device(): jac_trail = jac_split[:, :, 1:].reshape(gauges, trail)  9.5 us
  transfers between devices with their start and end apart: 2, of which 2 were waited for; matrix products, arithmetic and copies ran while one was open for 38% of the time, Pallas kernels for 0%

commit v1 on v0

--- a/solution.py
+++ b/solution.py
@@ -1,12 +1,344 @@
+import functools
+
 import jax
 import jax.numpy as jnp
 from jax import lax
+from jax.experimental import pallas as pl
+from jax.experimental.pallas import tpu as pltpu
 from jax.sharding import PartitionSpec as P
 
 LWIN = 8
+STRIDE = 8
+BLK = 256
+EXACT = lax.Precision.HIGHEST
+VMEM_LIMIT = 56 * 2**20
+
+SMEM_SPEC = pl.BlockSpec(memory_space=pltpu.SMEM)
+VMEM_SPEC = pl.BlockSpec(memory_space=pltpu.VMEM)
+NT = (((1,), (1,)), ((), ()))
+
+
+def f32(*shape):
+    return jax.ShapeDtypeStruct(shape, jnp.float32)
+
+
+def bf16(*shape):
+    return jax.ShapeDtypeStruct(shape, jnp.bfloat16)
+
+
+def dot_nt(a, b, precision=None):
+    return lax.dot_general(a, b, NT, precision=precision, preferred_element_type=jnp.float32)
+
+
+def call(kernel, ins, out_shape, scratch=(), flops=0, moved=0):
+    return pl.pallas_call(
+        kernel,
+        out_shape=out_shape,
+        in_specs=[SMEM_SPEC if x.dtype == jnp.int32 and x.ndim == 1 else VMEM_SPEC for x in ins],
+        out_specs=jax.tree.map(lambda _: VMEM_SPEC, out_shape),
+        scratch_shapes=list(scratch),
+        compiler_params=pltpu.CompilerParams(vmem_limit_bytes=VMEM_LIMIT),
+        cost_estimate=pl.CostEstimate(flops=flops, bytes_accessed=moved, transcendentals=0),
+    )(*ins)
+
+
+def owner_of(m, order):
+    last = len(order) - 1
+    return sum(((m >> (last - k)) & 1) << bit for k, bit in enumerate(order))
+
+
+def front_kernel(order, me_ref, count_ref, offset_ref, resid_ref, feat_ref, sent_ref, kept_ref, pan_sent_ref, jt_ref, jp_ref, r_ref, n11_ref):
+    tiles, slots = offset_ref.shape
+    depth, params = feat_ref.shape
+    samples = depth // tiles
+    cap = jp_ref.shape[1]
+    panel = jp_ref.shape[0]
+    trail = params - panel
+    core = me_ref[0] & 1
+    lane = lax.broadcasted_iota(jnp.int32, (8, cap), 1)
+    start = jnp.full((8, cap), -depth, jnp.int32)
+    resid = jnp.zeros((8, cap), jnp.float32)
+    before = jnp.int32(0)
+    for t in range(tiles):
+        count = count_ref[t]
+        live = (lane >= before) & (lane < before + count)
+        offs = jnp.concatenate([offset_ref[t : t + 1, :], jnp.zeros((1, cap - slots), jnp.int32)], axis=1)
+        offs = pltpu.roll(jnp.broadcast_to(offs, (8, cap)), before, 1)
+        res = jnp.concatenate([resid_ref[t : t + 1, :].astype(jnp.float32), jnp.zeros((1, cap - slots), jnp.float32)], axis=1)
+        res = pltpu.roll(jnp.broadcast_to(res, (8, cap)), before, 1)
+        start = jnp.where(live, offs + t * samples, start)
+        resid = jnp.where(live, res, resid)
+        before = before + count
+    first = lax.broadcasted_iota(jnp.int32, (8, cap), 0) == 0
+    resid = jnp.where(first, resid, 0.0).astype(jnp.bfloat16)
+    r_ref[...] = jnp.concatenate([resid, jnp.zeros((8, cap), jnp.bfloat16)], axis=0)
+    after = lax.broadcasted_iota(jnp.int32, (depth, cap), 0) - start[0:1, :]
+    window = jnp.where((after >= 0) & (after < LWIN), 1.0 / LWIN, 0.0).astype(jnp.bfloat16)
+    pan_b = BLK // STRIDE
+    row = lax.broadcasted_iota(jnp.int32, (BLK, BLK), 0)
+    col = lax.broadcasted_iota(jnp.int32, (BLK, BLK), 1)
+    rest = row - pan_b
+    source = jnp.where(row < pan_b, row * STRIDE, rest + 1 + ((rest * 9363) >> 16))
+    pick = jnp.where(source == col, 1.0, 0.0).astype(jnp.bfloat16)
+    trail_b = BLK - pan_b
+    for b in range(params // BLK):
+        turned = dot_nt(pick, feat_ref[:, b * BLK : (b + 1) * BLK]).astype(jnp.bfloat16)
+        jac = jnp.dot(turned, window, preferred_element_type=jnp.float32).astype(jnp.bfloat16)
+        jp_ref[b * pan_b : (b + 1) * pan_b, :] = jac[:pan_b]
+        jt_ref[b * trail_b : (b + 1) * trail_b, :] = jac[pan_b:]
+        if trail + (b + 1) * trail_b <= jt_ref.shape[0]:
+            jt_ref[trail + b * trail_b : trail + (b + 1) * trail_b, :] = jac[pan_b:]
+    jp = jp_ref[...]
+    n11_ref[:panel, :] = dot_nt(jp, jp)
+    n11_ref[panel:, :] = dot_nt(r_ref[...], jp)
+    half = kept_ref.shape[0]
+    kept_ref[...] = n11_ref[pl.ds(pl.multiple_of(core * half, 8), half), :]
+    sent_ref[...] = n11_ref[pl.ds(pl.multiple_of((1 - core) * half, 8), half), :]
+    panel_part(order, 1 - core, jt_ref, jp_ref, pan_sent_ref)
+
+
+def panel_part(order, core, jt_ref, jp_ref, out_ref):
+    own = out_ref.shape[1]
+
+    def step(m, carry):
+        owner = owner_of(m, order) + core
+        rows = jt_ref[pl.ds(pl.multiple_of(owner * own, 16), own), :]
+        out_ref[m] = dot_nt(rows, jp_ref[...])
+        return carry
+
+    lax.fori_loop(0, out_ref.shape[0], step, 0)
+
+
+def trail_part(orders, core, jt_ref, r_ref, out_refs):
+    own, wide = out_refs[0].shape[1:]
+    last = len(out_refs) - 1
+    extra = r_ref.shape[0]
+
+    def step(m, carry):
+        for q, out_ref in enumerate(out_refs):
+            base = (owner_of(m, orders[q]) + core) * own
+            rows = jt_ref[pl.ds(pl.multiple_of(base, 16), own), :]
+            if q < last:
+                others = jt_ref[pl.ds(pl.multiple_of(base + q * wide, 16), wide), :]
+            else:
+                others = jt_ref[pl.ds(pl.multiple_of(base + q * wide, 16), wide - extra), :]
+                others = jnp.concatenate([others, r_ref[...]], axis=0)
+            out_ref[m] = dot_nt(rows, others)
+        return carry
+
+    lax.fori_loop(0, out_refs[0].shape[0], step, 0)
+
+
+def sent_kernel(orders, order, me_ref, jt_ref, jp_ref, r_ref, pan_ref, *out_refs):
+    core = me_ref[0] & 1
+    panel_part(order, core, jt_ref, jp_ref, pan_ref)
+    trail_part(orders, 1 - core, jt_ref, r_ref, out_refs)
+
+
+def kept_kernel(orders, me_ref, jt_ref, r_ref, *out_refs):
+    trail_part(orders, me_ref[0] & 1, jt_ref, r_ref, out_refs)
+
+
+def swap(x, axis, bit):
+    n = lax.axis_size(axis)
+    return lax.ppermute(x, axis, [(i, i ^ (1 << bit)) for i in range(n)])
+
+
+def halve(kept, got, me, order, axis):
+    for bit in order:
+        mine = (me >> bit) & 1
+        size = kept.shape[0] // 2
+        kept = kept.reshape((2, size) + kept.shape[1:])
+        got = got.reshape(kept.shape)
+
+        def part(which, kept=kept, got=got):
+            return lax.dynamic_index_in_dim(kept, which, 0, False) + lax.dynamic_index_in_dim(got, which, 0, False)
+
+        got = swap(part(1 - mine), axis, bit)
+        kept = part(mine)
+    return (kept + got)[0]
+
+
+def mirror(chunks, own, count):
+    wide = chunks[0].shape[1]
+
+    def kernel(*refs):
+        ins, outs, g_ref, turned_ref = refs[: len(chunks)], refs[len(chunks) : -2], refs[-2], refs[-1]
+        for q, ref in enumerate(ins):
+            turned_ref[q * wide : (q + 1) * wide, :] = ref[...].T
+        for k, out in enumerate(outs):
+            out[...] = turned_ref[(k + 1) * own : (k + 2) * own, :]
+        g_ref[...] = turned_ref[(count + 2) * own : (count + 2) * own + 8, :]
+
+    total = wide * len(chunks)
+    return call(kernel, chunks, [f32(own, own)] * count + [f32(8, own)], [pltpu.VMEM((total, own), jnp.float32)], 0, 8 * total * own)
+
+
+def factor_block(a):
+    size = a.shape[0]
+    lane = lax.broadcasted_iota(jnp.int32, (8, size), 1)
+    groups = [a[8 * g : 8 * g + 8] for g in range(size // 8)]
+    sub = lax.broadcasted_iota(jnp.int32, (8, size), 0)
+    diag = jnp.zeros((1, size), jnp.float32)
+    for j in range(size):
+        g, s = divmod(j, 8)
+        row = groups[g][s : s + 1, :]
+        pivot = row[:, j : j + 1]
+        inv = lax.rsqrt(pivot)
+        inv = inv * (1.5 - 0.5 * pivot * inv * inv)
+        at = lane[0:1] == j
+        scaled = jnp.where(at, inv, row * inv)
+        diag = jnp.where(at, pivot * inv, diag)
+        for h in range(g, size // 8):
+            f = groups[h][:, j : j + 1] * inv
+            new = jnp.where(lane == j, 0.0, groups[h]) - f * scaled
+            if h == g:
+                new = jnp.where(sub > s, new, jnp.where(sub == s, scaled, groups[h]))
+            groups[h] = new
+    both = jnp.concatenate(groups, axis=0)
+    row = lax.broadcasted_iota(jnp.int32, (size, size), 0)
+    col = lax.broadcasted_iota(jnp.int32, (size, size), 1)
+    upper = jnp.where(row < col, both, jnp.where(row == col, diag, 0.0))
+    return upper.T, jnp.where(row >= col, both, 0.0)
+
+
+def factor_kernel(me_ref, mine_ref, other_ref, damp_ref, factor_ref, inverse_ref, g_ref, n_ref):
+    core = me_ref[0] & 1
+    half = mine_ref.shape[0]
+    size = factor_ref.shape[0]
+    n_ref[pl.ds(pl.multiple_of(core * half, 8), half), :] = mine_ref[...]
+    n_ref[pl.ds(pl.multiple_of((1 - core) * half, 8), half), :] = other_ref[...]
+    g_ref[...] = n_ref[size : size + 8, :]
+    row = lax.broadcasted_iota(jnp.int32, (size, size), 0)
+    col = lax.broadcasted_iota(jnp.int32, (size, size), 1)
+    n = n_ref[:size, :] + jnp.where(row == col, damp_ref[:, 0:1], 0.0)
+    h = size // 2
+    l11, i11 = factor_block(n[:h, :h])
+    l21 = dot_nt(n[h:, :h], i11, EXACT)
+    l22, i22 = factor_block(n[h:, h:] - dot_nt(l21, l21, EXACT))
+    i21 = -jnp.dot(i22, jnp.dot(l21, i11, precision=EXACT, preferred_element_type=jnp.float32), precision=EXACT, preferred_element_type=jnp.float32)
+    zero = jnp.zeros((h, h), jnp.float32)
+    factor_ref[:h, :h] = l11
+    factor_ref[:h, h:] = zero
+    factor_ref[h:, :h] = l21
+    factor_ref[h:, h:] = l22
+    inverse_ref[:h, :h] = i11
+    inverse_ref[:h, h:] = zero
+    inverse_ref[h:, :h] = i21
+    inverse_ref[h:, h:] = i22
+
+
+def last_kernel(bits, n_chunks, n_mirror, me_ref, inverse_ref, g1_ref, mine_ref, other_ref, damp_ref, g2_ref, *refs):
+    chunks, mirrors = refs[:n_chunks], refs[n_chunks : n_chunks + n_mirror]
+    lower_ref, schur_ref, y_ref, rhs_ref, all_ref = refs[n_chunks + n_mirror :]
+    me = me_ref[0]
+    own, size = lower_ref.shape
+    n = schur_ref.shape[1] // own
+    inverse = inverse_ref[...]
+    for j in range(n):
+        rel = me ^ j
+        place = sum(((rel >> bit) & 1) << k for k, bit in enumerate(bits[:-1]))
+        far = (rel >> bits[-1]) & 1
+        near = mine_ref[place]
+        away = other_ref[place]
+        all_ref[j * own : (j + 1) * own, :] = jnp.where(far == 1, away, near)
+    lower_all = dot_nt(all_ref[...], inverse, EXACT)
+    lower = dot_nt(mine_ref[0], inverse, EXACT)
+    lower_ref[...] = lower
+    whole = jnp.concatenate([c[...] for c in chunks], axis=1)[:, : own * (n_mirror + 2)]
+    row = lax.broadcasted_iota(jnp.int32, (own, own), 0)
+    col = lax.broadcasted_iota(jnp.int32, (own, own), 1)
+    nat = own * STRIDE // (STRIDE - 1)
+    target = lax.broadcasted_iota(jnp.int32, (own, nat), 0)
+    target = target + 1 + ((target * 9363) >> 16)
+    pick = target == lax.broadcasted_iota(jnp.int32, (own, nat), 1)
+    damp = jnp.sum(jnp.where(pick, damp_ref[pl.ds(me, 1), :], 0.0), axis=1, keepdims=True)
+    first = whole[:, :own] + jnp.where(row == col, damp, 0.0)
+    whole = jnp.concatenate([first, whole[:, own:]] + [m[...] for m in reversed(mirrors)], axis=1)
+    whole = pltpu.roll(whole, me * own, 1)
+    schur_ref[...] = whole - dot_nt(lower, lower_all, EXACT)
+    y = dot_nt(g1_ref[...], inverse, EXACT)
+    y_ref[...] = y
+    rhs_ref[...] = g2_ref[...] - dot_nt(y, lower, EXACT)
 
 
 def per_device(features, gauge_offset, gauge_count, gauge_resid, damping):
+    tiles_here, samples, params = features.shape
+    slots = gauge_offset.shape[1]
+    axis = "tile"
+    n = lax.axis_size(axis)
+    bits = n.bit_length() - 1
+    panel = params // STRIDE
+    trail = params - panel
+    own = trail // n
+    if 1 << bits != n or n != 16 or own % 16 or params % BLK:
+        return per_device_plain(features, gauge_offset, gauge_count, gauge_resid, damping)
+    cap = tiles_here * slots // 2
+    wide, n_chunks = 256, 4
+    count = n // 2 - 1
+    half = n // 2
+    me = lax.axis_index(axis)
+    me1 = me.astype(jnp.int32).reshape(1)
+    order = list(range(1, bits))
+    orders = [order, order, order, [2, 1] + order[2:]]
+    ext = trail + own * half
+    padded = panel + 16
+    sent, kept, pan_sent, jt, jp, r = call(
+        functools.partial(front_kernel, order),
+        (me1, gauge_count, gauge_offset, gauge_resid, features.reshape(tiles_here * samples, params)),
+        [f32(padded // 2, panel), f32(padded // 2, panel), f32(half, own, panel), bf16(ext, cap), bf16(panel, cap), bf16(16, cap)],
+        [pltpu.VMEM((padded, panel), jnp.float32)],
+        flops=2 * cap * params * (tiles_here * samples + 2 * panel),
+        moved=2 * tiles_here * samples * params,
+    )
+    n11 = kept + swap(sent, axis, 0)
+    pan_got = swap(pan_sent, axis, 0)
+    pan_kept, *t_sent = call(
+        functools.partial(sent_kernel, orders, order),
+        (me1, jt, jp, r),
+        [f32(half, own, panel)] + [f32(half, own, wide)] * n_chunks,
+        flops=2 * cap * half * own * wide * (n_chunks + 1),
+        moved=2 * ext * cap + 4 * half * own * wide * (n_chunks + 1),
+    )
+    t_got = [swap(x, axis, 0) for x in t_sent]
+    t_kept = call(
+        functools.partial(kept_kernel, orders),
+        (me1, jt, r),
+        [f32(half, own, wide)] * n_chunks,
+        flops=2 * cap * half * own * wide * n_chunks,
+        moved=2 * ext * cap + 4 * half * own * wide * n_chunks,
+    )
+    for bit in order:
+        n11 = n11 + swap(n11, axis, bit)
+    n11_other = swap(n11, axis, 0)
+    n21 = halve(pan_kept, pan_got, me, order, axis)
+    factor, inverse, g1 = call(
+        factor_kernel,
+        (me1, n11, n11_other, damping.reshape(panel, STRIDE)),
+        [f32(panel, panel), f32(panel, panel), f32(8, panel)],
+        [pltpu.VMEM((padded, panel), jnp.float32)],
+        flops=0,
+        moved=100_000_000,
+    )
+    held = n21[None]
+    for bit in reversed(order):
+        held = jnp.concatenate([held, swap(held, axis, bit)], axis=0)
+    held_other = swap(held, axis, 0)
+    chunks = [halve(k, g, me, o, axis) for k, g, o in zip(t_kept, t_got, orders)]
+    *blocks, g2 = mirror(chunks, own, count)
+    mirrors = [lax.ppermute(b, axis, [(i, (i + k + 1) % n) for i in range(n)]) for k, b in enumerate(blocks)]
+    lower, schur, y, rhs = call(
+        functools.partial(last_kernel, list(reversed(order)) + [0], n_chunks, count),
+        (me1, inverse, g1, held, held_other, damping.reshape(n, params // n), g2, *chunks, *mirrors),
+        [f32(own, panel), f32(own, trail), f32(8, panel), f32(8, own)],
+        [pltpu.VMEM((trail, panel), jnp.float32)],
+        flops=12 * panel * panel * trail,
+        moved=8 * trail * panel,
+    )
+    return (factor, lower, schur, y[0], rhs[0])
+
+
+def per_device_plain(features, gauge_offset, gauge_count, gauge_resid, damping):
     tiles_here, samples, params = features.shape
     slots = gauge_offset.shape[1]
     panel = params // 8
@@ -30,14 +362,10 @@
     jac_split = jac.reshape(gauges, panel, 8)
     jac_panel = jac_split[:, :, 0]
     jac_trail = jac_split[:, :, 1:].reshape(gauges, trail)
-    panel_local = lax.dot_general(
-        jac, jac_panel, (((0,), (0,)), ((), ())), preferred_element_type=jnp.float32
-    )
+    panel_local = lax.dot_general(jac, jac_panel, (((0,), (0,)), ((), ())), preferred_element_type=jnp.float32)
     panel_all, grad = lax.psum((panel_local, grad_local), "tile")
     own_trail = lax.psum_scatter(
-        lax.dot_general(
-            jac_trail, jac_trail, (((0,), (0,)), ((), ())), preferred_element_type=jnp.float32
-        ),
+        lax.dot_general(jac_trail, jac_trail, (((0,), (0,)), ((), ())), preferred_element_type=jnp.float32),
         "tile",
         scatter_dimension=0,
         tiled=True,
@@ -51,17 +379,13 @@
     n11 = panel_split[:, 0, :] + jnp.diag(damp_split[:, 0])
     n21 = panel_split[:, 1:, :].reshape(trail, panel)
     panel_factor = jnp.linalg.cholesky(n11)
-    lower_all = lax.linalg.triangular_solve(
-        panel_factor, n21, left_side=False, lower=True, transpose_a=True
-    )
+    lower_all = lax.linalg.triangular_solve(panel_factor, n21, left_side=False, lower=True, transpose_a=True)
     lower_own = lax.dynamic_slice_in_dim(lower_all, index * owned_trail, owned_trail, 0)
     schur = own_trail - jnp.dot(lower_own, lower_all.T, precision=lax.Precision.HIGHEST)
     grad_split = grad.reshape(panel, 8)
     first_part = grad_split[:, 0]
     second_part = grad_split[:, 1:].reshape(trail)
-    panel_rhs = lax.linalg.triangular_solve(
-        panel_factor, first_part[:, None], left_side=True, lower=True
-    )[:, 0]
+    panel_rhs = lax.linalg.triangular_solve(panel_factor, first_part[:, None], left_side=True, lower=True)[:, 0]
     second_own = lax.dynamic_slice_in_dim(second_part, index * owned_trail, owned_trail, 0)
     trail_rhs = second_own - jnp.dot(lower_own, panel_rhs, precision=lax.Precision.HIGHEST)
     return (panel_factor, lower_own, schur, panel_rhs, trail_rhs)

time: 301 us -> 185 us (0.61)
  Pallas kernels: 0 us -> 68.8 us
  blocking collectives: 59.6 us -> 0 us
  local copies, waits for them, and re-layouts: 58 us -> 4.15 us
  starting transfers between devices: 0.08 us -> 48.9 us
  other arithmetic: 58.1 us -> 10 us
  matrix products: 41.5 us -> 0 us
  waiting for transfers between devices: 65.2 us -> 50.5 us
  between operations: 15.6 us -> 1.02 us
    pallas_call x0 -> x6, Pallas kernels: none -> 68.8 us  [call(): pl.pallas_call(kernel, out_shape=out_shape, in_specs=[SMEM_SPEC if x.dtyp...]
    reduce_scatter x1 -> x0, waiting for transfers between devices: 64.8 us -> none  [per_device(): lax.psum_scatter(lax.dot_general(jac_trail, jac_trail, (((0,), (0,)), (()...]
    psum x1 -> x0, blocking collectives: 59.6 us -> none  [per_device(): panel_all, grad = lax.psum((panel_local, grad_local), 'tile')]
    another operation x11 -> x0, other arithmetic: 54.6 us -> none  [the longest x6 33.9 us: per_device(): panel_factor = jnp.linalg.cholesky(n11)]
    ppermute x0 -> x36, waiting for transfers between devices: none -> 50.5 us  [the longest x29 47.6 us: swap(): return lax.ppermute(x, axis, [(i, i ^ 1 << bit) for i in range(n)])]
    ppermute x0 -> x36, starting transfers between devices: none -> 48.9 us  [the longest x29 41.6 us: swap(): return lax.ppermute(x, axis, [(i, i ^ 1 << bit) for i in range(n)])]
    dot_general x6 -> x0, matrix products: 35.6 us -> none  [the longest x1 17.1 us: per_device(): lax.dot_general(jac_trail, jac_trail, (((0,), (0,)), ((), ())), preferred...]
    another operation x20 -> x0, local copies, waits for them, and re-layouts: 15.7 us -> none  [the longest x1 11 us: per_device(): jac_split = jac.reshape(gauges, panel, 8)]
  transfers between devices with their start and end apart: 2 -> 36, of which waited for: 2 -> 14; matrix products, arithmetic and copies ran while one was open for 38% -> 6% of each run, Pallas kernels for 0% -> 26%
where the time goes in v1:
time: 185 us; the launch traced here: 183 us
  Pallas kernels  68.8 us (37%)
  waiting for transfers between devices  50.5 us (27%)
  starting transfers between devices  48.9 us (26%)
  other arithmetic  10 us (5%)
  local copies, waits for them, and re-layouts  4.15 us (2%)
    pallas_call x6, Pallas kernels, call(): pl.pallas_call(kernel, out_shape=out_shape, in_specs=[SMEM_SPEC if x.dtyp...  68.8 us
    ppermute x29, waiting for transfers between devices, swap(): return lax.ppermute(x, axis, [(i, i ^ 1 << bit) for i in range(n)])  47.6 us
    ppermute x29, starting transfers between devices, swap(): return lax.ppermute(x, axis, [(i, i ^ 1 << bit) for i in range(n)])  41.6 us
    ppermute x7, starting transfers between devices, per_device(): lax.ppermute(b, axis, [(i, (i + k + 1) % n) for i in range(n)])  7.3 us
    add x15, other arithmetic, part(): lax.dynamic_index_in_dim(kept, which, 0, False)  7.1 us
  transfers between devices with their start and end apart: 36, of which 14 were waited for; matrix products, arithmetic and copies ran while one was open for 6% of the time, Pallas kernels for 26%

profile of v1, /device:TPU:1, one launch (start us, length us, event | category | flops | bytes accessed | tf_op | source)
XLA Modules:
  0.0 183.3 jit_solution(299846513502113806)
XLA Ops:
  0.6 12.0 %shard_map.92 = (f32[136,256]{1,0:T(8,128)}, f32[136,256]{1,0:T(8,128)}, f32[8,112,256]{2,1,0:T(8,128)}, bf16[2688,768]{1,0:T(8,128)(2,1)}, bf16[256,768]{1,0:T(8,128)(2,1)}, /*index=5*/bf16[16,768]{1,0:T(8,128)(2,1)}) custom-call(s32[1]{0:T(128)} %bitcast.me_ref, s32[4]{0:T(128)} %count_ref.1, s32[4,384]{1,0:T(4,128)} %offset_ref.1, ...), custom_call_target="tpu_custom_call" | custom-call | flops 4831838208 | bytes 4194304 | tf_op jit(solution)/shard_map/pallas_call | solution.py:34
  12.8 11.3 %shard_map.94 = (f32[8,112,256]{2,1,0:T(8,128)}, f32[8,112,256]{2,1,0:T(8,128)}, f32[8,112,256]{2,1,0:T(8,128)}, f32[8,112,256]{2,1,0:T(8,128)}, f32[8,112,256]{2,1,0:T(8,128)}) custom-call(s32[1]{0:T(128)} %bitcast.me_ref, bf16[2688,768]{1,0:T(8,128)(2,1)} %get-tuple-element.40.jt_ref, bf16[256,768]{1,0:T(8,128)(2,1)} %get-tuple-element.41.jp_ref, ...), custom_call_target="tpu_custom_call" | custom-call | flops 1761607680 | bytes 8716288 | tf_op jit(solution)/shard_map/pallas_call | solution.py:34
  25.1 1.9 %collective-permute-done = f32[136,256]{1,0:T(8,128)S(1)} collective-permute-done((f32[136,256]{1,0:T(8,128)S(1)}, f32[136,256]{1,0:T(8,128)S(1)}, u32[]{:S(2)}, u32[]{:S(2)}) %collective-permute-start) | collective-permute-done | bytes 139296 | tf_op jit(solution)/shard_map/ppermute | solution.py:144
  27.0 2.4 %collective-permute-start.1 = (f32[136,256]{1,0:T(8,128)S(1)}, f32[136,256]{1,0:T(8,128)S(1)}, u32[]{:S(2)}, u32[]{:S(2)}) collective-permute-start(f32[136,256]{1,0:T(8,128)S(1)} %add.270), channel_id=1, source_target_pairs={{0,2},{1,3},{2,0},{3,1},{4,6},{5,7},{6,4},{7,5},{8,10},{9,11},{10,... | collective-permute-start | bytes 417800 | tf_op jit(solution)/shard_map/ppermute | solution.py:144
  29.4 3.7 %collective-permute-done.1 = f32[136,256]{1,0:T(8,128)S(1)} collective-permute-done((f32[136,256]{1,0:T(8,128)S(1)}, f32[136,256]{1,0:T(8,128)S(1)}, u32[]{:S(2)}, u32[]{:S(2)}) %collective-permute-start.1) | collective-permute-done | bytes 139296 | tf_op jit(solution)/shard_map/ppermute | solution.py:144
  35.9 1.6 collective-permute-done.2
  37.6 1.8 collective-permute-start.13
  39.4 2.4 %collective-permute-start.3 = (f32[136,256]{1,0:T(8,128)S(1)}, f32[136,256]{1,0:T(8,128)S(1)}, u32[]{:S(2)}, u32[]{:S(2)}) collective-permute-start(f32[136,256]{1,0:T(8,128)S(1)} %add.272), channel_id=1, source_target_pairs={{0,8},{1,9},{2,10},{3,11},{4,12},{5,13},{6,14},{7,15},{8,0},{9,1},... | collective-permute-start | bytes 417800 | tf_op jit(solution)/shard_map/ppermute | solution.py:144
  41.8 2.3 %dynamic-slice_add_fusion.4 = (f32[1,4,112,256]{3,2,1,0:T(8,128)S(1)}, f32[4,112,256]{2,1,0:T(8,128)}) fusion(f32[2,4,112,256]{3,2,1,0:T(8,128)} %bitcast.3, s32[]{:T(128)S(6)} %select_n.75, f32[2,4,112,256]{3,2,1,0:T(8,128)} %bitcast.100, s32[]{:T(128)S(6)} %select_n.77), kind=kLoop, calls=%fused_computation.11 | loop fusion | flops 229376 | bytes 2752520 | tf_op jit(solution)/shard_map/add | solution.py:155
  44.1 4.5 %collective-permute-done.3 = f32[136,256]{1,0:T(8,128)S(1)} collective-permute-done((f32[136,256]{1,0:T(8,128)S(1)}, f32[136,256]{1,0:T(8,128)S(1)}, u32[]{:S(2)}, u32[]{:S(2)}) %collective-permute-start.3) | collective-permute-done | bytes 139296 | tf_op jit(solution)/shard_map/ppermute | solution.py:144
  49.9 8.9 %shard_map.95 = (f32[8,112,256]{2,1,0:T(8,128)}, f32[8,112,256]{2,1,0:T(8,128)}, f32[8,112,256]{2,1,0:T(8,128)}, f32[8,112,256]{2,1,0:T(8,128)}) custom-call(s32[1]{0:T(128)} %bitcast.me_ref, bf16[2688,768]{1,0:T(8,128)(2,1)} %get-tuple-element.40.jt_ref, bf16[16,768]{1,0:T(8,128)(2,1)} %get-tuple-element.42.r_ref), custom_call_target="tpu_custom_call" | custom-call | flops 1409286144 | bytes 7798784 | tf_op jit(solution)/shard_map/pallas_call | solution.py:34
  60.0 1.6 dynamic-slice_add_fusion
  67.7 11.0 %collective-permute-done.7 = f32[2,112,256]{2,1,0:T(8,128)S(1)} collective-permute-done((f32[2,112,256]{2,1,0:T(8,128)S(1)}, f32[2,112,256]{2,1,0:T(8,128)S(1)}, u32[]{:S(2)}, u32[]{:S(2)}) %collective-permute-start.7) | collective-permute-done | bytes 229408 | tf_op jit(solution)/shard_map/ppermute | solution.py:144
  78.9 2.4 %collective-permute-start.8 = (f32[1,112,256]{2,1,0:T(8,128)S(1)}, f32[1,112,256]{2,1,0:T(8,128)S(1)}, u32[]{:S(2)}, u32[]{:S(2)}) collective-permute-start(f32[1,112,256]{2,1,0:T(8,128)S(1)} %bitcast_add_fusion.8), channel_id=1, source_target_pairs={{0,8},{1,9},{2,10},{3,11},{4,12},{5,13},{6,14},{7,15},{8,0},{9,1},... | collective-permute-start | bytes 344072 | tf_op jit(solution)/shard_map/ppermute | solution.py:144
  81.3 5.1 %collective-permute-done.8 = f32[1,112,256]{2,1,0:T(8,128)S(1)} collective-permute-done((f32[1,112,256]{2,1,0:T(8,128)S(1)}, f32[1,112,256]{2,1,0:T(8,128)S(1)}, u32[]{:S(2)}, u32[]{:S(2)}) %collective-permute-start.8) | collective-permute-done | bytes 114720 | tf_op jit(solution)/shard_map/ppermute | solution.py:144
  88.0 4.5 %collective-permute-done.9 = f32[1,112,256]{2,1,0:T(8,128)S(1)} collective-permute-done((f32[1,112,256]{2,1,0:T(8,128)S(1)}, f32[1,112,256]{2,1,0:T(8,128)S(1)}, u32[]{:S(2)}, u32[]{:S(2)}) %collective-permute-start.9) | collective-permute-done | bytes 114720 | tf_op jit(solution)/shard_map/ppermute | solution.py:144
  92.4 2.4 %collective-permute-start.23 = (f32[2,112,256]{2,1,0:T(8,128)S(1)}, f32[2,112,256]{2,1,0:T(8,128)S(1)}, u32[]{:S(2)}, u32[]{:S(2)}) collective-permute-start(f32[2,112,256]{2,1,0:T(8,128)S(1)} %get-tuple-element.78), channel_id=1, source_target_pairs={{0,4},{1,5},{2,6},{3,7},{4,0},{5,1},{6,2},{7,3},{8,12},{9,13},{10,... | collective-permute-start | bytes 688136 | tf_op jit(solution)/shard_map/ppermute | solution.py:144
  95.1 1.5 collective-permute-start.19
  96.6 6.3 %collective-permute-done.10 = f32[2,112,256]{2,1,0:T(8,128)S(1)} collective-permute-done((f32[2,112,256]{2,1,0:T(8,128)S(1)}, f32[2,112,256]{2,1,0:T(8,128)S(1)}, u32[]{:S(2)}, u32[]{:S(2)}) %collective-permute-start.10) | collective-permute-done | bytes 229408 | tf_op jit(solution)/shard_map/ppermute | solution.py:144
  102.9 1.8 collective-permute-start.15
  105.1 3.2 %collective-permute-start.28 = (f32[1,112,256]{2,1,0:T(8,128)S(1)}, f32[1,112,256]{2,1,0:T(8,128)S(1)}, u32[]{:S(2)}, u32[]{:S(2)}) collective-permute-start(f32[1,112,256]{2,1,0:T(8,128)S(1)} %bitcast_add_fusion), channel_id=1, source_target_pairs={{0,8},{1,9},{2,10},{3,11},{4,12},{5,13},{6,14},{7,15},{8,0},{9,1},... | collective-permute-start | bytes 344072 | tf_op jit(solution)/shard_map/ppermute | solution.py:144
  108.3 3.3 %collective-permute-start.24 = (f32[1,112,256]{2,1,0:T(8,128)S(1)}, f32[1,112,256]{2,1,0:T(8,128)S(1)}, u32[]{:S(2)}, u32[]{:S(2)}) collective-permute-start(f32[1,112,256]{2,1,0:T(8,128)S(1)} %bitcast_add_fusion.2), channel_id=1, source_target_pairs={{0,8},{1,9},{2,10},{3,11},{4,12},{5,13},{6,14},{7,15},{8,0},{9,1},... | collective-permute-start | bytes 344072 | tf_op jit(solution)/shard_map/ppermute | solution.py:144
  111.7 3.6 %collective-permute-done.15 = f32[2,112,256]{2,1,0:T(8,128)S(1)} collective-permute-done((f32[2,112,256]{2,1,0:T(8,128)S(1)}, f32[2,112,256]{2,1,0:T(8,128)S(1)}, u32[]{:S(2)}, u32[]{:S(2)}) %collective-permute-start.15) | collective-permute-done | bytes 229408 | tf_op jit(solution)/shard_map/ppermute | solution.py:144
  115.2 2.3 %collective-permute-start.20 = (f32[1,112,256]{2,1,0:T(8,128)S(1)}, f32[1,112,256]{2,1,0:T(8,128)S(1)}, u32[]{:S(2)}, u32[]{:S(2)}) collective-permute-start(f32[1,112,256]{2,1,0:T(8,128)S(1)} %bitcast_add_fusion.4), channel_id=1, source_target_pairs={{0,8},{1,9},{2,10},{3,11},{4,12},{5,13},{6,14},{7,15},{8,0},{9,1},... | collective-permute-start | bytes 344072 | tf_op jit(solution)/shard_map/ppermute | solution.py:144
  117.8 6.5 %collective-permute-start.12 = (f32[8,112,256]{2,1,0:T(8,128)S(1)}, f32[8,112,256]{2,1,0:T(8,128)S(1)}, u32[]{:S(2)}, u32[]{:S(2)}) collective-permute-start(f32[8,112,256]{2,1,0:T(8,128)S(1)} %pad_maximum_fusion.mine_ref), channel_id=1, source_target_pairs={{0,1},{1,0},{2,3},{3,2},{4,5},{5,4},{6,7},{7,6},{8,9},{9,8},{10,11... | collective-permute-start | bytes 2752520 | tf_op jit(solution)/shard_map/ppermute | solution.py:144
  125.6 3.6 %collective-permute-done.20 = f32[1,112,256]{2,1,0:T(8,128)S(1)} collective-permute-done((f32[1,112,256]{2,1,0:T(8,128)S(1)}, f32[1,112,256]{2,1,0:T(8,128)S(1)}, u32[]{:S(2)}, u32[]{:S(2)}) %collective-permute-start.20) | collective-permute-done | bytes 114720 | tf_op jit(solution)/shard_map/ppermute | solution.py:144
  129.9 1.8 collective-permute-done.16
  132.3 2.0 %shard_map.96 = (f32[112,112]{1,0:T(8,128)}, f32[112,112]{1,0:T(8,128)}, f32[112,112]{1,0:T(8,128)}, f32[112,112]{1,0:T(8,128)}, f32[112,112]{1,0:T(8,128)}, /*i...) custom-call(f32[112,256]{1,0:T(8,128)} %fusion.7.refs_0_, f32[112,256]{1,0:T(8,128)} %fusion.5.refs_1_, ...), custom_call_target="tpu_custom_call" | custom-call | bytes 917504 | tf_op jit(solution)/shard_map/pallas_call | solution.py:34
  134.3 3.0 %collective-permute-start.29 = (f32[112,112]{1,0:T(8,128)}, f32[112,112]{1,0:T(8,128)S(1)}, u32[]{:S(2)}, u32[]{:S(2)}) collective-permute-start(f32[112,112]{1,0:T(8,128)} %get-tuple-element.54), channel_id=1, source_target_pairs={{0,1},{1,2},{2,3},{3,4},{4,5},{5,6},{6,7},{7,8},{8,9},{9,10},{10,1... | collective-permute-start | bytes 150536 | tf_op jit(solution)/shard_map/ppermute | solution.py:329
  138.9 4.0 %collective-permute-start.33 = (f32[112,112]{1,0:T(8,128)}, f32[112,112]{1,0:T(8,128)S(1)}, u32[]{:S(2)}, u32[]{:S(2)}) collective-permute-start(f32[112,112]{1,0:T(8,128)} %get-tuple-element.58), channel_id=1, source_target_pairs={{0,5},{1,6},{2,7},{3,8},{4,9},{5,10},{6,11},{7,12},{8,13},{9,14},{... | collective-permute-start | bytes 150536 | tf_op jit(solution)/shard_map/ppermute | solution.py:329
  145.3 26.3 %shard_map.93 = (f32[256,256]{1,0:T(8,128)}, f32[256,256]{1,0:T(8,128)}, f32[8,256]{1,0:T(8,128)}) custom-call(s32[1]{0:T(128)} %bitcast.me_ref, f32[136,256]{1,0:T(8,128)} %copy-done.3, f32[136,256]{1,0:T(8,128)} %copy-done.4, f32[256,8]{1,0:T(8,128)} %reshape.214.damp_ref), custom_call_target="tpu_custom_call" | custom-call | bytes 100000000 | tf_op jit(solution)/shard_map/pallas_call | solution.py:34
  172.6 8.3 %shard_map.97 = (f32[112,256]{1,0:T(8,128)}, f32[112,1792]{1,0:T(8,128)}, f32[8,256]{1,0:T(8,128)}, f32[8,112]{1,0:T(8,128)}) custom-call(s32[1]{0:T(128)} %bitcast.me_ref, f32[256,256]{1,0:T(8,128)} %get-tuple-element.38.inverse_ref, f32[8,256]{1,0:T(8,128)} %get-tuple-element.39.g1_ref, f32[8,112,256]{2,1,0:T(8,128)} %copy-done, f32[8,112,256]{2,1,0:T(8,128)} %copy-done.7, ...), custom_call_target="tpu_custom_call" | custom-call | flops 1409286144 | bytes 3670016 | tf_op jit(solution)/shard_map/pallas_call | solution.py:34
  (108 shorter events, 24.9 us)
Async XLA Ops:
  12.7 26.7 %collective-permute-start.5 = (f32[8,112,256]{2,1,0:T(8,128)}, f32[8,112,256]{2,1,0:T(8,128)}, u32[]{:S(2)}, u32[]{:S(2)}) collective-permute-start(f32[8,112,256]{2,1,0:T(8,128)} %get-tuple-element.44), channel_id=1, source_target_pairs={{0,1},{1,0},{2,3},{3,2},{4,5},{5,4},{6,7},{7,6},{8,9},{9,8},{10,11... | collective-permute-start | bytes 2752520 | tf_op jit(solution)/shard_map/ppermute | solution.py:144
  24.1 34.8 %collective-permute-start.25 = (f32[8,112,256]{2,1,0:T(8,128)}, f32[8,112,256]{2,1,0:T(8,128)}, u32[]{:S(2)}, u32[]{:S(2)}) collective-permute-start(f32[8,112,256]{2,1,0:T(8,128)} %get-tuple-element.52), channel_id=1, source_target_pairs={{0,1},{1,0},{2,3},{3,2},{4,5},{5,4},{6,7},{7,6},{8,9},{9,8},{10,11... | collective-permute-start | bytes 2752520 | tf_op jit(solution)/shard_map/ppermute | solution.py:144
  24.6 37.0 %collective-permute-start.21 = (f32[8,112,256]{2,1,0:T(8,128)}, f32[8,112,256]{2,1,0:T(8,128)S(1)}, u32[]{:S(2)}, u32[]{:S(2)}) collective-permute-start(f32[8,112,256]{2,1,0:T(8,128)} %get-tuple-element.50), channel_id=1, source_target_pairs={{0,1},{1,0},{2,3},{3,2},{4,5},{5,4},{6,7},{7,6},{8,9},{9,8},{10,11... | collective-permute-start | bytes 2752520 | tf_op jit(solution)/shard_map/ppermute | solution.py:144
  27.0 6.2 %collective-permute-start.1 = (f32[136,256]{1,0:T(8,128)S(1)}, f32[136,256]{1,0:T(8,128)S(1)}, u32[]{:S(2)}, u32[]{:S(2)}) collective-permute-start(f32[136,256]{1,0:T(8,128)S(1)} %add.270), channel_id=1, source_target_pairs={{0,2},{1,3},{2,0},{3,1},{4,6},{5,7},{6,4},{7,5},{8,10},{9,11},{10,... | collective-permute-start | bytes 417800 | tf_op jit(solution)/shard_map/ppermute | solution.py:144
  34.4 30.5 %collective-permute-start.17 = (f32[8,112,256]{2,1,0:T(8,128)}, f32[8,112,256]{2,1,0:T(8,128)S(1)}, u32[]{:S(2)}, u32[]{:S(2)}) collective-permute-start(f32[8,112,256]{2,1,0:T(8,128)} %get-tuple-element.48), channel_id=1, source_target_pairs={{0,1},{1,0},{2,3},{3,2},{4,5},{5,4},{6,7},{7,6},{8,9},{9,8},{10,11... | collective-permute-start | bytes 2752520 | tf_op jit(solution)/shard_map/ppermute | solution.py:144
  37.6 28.6 %collective-permute-start.13 = (f32[8,112,256]{2,1,0:T(8,128)}, f32[8,112,256]{2,1,0:T(8,128)S(1)}, u32[]{:S(2)}, u32[]{:S(2)}) collective-permute-start(f32[8,112,256]{2,1,0:T(8,128)} %get-tuple-element.46), channel_id=1, source_target_pairs={{0,1},{1,0},{2,3},{3,2},{4,5},{5,4},{6,7},{7,6},{8,9},{9,8},{10,11... | collective-permute-start | bytes 2752520 | tf_op jit(solution)/shard_map/ppermute | solution.py:144
  39.4 9.3 %collective-permute-start.3 = (f32[136,256]{1,0:T(8,128)S(1)}, f32[136,256]{1,0:T(8,128)S(1)}, u32[]{:S(2)}, u32[]{:S(2)}) collective-permute-start(f32[136,256]{1,0:T(8,128)S(1)} %add.272), channel_id=1, source_target_pairs={{0,8},{1,9},{2,10},{3,11},{4,12},{5,13},{6,14},{7,15},{8,0},{9,1},... | collective-permute-start | bytes 417800 | tf_op jit(solution)/shard_map/ppermute | solution.py:144
  48.7 14.8 %collective-permute-start.6 = (f32[4,112,256]{2,1,0:T(8,128)}, f32[4,112,256]{2,1,0:T(8,128)}, u32[]{:S(2)}, u32[]{:S(2)}) collective-permute-start(f32[4,112,256]{2,1,0:T(8,128)} %get-tuple-element.74), channel_id=1, source_target_pairs={{0,2},{1,3},{2,0},{3,1},{4,6},{5,7},{6,4},{7,5},{8,10},{9,11},{10,... | collective-permute-start | bytes 1376264 | tf_op jit(solution)/shard_map/ppermute | solution.py:144
  58.9 78.5 %collective-permute-start.4 = (f32[136,256]{1,0:T(8,128)S(1)}, f32[136,256]{1,0:T(8,128)S(1)}, u32[]{:S(2)}, u32[]{:S(2)}) collective-permute-start(f32[136,256]{1,0:T(8,128)S(1)} %add.273.mine_ref), channel_id=1, source_target_pairs={{0,1},{1,0},{2,3},{3,2},{4,5},{5,4},{6,7},{7,6},{8,9},{9,8},{10,11... | collective-permute-start | bytes 417800 | tf_op jit(solution)/shard_map/ppermute | solution.py:144
  61.7 17.2 %collective-permute-start.26 = (f32[4,112,256]{2,1,0:T(8,128)S(1)}, f32[4,112,256]{2,1,0:T(8,128)S(1)}, u32[]{:S(2)}, u32[]{:S(2)}) collective-permute-start(f32[4,112,256]{2,1,0:T(8,128)S(1)} %get-tuple-element.66), channel_id=1, source_target_pairs={{0,4},{1,5},{2,6},{3,7},{4,0},{5,1},{6,2},{7,3},{8,12},{9,13},{10,... | collective-permute-start | bytes 1376264 | tf_op jit(solution)/shard_map/ppermute | solution.py:144
  63.5 24.3 %collective-permute-start.22 = (f32[4,112,256]{2,1,0:T(8,128)S(1)}, f32[4,112,256]{2,1,0:T(8,128)S(1)}, u32[]{:S(2)}, u32[]{:S(2)}) collective-permute-start(f32[4,112,256]{2,1,0:T(8,128)S(1)} %get-tuple-element.68), channel_id=1, source_target_pairs={{0,2},{1,3},{2,0},{3,1},{4,6},{5,7},{6,4},{7,5},{8,10},{9,11},{10,... | collective-permute-start | bytes 1376264 | tf_op jit(solution)/shard_map/ppermute | solution.py:144
  64.9 13.8 %collective-permute-start.7 = (f32[2,112,256]{2,1,0:T(8,128)S(1)}, f32[2,112,256]{2,1,0:T(8,128)S(1)}, u32[]{:S(2)}, u32[]{:S(2)}) collective-permute-start(f32[2,112,256]{2,1,0:T(8,128)S(1)} %get-tuple-element.84), channel_id=1, source_target_pairs={{0,4},{1,5},{2,6},{3,7},{4,0},{5,1},{6,2},{7,3},{8,12},{9,13},{10,... | collective-permute-start | bytes 688136 | tf_op jit(solution)/shard_map/ppermute | solution.py:144
  66.2 28.7 %collective-permute-start.18 = (f32[4,112,256]{2,1,0:T(8,128)S(1)}, f32[4,112,256]{2,1,0:T(8,128)S(1)}, u32[]{:S(2)}, u32[]{:S(2)}) collective-permute-start(f32[4,112,256]{2,1,0:T(8,128)S(1)} %get-tuple-element.70), channel_id=1, source_target_pairs={{0,2},{1,3},{2,0},{3,1},{4,6},{5,7},{6,4},{7,5},{8,10},{9,11},{10,... | collective-permute-start | bytes 1376264 | tf_op jit(solution)/shard_map/ppermute | solution.py:144
  78.7 16.3 %collective-permute-start.14 = (f32[4,112,256]{2,1,0:T(8,128)S(1)}, f32[4,112,256]{2,1,0:T(8,128)S(1)}, u32[]{:S(2)}, u32[]{:S(2)}) collective-permute-start(f32[4,112,256]{2,1,0:T(8,128)S(1)} %get-tuple-element.72), channel_id=1, source_target_pairs={{0,2},{1,3},{2,0},{3,1},{4,6},{5,7},{6,4},{7,5},{8,10},{9,11},{10,... | collective-permute-start | bytes 1376264 | tf_op jit(solution)/shard_map/ppermute | solution.py:144
  78.9 7.5 %collective-permute-start.8 = (f32[1,112,256]{2,1,0:T(8,128)S(1)}, f32[1,112,256]{2,1,0:T(8,128)S(1)}, u32[]{:S(2)}, u32[]{:S(2)}) collective-permute-start(f32[1,112,256]{2,1,0:T(8,128)S(1)} %bitcast_add_fusion.8), channel_id=1, source_target_pairs={{0,8},{1,9},{2,10},{3,11},{4,12},{5,13},{6,14},{7,15},{8,0},{9,1},... | collective-permute-start | bytes 344072 | tf_op jit(solution)/shard_map/ppermute | solution.py:144
  86.4 18.3 %collective-permute-start.27 = (f32[2,112,256]{2,1,0:T(8,128)S(1)}, f32[2,112,256]{2,1,0:T(8,128)S(1)}, u32[]{:S(2)}, u32[]{:S(2)}) collective-permute-start(f32[2,112,256]{2,1,0:T(8,128)S(1)} %get-tuple-element.76), channel_id=1, source_target_pairs={{0,2},{1,3},{2,0},{3,1},{4,6},{5,7},{6,4},{7,5},{8,10},{9,11},{10,... | collective-permute-start | bytes 688136 | tf_op jit(solution)/shard_map/ppermute | solution.py:144
  92.4 12.6 %collective-permute-start.23 = (f32[2,112,256]{2,1,0:T(8,128)S(1)}, f32[2,112,256]{2,1,0:T(8,128)S(1)}, u32[]{:S(2)}, u32[]{:S(2)}) collective-permute-start(f32[2,112,256]{2,1,0:T(8,128)S(1)} %get-tuple-element.78), channel_id=1, source_target_pairs={{0,4},{1,5},{2,6},{3,7},{4,0},{5,1},{6,2},{7,3},{8,12},{9,13},{10,... | collective-permute-start | bytes 688136 | tf_op jit(solution)/shard_map/ppermute | solution.py:144
  94.9 8.1 %collective-permute-start.10 = (f32[2,112,256]{2,1,0:T(8,128)S(1)}, f32[2,112,256]{2,1,0:T(8,128)S(1)}, u32[]{:S(2)}, u32[]{:S(2)}) collective-permute-start(f32[2,112,256]{2,1,0:T(8,128)S(1)} %pad_maximum_fusion.2), channel_id=1, source_target_pairs={{0,4},{1,5},{2,6},{3,7},{4,0},{5,1},{6,2},{7,3},{8,12},{9,13},{10,... | collective-permute-start | bytes 688136 | tf_op jit(solution)/shard_map/ppermute | solution.py:144
  95.1 13.2 %collective-permute-start.19 = (f32[2,112,256]{2,1,0:T(8,128)S(1)}, f32[2,112,256]{2,1,0:T(8,128)S(1)}, u32[]{:S(2)}, u32[]{:S(2)}) collective-permute-start(f32[2,112,256]{2,1,0:T(8,128)S(1)} %get-tuple-element.80), channel_id=1, source_target_pairs={{0,4},{1,5},{2,6},{3,7},{4,0},{5,1},{6,2},{7,3},{8,12},{9,13},{10,... | collective-permute-start | bytes 688136 | tf_op jit(solution)/shard_map/ppermute | solution.py:144
  102.9 12.3 %collective-permute-start.15 = (f32[2,112,256]{2,1,0:T(8,128)S(1)}, f32[2,112,256]{2,1,0:T(8,128)S(1)}, u32[]{:S(2)}, u32[]{:S(2)}) collective-permute-start(f32[2,112,256]{2,1,0:T(8,128)S(1)} %get-tuple-element.82), channel_id=1, source_target_pairs={{0,4},{1,5},{2,6},{3,7},{4,0},{5,1},{6,2},{7,3},{8,12},{9,13},{10,... | collective-permute-start | bytes 688136 | tf_op jit(solution)/shard_map/ppermute | solution.py:144
  104.8 12.8 %collective-permute-start.11 = (f32[4,112,256]{2,1,0:T(8,128)S(1)}, f32[4,112,256]{2,1,0:T(8,128)S(1)}, u32[]{:S(2)}, u32[]{:S(2)}) collective-permute-start(f32[4,112,256]{2,1,0:T(8,128)S(1)} %pad_maximum_fusion.1), channel_id=1, source_target_pairs={{0,2},{1,3},{2,0},{3,1},{4,6},{5,7},{6,4},{7,5},{8,10},{9,11},{10,... | collective-permute-start | bytes 1376264 | tf_op jit(solution)/shard_map/ppermute | solution.py:144
  105.1 12.7 %collective-permute-start.28 = (f32[1,112,256]{2,1,0:T(8,128)S(1)}, f32[1,112,256]{2,1,0:T(8,128)S(1)}, u32[]{:S(2)}, u32[]{:S(2)}) collective-permute-start(f32[1,112,256]{2,1,0:T(8,128)S(1)} %bitcast_add_fusion), channel_id=1, source_target_pairs={{0,8},{1,9},{2,10},{3,11},{4,12},{5,13},{6,14},{7,15},{8,0},{9,1},... | collective-permute-start | bytes 344072 | tf_op jit(solution)/shard_map/ppermute | solution.py:144
  108.3 16.6 %collective-permute-start.24 = (f32[1,112,256]{2,1,0:T(8,128)S(1)}, f32[1,112,256]{2,1,0:T(8,128)S(1)}, u32[]{:S(2)}, u32[]{:S(2)}) collective-permute-start(f32[1,112,256]{2,1,0:T(8,128)S(1)} %bitcast_add_fusion.2), channel_id=1, source_target_pairs={{0,8},{1,9},{2,10},{3,11},{4,12},{5,13},{6,14},{7,15},{8,0},{9,1},... | collective-permute-start | bytes 344072 | tf_op jit(solution)/shard_map/ppermute | solution.py:144
  115.2 14.0 %collective-permute-start.20 = (f32[1,112,256]{2,1,0:T(8,128)S(1)}, f32[1,112,256]{2,1,0:T(8,128)S(1)}, u32[]{:S(2)}, u32[]{:S(2)}) collective-permute-start(f32[1,112,256]{2,1,0:T(8,128)S(1)} %bitcast_add_fusion.4), channel_id=1, source_target_pairs={{0,8},{1,9},{2,10},{3,11},{4,12},{5,13},{6,14},{7,15},{8,0},{9,1},... | collective-permute-start | bytes 344072 | tf_op jit(solution)/shard_map/ppermute | solution.py:144
  117.5 14.1 %collective-permute-start.16 = (f32[1,112,256]{2,1,0:T(8,128)S(1)}, f32[1,112,256]{2,1,0:T(8,128)S(1)}, u32[]{:S(2)}, u32[]{:S(2)}) collective-permute-start(f32[1,112,256]{2,1,0:T(8,128)S(1)} %bitcast_add_fusion.6), channel_id=1, source_target_pairs={{0,8},{1,9},{2,10},{3,11},{4,12},{5,13},{6,14},{7,15},{8,0},{9,1},... | collective-permute-start | bytes 344072 | tf_op jit(solution)/shard_map/ppermute | solution.py:144
  117.8 53.8 %collective-permute-start.12 = (f32[8,112,256]{2,1,0:T(8,128)S(1)}, f32[8,112,256]{2,1,0:T(8,128)S(1)}, u32[]{:S(2)}, u32[]{:S(2)}) collective-permute-start(f32[8,112,256]{2,1,0:T(8,128)S(1)} %pad_maximum_fusion.mine_ref), channel_id=1, source_target_pairs={{0,1},{1,0},{2,3},{3,2},{4,5},{5,4},{6,7},{7,6},{8,9},{9,8},{10,11... | collective-permute-start | bytes 2752520 | tf_op jit(solution)/shard_map/ppermute | solution.py:144
  137.3 6.5 %collective-permute-start.30 = (f32[112,112]{1,0:T(8,128)}, f32[112,112]{1,0:T(8,128)S(1)}, u32[]{:S(2)}, u32[]{:S(2)}) collective-permute-start(f32[112,112]{1,0:T(8,128)} %get-tuple-element.55), channel_id=1, source_target_pairs={{0,2},{1,3},{2,4},{3,5},{4,6},{5,7},{6,8},{7,9},{8,10},{9,11},{10,... | collective-permute-start | bytes 150536 | tf_op jit(solution)/shard_map/ppermute | solution.py:329
  137.3 7.2 %collective-permute-start.31 = (f32[112,112]{1,0:T(8,128)}, f32[112,112]{1,0:T(8,128)S(1)}, u32[]{:S(2)}, u32[]{:S(2)}) collective-permute-start(f32[112,112]{1,0:T(8,128)} %get-tuple-element.56), channel_id=1, source_target_pairs={{0,3},{1,4},{2,5},{3,6},{4,7},{5,8},{6,9},{7,10},{8,11},{9,12},{10... | collective-permute-start | bytes 150536 | tf_op jit(solution)/shard_map/ppermute | solution.py:329
  137.4 34.2 %collective-permute-start.32 = (f32[112,112]{1,0:T(8,128)}, f32[112,112]{1,0:T(8,128)S(1)}, u32[]{:S(2)}, u32[]{:S(2)}) collective-permute-start(f32[112,112]{1,0:T(8,128)} %get-tuple-element.57), channel_id=1, source_target_pairs={{0,4},{1,5},{2,6},{3,7},{4,8},{5,9},{6,10},{7,11},{8,12},{9,13},{1... | collective-permute-start | bytes 150536 | tf_op jit(solution)/shard_map/ppermute | solution.py:329
  138.9 32.6 %collective-permute-start.33 = (f32[112,112]{1,0:T(8,128)}, f32[112,112]{1,0:T(8,128)S(1)}, u32[]{:S(2)}, u32[]{:S(2)}) collective-permute-start(f32[112,112]{1,0:T(8,128)} %get-tuple-element.58), channel_id=1, source_target_pairs={{0,5},{1,6},{2,7},{3,8},{4,9},{5,10},{6,11},{7,12},{8,13},{9,14},{... | collective-permute-start | bytes 150536 | tf_op jit(solution)/shard_map/ppermute | solution.py:329
  143.9 27.7 %collective-permute-start.34 = (f32[112,112]{1,0:T(8,128)}, f32[112,112]{1,0:T(8,128)S(1)}, u32[]{:S(2)}, u32[]{:S(2)}) collective-permute-start(f32[112,112]{1,0:T(8,128)} %get-tuple-element.59), channel_id=1, source_target_pairs={{0,6},{1,7},{2,8},{3,9},{4,10},{5,11},{6,12},{7,13},{8,14},{9,15},... | collective-permute-start | bytes 150536 | tf_op jit(solution)/shard_map/ppermute | solution.py:329
  144.5 27.1 %collective-permute-start.35 = (f32[112,112]{1,0:T(8,128)}, f32[112,112]{1,0:T(8,128)S(1)}, u32[]{:S(2)}, u32[]{:S(2)}) collective-permute-start(f32[112,112]{1,0:T(8,128)} %get-tuple-element.60), channel_id=1, source_target_pairs={{0,7},{1,8},{2,9},{3,10},{4,11},{5,12},{6,13},{7,14},{8,15},{9,0},... | collective-permute-start | bytes 150536 | tf_op jit(solution)/shard_map/ppermute | solution.py:329
  (20 other events, 266.6 us)

commit v2 on v0

--- a/solution.py
+++ b/solution.py
@@ -1,12 +1,459 @@
+import functools
+
 import jax
 import jax.numpy as jnp
 from jax import lax
+from jax.experimental import pallas as pl
+from jax.experimental.pallas import tpu as pltpu
 from jax.sharding import PartitionSpec as P
 
 LWIN = 8
+STRIDE = 8
+BLK = 256
+EXACT = lax.Precision.HIGHEST
+VMEM_LIMIT = 56 * 2**20
+
+SMEM_SPEC = pl.BlockSpec(memory_space=pltpu.SMEM)
+VMEM_SPEC = pl.BlockSpec(memory_space=pltpu.VMEM)
+NT = (((1,), (1,)), ((), ()))
+
+
+def f32(*shape):
+    return jax.ShapeDtypeStruct(shape, jnp.float32)
+
+
+def bf16(*shape):
+    return jax.ShapeDtypeStruct(shape, jnp.bfloat16)
+
+
+def dot_nt(a, b, precision=None):
+    return lax.dot_general(a, b, NT, precision=precision, preferred_element_type=jnp.float32)
+
+
+def call(kernel, ins, out_shape, scratch=()):
+    return pl.pallas_call(
+        kernel,
+        out_shape=out_shape,
+        in_specs=[SMEM_SPEC if x.dtype == jnp.int32 and x.ndim == 1 else VMEM_SPEC for x in ins],
+        out_specs=jax.tree.map(lambda _: VMEM_SPEC, out_shape),
+        scratch_shapes=list(scratch),
+        compiler_params=pltpu.CompilerParams(vmem_limit_bytes=VMEM_LIMIT),
+        cost_estimate=pl.CostEstimate(flops=1, bytes_accessed=1, transcendentals=0),
+    )(*ins)
+
+
+def owner_of(m, order):
+    last = len(order) - 1
+    return sum(((m >> (last - k)) & 1) << bit for k, bit in enumerate(order))
+
+
+def front_kernel(order, me_ref, count_ref, offset_ref, resid_ref, feat_ref, sent_ref, kept_ref, jt_ref, r_ref, jp_ref, n21_ref):
+    tiles, slots = offset_ref.shape
+    depth, params = feat_ref.shape
+    samples = depth // tiles
+    cap = jp_ref.shape[1]
+    panel = jp_ref.shape[0]
+    trail = params - panel
+    core = me_ref[0] & 1
+    lane = lax.broadcasted_iota(jnp.int32, (8, cap), 1)
+    start = jnp.full((8, cap), -depth, jnp.int32)
+    resid = jnp.zeros((8, cap), jnp.float32)
+    before = jnp.int32(0)
+    for t in range(tiles):
+        count = count_ref[t]
+        live = (lane >= before) & (lane < before + count)
+        offs = jnp.concatenate([offset_ref[t : t + 1, :], jnp.zeros((1, cap - slots), jnp.int32)], axis=1)
+        offs = pltpu.roll(jnp.broadcast_to(offs, (8, cap)), before, 1)
+        res = jnp.concatenate([resid_ref[t : t + 1, :].astype(jnp.float32), jnp.zeros((1, cap - slots), jnp.float32)], axis=1)
+        res = pltpu.roll(jnp.broadcast_to(res, (8, cap)), before, 1)
+        start = jnp.where(live, offs + t * samples, start)
+        resid = jnp.where(live, res, resid)
+        before = before + count
+    first = lax.broadcasted_iota(jnp.int32, (8, cap), 0) == 0
+    resid = jnp.where(first, resid, 0.0).astype(jnp.bfloat16)
+    r_ref[...] = jnp.concatenate([resid, jnp.zeros((8, cap), jnp.bfloat16)], axis=0)
+    after = lax.broadcasted_iota(jnp.int32, (depth, cap), 0) - start[0:1, :]
+    window = jnp.where((after >= 0) & (after < LWIN), 1.0 / LWIN, 0.0).astype(jnp.bfloat16)
+    pan_b = BLK // STRIDE
+    row = lax.broadcasted_iota(jnp.int32, (BLK, BLK), 0)
+    col = lax.broadcasted_iota(jnp.int32, (BLK, BLK), 1)
+    rest = row - pan_b
+    source = jnp.where(row < pan_b, row * STRIDE, rest + 1 + ((rest * 9363) >> 16))
+    pick = jnp.where(source == col, 1.0, 0.0).astype(jnp.bfloat16)
+    trail_b = BLK - pan_b
+    for b in range(params // BLK):
+        turned = dot_nt(pick, feat_ref[:, b * BLK : (b + 1) * BLK]).astype(jnp.bfloat16)
+        jac = jnp.dot(turned, window, preferred_element_type=jnp.float32).astype(jnp.bfloat16)
+        jp_ref[b * pan_b : (b + 1) * pan_b, :] = jac[:pan_b]
+        jt_ref[b * trail_b : (b + 1) * trail_b, :] = jac[pan_b:]
+        if trail + (b + 1) * trail_b <= jt_ref.shape[0]:
+            jt_ref[trail + b * trail_b : trail + (b + 1) * trail_b, :] = jac[pan_b:]
+    jp = jp_ref[...]
+    n21_ref[...] = dot_nt(jt_ref[:trail, :], jp)
+    own, count = sent_ref.shape[1], sent_ref.shape[0] - 1
+    for m in range(count):
+        base = owner_of(m, order) * own
+        sent_ref[m] = n21_ref[pl.ds(pl.multiple_of(base + (1 - core) * own, 16), own), :]
+        kept_ref[m] = n21_ref[pl.ds(pl.multiple_of(base + core * own, 16), own), :]
+    half, rows = panel // 2, panel // 4
+    n21_ref[:panel, :] = dot_nt(jp, jp)
+    grad = dot_nt(r_ref[...], jp)
+    for ref, which in ((sent_ref, 1 - core), (kept_ref, core)):
+        for side in range(2):
+            lanes = slice(side * half, (side + 1) * half)
+            at = pl.multiple_of(which * half + side * rows, 16)
+            first = n21_ref[pl.ds(at, rows), :]
+            ref[count, :rows, lanes] = jnp.where(which == 1, first[:, half:], first[:, :half])
+            at = pl.multiple_of(half + which * rows + side * (rows // 2), 16)
+            ref[count, rows : rows + rows // 2, lanes] = n21_ref[pl.ds(at, rows // 2), :half]
+        ref[count, rows + rows // 2 :, :] = grad[: own - rows - rows // 2]
+
+
+def trail_kernel(me_ref, jt_ref, r_ref, sent1_ref, sent2_ref, kept1_ref, kept2_ref, pair_ref):
+    base = pl.program_id(0) * 2 * sent1_ref.shape[1]
+    core = me_ref[0] & 1
+    own, wide = sent1_ref.shape[1:]
+    end = wide + sent2_ref.shape[2]
+    real = end - r_ref.shape[0]
+    rows = jt_ref[pl.ds(pl.multiple_of(base, 16), 2 * own), :]
+    others = jt_ref[pl.ds(pl.multiple_of(base, 16), real + own), :]
+    both = dot_nt(rows, others)
+    last = dot_nt(rows, r_ref[...])
+    pair_ref[0, :, :real] = both[:own, :real]
+    pair_ref[0, :, real:] = last[:own]
+    pair_ref[1, :, :real] = both[own:, own:]
+    pair_ref[1, :, real:] = last[own:]
+    for first, second, which in ((sent1_ref, sent2_ref, 1 - core), (kept1_ref, kept2_ref, core)):
+        first[0] = pair_ref[which, :, :wide]
+        second[0] = pair_ref[which, :, wide:]
+
+
+def place_of(m, order):
+    return sum(((m >> (bit - 1)) & 1) << (len(order) - 1 - k) for k, bit in enumerate(order))
+
+
+def trailing(me1, jt, r, orders, half, own, widths):
+    def spec(order, wide):
+        return pl.BlockSpec((1, own, wide), lambda m: (place_of(m, order), 0, 0))
+
+    return pl.pallas_call(
+        trail_kernel,
+        grid=(half,),
+        out_shape=[f32(half, own, wide) for wide in widths] * 2,
+        in_specs=[SMEM_SPEC, pl.BlockSpec(jt.shape, lambda m: (0, 0)), pl.BlockSpec(r.shape, lambda m: (0, 0))],
+        out_specs=[spec(order, wide) for order, wide in zip(orders, widths)] * 2,
+        scratch_shapes=[pltpu.VMEM((2, own, sum(widths)), jnp.float32)],
+        compiler_params=pltpu.CompilerParams(vmem_limit_bytes=VMEM_LIMIT),
+        cost_estimate=pl.CostEstimate(flops=1, bytes_accessed=1, transcendentals=0),
+    )(me1, jt, r)
+
+
+def swap(x, axis, bit):
+    n = lax.axis_size(axis)
+    return lax.ppermute(x, axis, [(i, i ^ (1 << bit)) for i in range(n)])
+
+
+def panel_fold_kernel(bit, me_ref, kept_ref, got_ref, sent_out, kept_out):
+    mine = (me_ref[0] >> bit) & 1
+    size = kept_out.shape[0] - 1
+    for k in range(size):
+        sent_out[k] = kept_ref[(1 - mine) * size + k] + got_ref[(1 - mine) * size + k]
+        kept_out[k] = kept_ref[mine * size + k] + got_ref[mine * size + k]
+    total = kept_ref[2 * size] + got_ref[2 * size]
+    sent_out[size] = total
+    kept_out[size] = total
+
+
+def fold(kept, got, me, bit):
+    mine = (me >> bit) & 1
+    size = kept.shape[0] // 2
+    kept = kept.reshape((2, size) + kept.shape[1:])
+    got = got.reshape(kept.shape)
+
+    def part(which):
+        return lax.dynamic_index_in_dim(kept, which, 0, False) + lax.dynamic_index_in_dim(got, which, 0, False)
+
+    return part(1 - mine), part(mine)
+
+
+def mirror(sums, own, ks, row):
+    flat = [x for pair in sums for x in pair]
+    widths = [pair[0].shape[-1] for pair in sums]
+    new = [len(pair) == 2 for pair in sums]
+    total = sum(widths)
+
+    def kernel(*refs):
+        ins, outs = list(refs[: len(flat)]), list(refs[len(flat) :])
+        turned_ref = outs.pop()
+        at = 0
+        for wide, pair in zip(widths, new):
+            x = ins.pop(0)
+            x = x[0] + ins.pop(0)[0] if pair else x[...]
+            if pair:
+                outs.pop(0)[...] = x
+            turned_ref[at : at + wide, :] = x.T
+            at += wide
+        for k in ks:
+            outs.pop(0)[...] = turned_ref[k * own : (k + 1) * own, :]
+        if row:
+            outs.pop(0)[...] = turned_ref[row : row + 8, :]
+
+    shapes = [f32(own, w) for w, pair in zip(widths, new) if pair] + [f32(own, own)] * len(ks) + [f32(8, own)] * bool(row)
+    out = list(call(kernel, flat, shapes, [pltpu.VMEM((total, own), jnp.float32)]))
+    return out[: sum(new)], out[sum(new) : sum(new) + len(ks)], out[-1]
+
+
+def factor_block(a):
+    size = a.shape[0]
+    shape = (8, size)
+    lane = lax.broadcasted_iota(jnp.int32, shape, 1)
+    sub = lax.broadcasted_iota(jnp.int32, shape, 0)
+    groups = [a[at : at + 8] for at in range(0, size, 8)]
+
+    def column(x, j):
+        return jnp.broadcast_to(x[:, j : j + 1], shape)
+
+    def row(x, s):
+        return jnp.broadcast_to(x[s : s + 1, :], shape)
+
+    uppers, lowers = [], []
+    for g, x in enumerate(groups):
+        first = 8 * g
+        inside = (lane >= first) & (lane < first + 8)
+        columns = [column(x, first + k) for k in range(8)]
+        pivots = jnp.zeros(shape, jnp.float32)
+        inverses, rows, cross = [], [], {}
+        for k in range(8):
+            pivot = row(columns[k], k)
+            inverse = pltpu.reciprocal(pivot, approx=True)
+            inverse = inverse * (2.0 - pivot * inverse)
+            scaled = columns[k] * inverse
+            for m in range(k + 1, 8):
+                cross[k, m] = row(columns[m], k)
+                columns[m] = columns[m] - scaled * cross[k, m]
+            at = lane == first + k
+            this = jnp.where(at, 1.0, row(x, k))
+            x = jnp.where(at & (sub >= k), jnp.where(sub == k, 1.0, 0.0), x) - jnp.where(sub > k, scaled, 0.0) * this
+            pivots = jnp.where(sub == k, pivot, pivots)
+            inverses.append(inverse)
+            rows.append(jnp.where(inside & (lane > first + k), 0.0, this))
+        for h in range(g + 1, len(groups)):
+            below = groups[h]
+            columns = [column(below, first + k) for k in range(8)]
+            below = jnp.where(inside, 0.0, below)
+            for k in range(8):
+                scaled = columns[k] * inverses[k]
+                for m in range(k + 1, 8):
+                    columns[m] = columns[m] - scaled * cross[k, m]
+                below = below - scaled * rows[k]
+            groups[h] = below
+        root = lax.rsqrt(pivots)
+        root = root * (1.5 - 0.5 * pivots * root * root)
+        scaled = x * root
+        off = lane - first - sub
+        uppers.append(jnp.where(off > 0, scaled, jnp.where(off == 0, pivots * root, 0.0)))
+        lowers.append(jnp.where(off <= 0, scaled, 0.0))
+    return jnp.concatenate(uppers, axis=0).T, jnp.concatenate(lowers, axis=0)
+
+
+def factor_first_kernel(me_ref, mine_ref, other_ref, damp_ref, g_ref, l11_ref, i11_ref, l21_ref, rest_ref):
+    core = me_ref[0] & 1
+    half = l11_ref.shape[0]
+    rows = half // 2
+    mine, other = mine_ref[0], other_ref[0]
+    low, high = jnp.where(core == 0, mine, other), jnp.where(core == 0, other, mine)
+
+    def opened(x):
+        return jnp.concatenate([x[:, :half], x[:, half:]], axis=0)
+
+    row = lax.broadcasted_iota(jnp.int32, (half, half), 0)
+    col = lax.broadcasted_iota(jnp.int32, (half, half), 1)
+    n11 = opened(low[:rows]) + jnp.where(row == col, damp_ref[:half, 0:1], 0.0)
+    n22 = opened(high[:rows]) + jnp.where(row == col, damp_ref[half:, 0:1], 0.0)
+    n21 = jnp.concatenate([opened(x[rows : rows + rows // 2]) for x in (low, high)], axis=0)
+    g_ref[...] = mine[rows + rows // 2 : rows + rows // 2 + 8]
+    l11, i11 = factor_block(n11)
+    l21 = dot_nt(n21, i11, EXACT)
+    l11_ref[...] = l11
+    i11_ref[...] = i11
+    l21_ref[...] = l21
+    rest_ref[...] = n22 - dot_nt(l21, l21, EXACT)
+
+
+def factor_second_kernel(l11_ref, i11_ref, l21_ref, rest_ref, factor_ref, inverse_ref):
+    half = l11_ref.shape[0]
+    l22, i22 = factor_block(rest_ref[...])
+    before = jnp.dot(l21_ref[...], i11_ref[...], precision=EXACT, preferred_element_type=jnp.float32)
+    zero = jnp.zeros((half, half), jnp.float32)
+    factor_ref[:half, :half] = l11_ref[...]
+    factor_ref[:half, half:] = zero
+    factor_ref[half:, :half] = l21_ref[...]
+    factor_ref[half:, half:] = l22
+    inverse_ref[:half, :half] = i11_ref[...]
+    inverse_ref[:half, half:] = zero
+    inverse_ref[half:, :half] = -jnp.dot(i22, before, precision=EXACT, preferred_element_type=jnp.float32)
+    inverse_ref[half:, half:] = i22
+
+
+def lower_kernel(inverse_ref, g1_ref, held_ref, lower_ref, out_ref, y_ref, flat_ref):
+    inverse = inverse_ref[...]
+    count, own, size = held_ref.shape
+    lower = dot_nt(held_ref[...].reshape(count * own, size), inverse, EXACT).reshape(count, own, size)
+    lower_ref[...] = lower
+    out_ref[...] = lower[0]
+    y = dot_nt(g1_ref[...], inverse, EXACT)
+    y_ref[...] = y
+    flat_ref[...] = y[0]
+
+
+def product_kernel(bits, me_ref, mine_ref, other_ref, product_ref, all_ref):
+    me = me_ref[0]
+    own = product_ref.shape[0]
+    for k in range(mine_ref.shape[0]):
+        owner = me ^ sum(((k >> i) & 1) << bit for i, bit in enumerate(bits))
+        all_ref[pl.ds(pl.multiple_of(owner * own, 16), own), :] = mine_ref[k]
+        all_ref[pl.ds(pl.multiple_of((owner ^ 1) * own, 16), own), :] = other_ref[k]
+    product_ref[...] = dot_nt(mine_ref[0], all_ref[...], EXACT)
+
+
+def last_kernel(n_chunks, me_ref, damp_ref, product_ref, g2_ref, y_ref, lower_ref, *refs):
+    chunks, mirrors, (schur_ref, rhs_ref) = refs[:n_chunks], refs[n_chunks:-2], refs[-2:]
+    rhs_ref[...] = (g2_ref[...] - dot_nt(y_ref[...], lower_ref[...], EXACT))[0]
+    me = me_ref[0]
+    own = schur_ref.shape[0]
+    whole = jnp.concatenate([c[...] for c in chunks], axis=1)[:, : own * (len(mirrors) + 2)]
+    row = lax.broadcasted_iota(jnp.int32, (own, own), 0)
+    col = lax.broadcasted_iota(jnp.int32, (own, own), 1)
+    nat = own * STRIDE // (STRIDE - 1)
+    target = lax.broadcasted_iota(jnp.int32, (own, nat), 0)
+    target = target + 1 + ((target * 9363) >> 16)
+    pick = target == lax.broadcasted_iota(jnp.int32, (own, nat), 1)
+    damp = jnp.sum(jnp.where(pick, damp_ref[pl.ds(me, 1), :], 0.0), axis=1, keepdims=True)
+    first = whole[:, :own] + jnp.where(row == col, damp, 0.0)
+    whole = jnp.concatenate([first, whole[:, own:]] + [m[...] for m in reversed(mirrors)], axis=1)
+    schur_ref[...] = pltpu.roll(whole, me * own, 1) - product_ref[...]
 
 
 def per_device(features, gauge_offset, gauge_count, gauge_resid, damping):
+    tiles_here, samples, params = features.shape
+    slots = gauge_offset.shape[1]
+    axis = "tile"
+    n = lax.axis_size(axis)
+    panel = params // STRIDE
+    trail = params - panel
+    own = trail // n
+    if n != 16 or own != 112 or params % BLK:
+        return per_device_plain(features, gauge_offset, gauge_count, gauge_resid, damping)
+    cap = tiles_here * slots // 2
+    count = n // 2 - 1
+    half = n // 2
+    widths = (640, 384)
+    me = lax.axis_index(axis)
+    me1 = me.astype(jnp.int32).reshape(1)
+    order = [1, 2, 3]
+    orders = [order, order]
+    ext = trail + own * half
+    last = [()]
+
+    def then(*xs):
+        xs, last[0] = lax.optimization_barrier((xs, last[0]))
+        return xs
+
+    def did(x):
+        last[0] = x
+        return x
+
+    sent, p, jt, r = did(
+        call(
+            functools.partial(front_kernel, order),
+            (me1, gauge_count, gauge_offset, gauge_resid, features.reshape(tiles_here * samples, params)),
+            [f32(half + 1, own, panel)] * 2 + [bf16(ext, cap), bf16(16, cap)],
+            [pltpu.VMEM((panel, cap), jnp.bfloat16), pltpu.VMEM((trail, panel), jnp.float32)],
+        )
+    )
+    p_got = swap(sent, axis, 0)
+    t, t_got = [None, None], [None, None]
+
+    def panel_fold(p, got, bit):
+        shape = f32(p.shape[0] // 2 + 1, *p.shape[1:])
+        sent, p = did(call(functools.partial(panel_fold_kernel, bit), then(me1, p, got), [shape] * 2))
+        return p, swap(sent, axis, bit)
+
+    def trail_fold(q, step):
+        bit = orders[q][step]
+        sent, t[q] = did(fold(*then(t[q], t_got[q]), me, bit))
+        t_sent[q] = sent
+
+    def trail_send(q, step):
+        t_got[q] = swap(t_sent[q], axis, orders[q][step])
+
+    def trail_step(q, step):
+        trail_fold(q, step)
+        trail_send(q, step)
+
+    def joined(held, got):
+        return did(jnp.concatenate(then(held, got), axis=0))
+
+    t_sent = [None, None]
+    p, p_got = panel_fold(p, p_got, order[0])
+    *t_sent, t[0], t[1] = did(trailing(*then(me1, jt, r), orders, half, own, widths))
+    t_sent, p_got = lax.optimization_barrier((t_sent, p_got))
+    t_got = [swap(x, axis, 0) for x in t_sent]
+    p, p_got = panel_fold(p, p_got, order[1])
+    trail_step(0, 0)
+    p, p_got = panel_fold(p, p_got, order[2])
+    trail_step(1, 0)
+    damp_panel, damp_trail = then(damping)[0].reshape(panel, STRIDE), damping.reshape(n, params // n)
+    damp_panel = did(damp_panel)
+    p, p_got = then(p, p_got)
+    p = did(p + p_got)
+    held, n11 = p[:1], p[1:]
+    n11_got = swap(n11, axis, 0)
+    got = swap(held, axis, order[2])
+    g1, *state = did(
+        call(factor_first_kernel, then(me1, n11, n11_got, damp_panel), [f32(8, panel)] + [f32(panel // 2, panel // 2)] * 4)
+    )
+    held = joined(held, got)
+    got = swap(held, axis, order[1])
+    trail_step(0, 1)
+    factor, inverse = did(call(factor_second_kernel, then(*state), [f32(panel, panel)] * 2))
+    held = joined(held, got)
+    got = swap(held, axis, order[0])
+    trail_step(1, 1)
+    trail_step(0, 2)
+    held = joined(held, got)
+    mine, lower, y, y0 = did(
+        call(lower_kernel, then(inverse, g1, held), [f32(half, own, panel), f32(own, panel), f32(8, panel), f32(panel)])
+    )
+    trail_step(1, 2)
+    other = swap(lax.optimization_barrier((mine, t[1]))[0], axis, 0)
+    ks = [range(1, widths[0] // own), range(widths[0] // own, count + 1)]
+    (c0,), blocks, _ = did(mirror([then(t[0], t_got[0])], own, ks[0], 0))
+
+    def mirrored(blocks, ks):
+        return [lax.ppermute(b, axis, [(i, (i + k) % n) for i in range(n)]) for k, b in zip(ks, blocks)]
+
+    mirrors = mirrored(blocks, ks[0])
+    product = did(
+        call(
+            functools.partial(product_kernel, list(reversed(order))),
+            then(me1, mine, other),
+            f32(own, trail),
+            [pltpu.VMEM((trail, panel), jnp.float32)],
+        )
+    )
+    (c1,), blocks, g2 = did(mirror([(c0,), then(t[1], t_got[1])], own, ks[1], (count + 2) * own))
+    mirrors += mirrored(blocks, ks[1])
+    chunks = [c0, c1]
+    schur, rhs0 = call(
+        functools.partial(last_kernel, 2),
+        then(me1, damp_trail, product, g2, y, lower, *chunks, *mirrors),
+        [f32(own, trail), f32(own)],
+    )
+    return (factor, lower, schur, y0, rhs0)
+
+
+def per_device_plain(features, gauge_offset, gauge_count, gauge_resid, damping):
     tiles_here, samples, params = features.shape
     slots = gauge_offset.shape[1]
     panel = params // 8
@@ -30,14 +477,10 @@
     jac_split = jac.reshape(gauges, panel, 8)
     jac_panel = jac_split[:, :, 0]
     jac_trail = jac_split[:, :, 1:].reshape(gauges, trail)
-    panel_local = lax.dot_general(
-        jac, jac_panel, (((0,), (0,)), ((), ())), preferred_element_type=jnp.float32
-    )
+    panel_local = lax.dot_general(jac, jac_panel, (((0,), (0,)), ((), ())), preferred_element_type=jnp.float32)
     panel_all, grad = lax.psum((panel_local, grad_local), "tile")
     own_trail = lax.psum_scatter(
-        lax.dot_general(
-            jac_trail, jac_trail, (((0,), (0,)), ((), ())), preferred_element_type=jnp.float32
-        ),
+        lax.dot_general(jac_trail, jac_trail, (((0,), (0,)), ((), ())), preferred_element_type=jnp.float32),
         "tile",
         scatter_dimension=0,
         tiled=True,
@@ -51,17 +494,13 @@
     n11 = panel_split[:, 0, :] + jnp.diag(damp_split[:, 0])
     n21 = panel_split[:, 1:, :].reshape(trail, panel)
     panel_factor = jnp.linalg.cholesky(n11)
-    lower_all = lax.linalg.triangular_solve(
-        panel_factor, n21, left_side=False, lower=True, transpose_a=True
-    )
+    lower_all = lax.linalg.triangular_solve(panel_factor, n21, left_side=False, lower=True, transpose_a=True)
     lower_own = lax.dynamic_slice_in_dim(lower_all, index * owned_trail, owned_trail, 0)
     schur = own_trail - jnp.dot(lower_own, lower_all.T, precision=lax.Precision.HIGHEST)
     grad_split = grad.reshape(panel, 8)
     first_part = grad_split[:, 0]
     second_part = grad_split[:, 1:].reshape(trail)
-    panel_rhs = lax.linalg.triangular_solve(
-        panel_factor, first_part[:, None], left_side=True, lower=True
-    )[:, 0]
+    panel_rhs = lax.linalg.triangular_solve(panel_factor, first_part[:, None], left_side=True, lower=True)[:, 0]
     second_own = lax.dynamic_slice_in_dim(second_part, index * owned_trail, owned_trail, 0)
     trail_rhs = second_own - jnp.dot(lower_own, panel_rhs, precision=lax.Precision.HIGHEST)
     return (panel_factor, lower_own, schur, panel_rhs, trail_rhs)

time: 301 us -> 153 us (0.51)
  blocking collectives: 59.6 us -> 0 us
  Pallas kernels: 0 us -> 56.1 us
  local copies, waits for them, and re-layouts: 58 us -> 8.48 us
  other arithmetic: 58.1 us -> 10.9 us
  matrix products: 41.5 us -> 0 us
  starting transfers between devices: 0.08 us -> 28.6 us
  waiting for transfers between devices: 65.2 us -> 47.5 us
  between operations: 15.6 us -> 0.79 us
    reduce_scatter x1 -> x0, waiting for transfers between devices: 64.8 us -> none  [per_device(): lax.psum_scatter(lax.dot_general(jac_trail, jac_trail, (((0,), (0,)), (()...]
    psum x1 -> x0, blocking collectives: 59.6 us -> none  [per_device(): panel_all, grad = lax.psum((panel_local, grad_local), 'tile')]
    pallas_call x0 -> x12, Pallas kernels: none -> 56.1 us  [the longest x11 45.2 us: call(): pl.pallas_call(kernel, out_shape=out_shape, in_specs=[SMEM_SPEC if x.dtyp...]
    another operation x11 -> x0, other arithmetic: 54.6 us -> none  [the longest x6 33.9 us: per_device(): panel_factor = jnp.linalg.cholesky(n11)]
    ppermute x0 -> x24, waiting for transfers between devices: none -> 47.5 us  [the longest x17 40.1 us: swap(): return lax.ppermute(x, axis, [(i, i ^ 1 << bit) for i in range(n)])]
    dot_general x6 -> x0, matrix products: 35.6 us -> none  [the longest x1 17.1 us: per_device(): lax.dot_general(jac_trail, jac_trail, (((0,), (0,)), ((), ())), preferred...]
    ppermute x0 -> x24, starting transfers between devices: none -> 28.6 us  [the longest x17 20.6 us: swap(): return lax.ppermute(x, axis, [(i, i ^ 1 << bit) for i in range(n)])]
    slice x8 -> x1, local copies, waits for them, and re-layouts: 15.8 us -> 0.02 us  [per_device(): held, n11 = (p[:1], p[1:])]
  transfers between devices with their start and end apart: 2 -> 24, of which waited for: 2 -> 12; matrix products, arithmetic and copies ran while one was open for 38% -> 9% of each run, Pallas kernels for 0% -> 26%
where the time goes in v2:
time: 153 us; the launch traced here: 152 us
  Pallas kernels  56.1 us (37%)
  waiting for transfers between devices  47.5 us (31%)
  starting transfers between devices  28.6 us (19%)
  other arithmetic  10.9 us (7%)
  local copies, waits for them, and re-layouts  8.48 us (6%)
    pallas_call x11, Pallas kernels, call(): pl.pallas_call(kernel, out_shape=out_shape, in_specs=[SMEM_SPEC if x.dtyp...  45.2 us
    ppermute x17, waiting for transfers between devices, swap(): return lax.ppermute(x, axis, [(i, i ^ 1 << bit) for i in range(n)])  40.1 us
    ppermute x17, starting transfers between devices, swap(): return lax.ppermute(x, axis, [(i, i ^ 1 << bit) for i in range(n)])  20.6 us
    pallas_call x1, Pallas kernels, trailing(): pl.pallas_call(trail_kernel, grid=(half,), out_shape=[f32(half, own, wide...  11 us
    add x6, other arithmetic, part(): lax.dynamic_index_in_dim(kept, which, 0, False)  8.93 us
    ppermute x7, starting transfers between devices, mirrored(): lax.ppermute(b, axis, [(i, (i + k) % n) for i in range(n)])  7.95 us
    ppermute x7, waiting for transfers between devices, mirrored(): lax.ppermute(b, axis, [(i, (i + k) % n) for i in range(n)])  7.35 us
    unnamed x38, local copies, waits for them, and re-layouts  6.12 us
  transfers between devices with their start and end apart: 24, of which 12 were waited for; matrix products, arithmetic and copies ran while one was open for 9% of the time, Pallas kernels for 26%

profile of v2, /device:TPU:1, one launch (start us, length us, event | category | flops | bytes accessed | tf_op | source)
XLA Modules:
  0.0 152.4 jit_solution(11844313327803436304)
XLA Ops:
  0.6 11.0 %shard_map.92 = (f32[9,112,256]{2,1,0:T(8,128)}, f32[9,112,256]{2,1,0:T(8,128)}, bf16[2688,768]{1,0:T(8,128)(2,1)}, bf16[16,768]{1,0:T(8,128)(2,1)}) custom-call(s32[1]{0:T(128)} %bitcast.me_ref, s32[4]{0:T(128)} %count_ref.1, s32[4,384]{1,0:T(4,128)} %offset_ref.1, bf16[4,384]{1,0:T(4,128)(2,1)} %resid_ref.1, bf16[1024,2048]{1,0:T(8,128)(2,1)} %bitcast.28), custom_call_target="tpu_custom_call" | custom-call | flops 1 | bytes 1 | tf_op jit(solution)/shard_map/pallas_call | solution.py:34
  11.7 2.8 %collective-permute-done.got_ref = f32[9,112,256]{2,1,0:T(8,128)S(1)} collective-permute-done((f32[9,112,256]{2,1,0:T(8,128)}, f32[9,112,256]{2,1,0:T(8,128)S(1)}, u32[]{:S(2)}, u32[]{:S(2)}) %collective-permute-start) | collective-permute-done | bytes 1032224 | tf_op jit(solution)/shard_map/ppermute | solution.py:153
  15.5 2.6 %shard_map.93 = (f32[5,112,256]{2,1,0:T(8,128)}, f32[5,112,256]{2,1,0:T(8,128)}) custom-call(s32[1]{0:T(128)} %bitcast.me_ref, f32[9,112,256]{2,1,0:T(8,128)} %get-tuple-element.117.kept_ref, f32[9,112,256]{2,1,0:T(8,128)} %copy-done.1), custom_call_target="tpu_custom_call" | custom-call | flops 1 | bytes 1 | tf_op jit(solution)/shard_map/pallas_call | solution.py:34
  18.1 2.4 %collective-permute-start.1 = (f32[5,112,256]{2,1,0:T(8,128)}, f32[5,112,256]{2,1,0:T(8,128)S(1)}, u32[]{:S(2)}, u32[]{:S(2)}) collective-permute-start(f32[5,112,256]{2,1,0:T(8,128)} %get-tuple-element.120), channel_id=1, source_target_pairs={{0,2},{1,3},{2,0},{3,1},{4,6},{5,7},{6,4},{7,5},{8,10},{9,11},{10,... | collective-permute-start | bytes 1720328 | tf_op jit(solution)/shard_map/ppermute | solution.py:153
  20.5 11.0 %shard_map.94 = (f32[8,112,640]{2,1,0:T(8,128)}, f32[8,112,384]{2,1,0:T(8,128)}, f32[8,112,640]{2,1,0:T(8,128)}, f32[8,112,384]{2,1,0:T(8,128)}) custom-call(s32[1]{0:T(128)} %bitcast.me_ref, bf16[2688,768]{1,0:T(8,128)(2,1)} %get-tuple-element.122.jt_ref, bf16[16,768]{1,0:T(8,128)(2,1)} %get-tuple-element.123.r_ref), custom_call_target="tpu_custom_call" | custom-call | flops 1 | bytes 1 | tf_op jit(solution)/shard_map/pallas_call | solution.py:139
  31.5 2.3 %collective-permute-done.1.got_ref = f32[5,112,256]{2,1,0:T(8,128)S(1)} collective-permute-done((f32[5,112,256]{2,1,0:T(8,128)}, f32[5,112,256]{2,1,0:T(8,128)S(1)}, u32[]{:S(2)}, u32[]{:S(2)}) %collective-permute-start.1) | collective-permute-done | bytes 573472 | tf_op jit(solution)/shard_map/ppermute | solution.py:153
  34.7 2.1 %shard_map.95 = (f32[3,112,256]{2,1,0:T(8,128)}, f32[3,112,256]{2,1,0:T(8,128)}) custom-call(s32[1]{0:T(128)} %bitcast.me_ref, f32[5,112,256]{2,1,0:T(8,128)} %get-tuple-element.130.kept_ref, f32[5,112,256]{2,1,0:T(8,128)} %copy-done.3), custom_call_target="tpu_custom_call" | custom-call | flops 1 | bytes 1 | tf_op jit(solution)/shard_map/pallas_call | solution.py:34
  36.8 1.5 collective-permute-start.2
  38.3 2.6 %collective-permute-done.3 = f32[8,112,640]{2,1,0:T(8,128)S(1)} collective-permute-done((f32[8,112,640]{2,1,0:T(8,128)}, f32[8,112,640]{2,1,0:T(8,128)S(1)}, u32[]{:S(2)}, u32[]{:S(2)}) %collective-permute-start.3) | collective-permute-done | bytes 2293792 | tf_op jit(solution)/shard_map/ppermute | solution.py:153
  40.9 3.0 %add_bitcast_fusion = (f32[4,112,640]{2,1,0:T(8,128)S(1)}, f32[4,112,640]{2,1,0:T(8,128)}) fusion(f32[2,4,112,640]{3,2,1,0:T(8,128)S(1)} %bitcast.31, s32[]{:T(128)S(6)} %select_n.43, f32[2,4,112,640]{3,2,1,0:T(8,128)} %bitcast.30, s32[]{:T(128)S(6)} %select_n.42), kind=kLoop, calls=%fused_computation | loop fusion | flops 573440 | bytes 6881288 | tf_op jit(solution)/shard_map/add | solution.py:174
  43.9 1.5 collective-permute-start.7
  46.6 1.9 %shard_map.96 = (f32[2,112,256]{2,1,0:T(8,128)}, f32[2,112,256]{2,1,0:T(8,128)}) custom-call(s32[1]{0:T(128)} %bitcast.me_ref, f32[3,112,256]{2,1,0:T(8,128)} %get-tuple-element.138.kept_ref, f32[3,112,256]{2,1,0:T(8,128)} %copy-done.5), custom_call_target="tpu_custom_call" | custom-call | flops 1 | bytes 1 | tf_op jit(solution)/shard_map/pallas_call | solution.py:34
  48.6 2.4 %collective-permute-start.4 = (f32[2,112,256]{2,1,0:T(8,128)}, f32[2,112,256]{2,1,0:T(8,128)}, u32[]{:S(2)}, u32[]{:S(2)}) collective-permute-start(f32[2,112,256]{2,1,0:T(8,128)} %get-tuple-element.141), channel_id=1, source_target_pairs={{0,8},{1,9},{2,10},{3,11},{4,12},{5,13},{6,14},{7,15},{8,0},{9,1},... | collective-permute-start | bytes 688136 | tf_op jit(solution)/shard_map/ppermute | solution.py:153
  51.0 2.3 %add_bitcast_fusion.2 = (f32[4,112,384]{2,1,0:T(8,128)S(1)}, f32[4,112,384]{2,1,0:T(8,128)}) fusion(f32[2,4,112,384]{3,2,1,0:T(8,128)} %bitcast.7, s32[]{:T(128)S(6)} %select_n.43, f32[2,4,112,384]{3,2,1,0:T(8,128)S(1)} %bitcast.32, s32[]{:T(128)S(6)} %select_n.42), kind=kLoop, calls=%fused_computation.3 | loop fusion | flops 344064 | bytes 4128776 | tf_op jit(solution)/shard_map/add | solution.py:174
  54.1 7.0 %collective-permute-done.4 = f32[2,112,256]{2,1,0:T(8,128)} collective-permute-done((f32[2,112,256]{2,1,0:T(8,128)}, f32[2,112,256]{2,1,0:T(8,128)}, u32[]{:S(2)}, u32[]{:S(2)}) %collective-permute-start.4) | collective-permute-done | bytes 229408 | tf_op jit(solution)/shard_map/ppermute | solution.py:153
  62.1 1.7 %collective-permute-start.6 = (f32[1,112,256]{2,1,0:T(8,128)S(1)}, f32[1,112,256]{2,1,0:T(8,128)S(1)}, u32[]{:S(2)}, u32[]{:S(2)}) collective-permute-start(f32[1,112,256]{2,1,0:T(8,128)S(1)} %get-tuple-element.149.mine_ref), channel_id=1, source_target_pairs={{0,1},{1,0},{2,3},{3,2},{4,5},{5,4},{6,7},{7,6},{8,9},{9,8},{10,11... | collective-permute-start | bytes 344072 | tf_op jit(solution)/shard_map/ppermute | solution.py:153
  63.8 1.3 collective-permute-start.12
  65.8 6.9 %shard_map.97 = (f32[8,256]{1,0:T(8,128)}, f32[128,128]{1,0:T(8,128)}, f32[128,128]{1,0:T(8,128)}, f32[128,128]{1,0:T(8,128)}, f32[128,128]{1,0:T(8,128)}) custom-call(s32[1]{0:T(128)} %bitcast.me_ref, f32[1,112,256]{2,1,0:T(8,128)} %copy-done.4, f32[1,112,256]{2,1,0:T(8,128)} %copy-done.9, f32[256,8]{1,0:T(8,128)} %reshape.92.damp_ref), custom_call_target="tpu_custom_call" | custom-call | flops 1 | bytes 1 | tf_op jit(solution)/shard_map/pallas_call | solution.py:34
  73.9 3.5 %collective-permute-start.9 = (f32[2,112,256]{2,1,0:T(8,128)}, f32[2,112,256]{2,1,0:T(8,128)}, u32[]{:S(2)}, u32[]{:S(2)}) collective-permute-start(f32[2,112,256]{2,1,0:T(8,128)} %constant_dynamic-update-slice_fusion), channel_id=1, source_target_pairs={{0,4},{1,5},{2,6},{3,7},{4,0},{5,1},{6,2},{7,3},{8,12},{9,13},{10,... | collective-permute-start | bytes 688136 | tf_op jit(solution)/shard_map/ppermute | solution.py:153
  78.4 6.2 %shard_map.98 = (f32[256,256]{1,0:T(8,128)}, f32[256,256]{1,0:T(8,128)}) custom-call(f32[128,128]{1,0:T(8,128)} %get-tuple-element.161.l11_ref, f32[128,128]{1,0:T(8,128)} %get-tuple-element.162.i11_ref, f32[128,128]{1,0:T(8,128)} %get-tuple-element.163.l21_ref, f32[128,128]{1,0:T(8,128)} %get-tuple-element.164.rest_ref), custom_call_target="tpu_custom_call" | custom-call | flops 1 | bytes 1 | tf_op jit(solution)/shard_map/pallas_call | solution.py:34
  88.0 1.5 %collective-permute-start.13 = (f32[2,112,384]{2,1,0:T(8,128)S(1)}, f32[2,112,384]{2,1,0:T(8,128)S(1)}, u32[]{:S(2)}, u32[]{:S(2)}) collective-permute-start(f32[2,112,384]{2,1,0:T(8,128)S(1)} %get-tuple-element.226), channel_id=1, source_target_pairs={{0,4},{1,5},{2,6},{3,7},{4,0},{5,1},{6,2},{7,3},{8,12},{9,13},{10,... | collective-permute-start | bytes 1032200 | tf_op jit(solution)/shard_map/ppermute | solution.py:153
  89.5 5.8 %collective-permute-done.11 = f32[2,112,640]{2,1,0:T(8,128)S(1)} collective-permute-done((f32[2,112,640]{2,1,0:T(8,128)}, f32[2,112,640]{2,1,0:T(8,128)S(1)}, u32[]{:S(2)}, u32[]{:S(2)}) %collective-permute-start.11) | collective-permute-done | bytes 573472 | tf_op jit(solution)/shard_map/ppermute | solution.py:153
  96.1 1.6 %collective-permute-done.10 = f32[4,112,256]{2,1,0:T(8,128)S(1)} collective-permute-done((f32[4,112,256]{2,1,0:T(8,128)S(1)}, f32[4,112,256]{2,1,0:T(8,128)S(1)}, u32[]{:S(2)}, u32[]{:S(2)}) %collective-permute-start.10) | collective-permute-done | bytes 458784 | tf_op jit(solution)/shard_map/ppermute | solution.py:153
  98.7 3.4 %shard_map.99 = (f32[8,112,256]{2,1,0:T(8,128)}, f32[112,256]{1,0:T(8,128)}, f32[8,256]{1,0:T(8,128)}, f32[256]{0:T(256)}) custom-call(f32[256,256]{1,0:T(8,128)} %get-tuple-element.175.inverse_ref, f32[8,256]{1,0:T(8,128)} %get-tuple-element.176.g1_ref, f32[8,112,256]{2,1,0:T(8,128)} %pad_maximum_fusion.held_ref), custom_call_target="tpu_custom_call" | custom-call | flops 1 | bytes 1 | tf_op jit(solution)/shard_map/pallas_call | solution.py:34
  105.0 2.0 %collective-permute-start.16 = (f32[1,112,384]{2,1,0:T(8,128)S(1)}, f32[1,112,384]{2,1,0:T(8,128)S(1)}, u32[]{:S(2)}, u32[]{:S(2)}) collective-permute-start(f32[1,112,384]{2,1,0:T(8,128)S(1)} %get-tuple-element.229), channel_id=1, source_target_pairs={{0,8},{1,9},{2,10},{3,11},{4,12},{5,13},{6,14},{7,15},{8,0},{9,1},... | collective-permute-start | bytes 516104 | tf_op jit(solution)/shard_map/ppermute | solution.py:153
  107.0 16.8 %collective-permute-done.15.refs_1_ = f32[1,112,640]{2,1,0:T(8,128)S(1)} collective-permute-done((f32[1,112,640]{2,1,0:T(8,128)S(1)}, f32[1,112,640]{2,1,0:T(8,128)S(1)}, u32[]{:S(2)}, u32[]{:S(2)}) %collective-permute-start.15) | collective-permute-done | bytes 286752 | tf_op jit(solution)/shard_map/ppermute | solution.py:153
  124.5 1.9 %shard_map.100 = (f32[112,640]{1,0:T(8,128)}, f32[112,112]{1,0:T(8,128)}, f32[112,112]{1,0:T(8,128)}, f32[112,112]{1,0:T(8,128)}, f32[112,112]{1,0:T(8,128)}) custom-call(f32[1,112,640]{2,1,0:T(8,128)} %get-tuple-element.185.refs_0_, f32[1,112,640]{2,1,0:T(8,128)} %copy-done.6), custom_call_target="tpu_custom_call" | custom-call | flops 1 | bytes 1 | tf_op jit(solution)/shard_map/pallas_call | solution.py:34
  128.6 4.4 %shard_map.101.product_ref = f32[112,1792]{1,0:T(8,128)} custom-call(s32[1]{0:T(128)} %bitcast.me_ref, f32[8,112,256]{2,1,0:T(8,128)} %get-tuple-element.193.mine_ref, f32[8,112,256]{2,1,0:T(8,128)} %copy-done.2), custom_call_target="tpu_custom_call" | custom-call | flops 1 | bytes 1 | tf_op jit(solution)/shard_map/pallas_call | solution.py:34
  133.7 2.0 %shard_map.102 = (f32[112,384]{1,0:T(8,128)}, f32[112,112]{1,0:T(8,128)}, f32[112,112]{1,0:T(8,128)}, f32[112,112]{1,0:T(8,128)}, f32[8,112]{1,0:T(8,128)}) custom-call(f32[112,640]{1,0:T(8,128)} %get-tuple-element.208.refs_0_, f32[1,112,384]{2,1,0:T(8,128)} %get-tuple-element.195.refs_1_, f32[1,112,384]{2,1,0:T(8,128)} %copy-done.8), custom_call_target="tpu_custom_call" | custom-call | flops 1 | bytes 1 | tf_op jit(solution)/shard_map/pallas_call | solution.py:34
  135.7 5.3 %collective-permute-start.21 = (f32[112,112]{1,0:T(8,128)}, f32[112,112]{1,0:T(8,128)S(1)}, u32[]{:S(2)}, u32[]{:S(2)}) collective-permute-start(f32[112,112]{1,0:T(8,128)} %get-tuple-element.199), channel_id=1, source_target_pairs={{0,5},{1,6},{2,7},{3,8},{4,9},{5,10},{6,11},{7,12},{8,13},{9,14},{... | collective-permute-start | bytes 150536 | tf_op jit(solution)/shard_map/ppermute | solution.py:434
  142.5 5.4 %collective-permute-done.22.refs_7_ = f32[112,112]{1,0:T(8,128)S(1)} collective-permute-done((f32[112,112]{1,0:T(8,128)}, f32[112,112]{1,0:T(8,128)S(1)}, u32[]{:S(2)}, u32[]{:S(2)}) %collective-permute-start.22) | collective-permute-done | bytes 50208 | tf_op jit(solution)/shard_map/ppermute | solution.py:434
  149.6 2.8 %shard_map.103 = (f32[112,1792]{1,0:T(8,128)}, f32[112]{0:T(128)}) custom-call(s32[1]{0:T(128)} %bitcast.me_ref, f32[16,128]{1,0:T(8,128)} %bitcast.34, f32[112,1792]{1,0:T(8,128)} %shard_map.101.product_ref, f32[8,112]{1,0:T(8,128)} %get-tuple-element.205.g2_ref, f32[8,256]{1,0:T(8,128)} %get-tuple-element.206.y_ref, ...), custom_call_target="tpu_custom_call" | custom-call | flops 1 | bytes 1 | tf_op jit(solution)/shard_map/pallas_call | solution.py:34
  (78 shorter events, 22.6 us)
Async XLA Ops:
  11.6 2.8 %collective-permute-start = (f32[9,112,256]{2,1,0:T(8,128)}, f32[9,112,256]{2,1,0:T(8,128)S(1)}, u32[]{:S(2)}, u32[]{:S(2)}) collective-permute-start(f32[9,112,256]{2,1,0:T(8,128)} %get-tuple-element.113), channel_id=1, source_target_pairs={{0,1},{1,0},{2,3},{3,2},{4,5},{5,4},{6,7},{7,6},{8,9},{9,8},{10,11... | collective-permute-start | bytes 3096584 | tf_op jit(solution)/shard_map/ppermute | solution.py:153
  18.1 15.6 %collective-permute-start.1 = (f32[5,112,256]{2,1,0:T(8,128)}, f32[5,112,256]{2,1,0:T(8,128)S(1)}, u32[]{:S(2)}, u32[]{:S(2)}) collective-permute-start(f32[5,112,256]{2,1,0:T(8,128)} %get-tuple-element.120), channel_id=1, source_target_pairs={{0,2},{1,3},{2,0},{3,1},{4,6},{5,7},{6,4},{7,5},{8,10},{9,11},{10,... | collective-permute-start | bytes 1720328 | tf_op jit(solution)/shard_map/ppermute | solution.py:153
  33.8 7.1 %collective-permute-start.3 = (f32[8,112,640]{2,1,0:T(8,128)}, f32[8,112,640]{2,1,0:T(8,128)S(1)}, u32[]{:S(2)}, u32[]{:S(2)}) collective-permute-start(f32[8,112,640]{2,1,0:T(8,128)} %get-tuple-element.134), channel_id=1, source_target_pairs={{0,1},{1,0},{2,3},{3,2},{4,5},{5,4},{6,7},{7,6},{8,9},{9,8},{10,11... | collective-permute-start | bytes 6881288 | tf_op jit(solution)/shard_map/ppermute | solution.py:153
  34.6 16.3 %collective-permute-start.5 = (f32[8,112,384]{2,1,0:T(8,128)}, f32[8,112,384]{2,1,0:T(8,128)}, u32[]{:S(2)}, u32[]{:S(2)}) collective-permute-start(f32[8,112,384]{2,1,0:T(8,128)} %get-tuple-element.142), channel_id=1, source_target_pairs={{0,1},{1,0},{2,3},{3,2},{4,5},{5,4},{6,7},{7,6},{8,9},{9,8},{10,11... | collective-permute-start | bytes 4128776 | tf_op jit(solution)/shard_map/ppermute | solution.py:153
  36.8 9.1 %collective-permute-start.2 = (f32[3,112,256]{2,1,0:T(8,128)}, f32[3,112,256]{2,1,0:T(8,128)S(1)}, u32[]{:S(2)}, u32[]{:S(2)}) collective-permute-start(f32[3,112,256]{2,1,0:T(8,128)} %get-tuple-element.133), channel_id=1, source_target_pairs={{0,4},{1,5},{2,6},{3,7},{4,0},{5,1},{6,2},{7,3},{8,12},{9,13},{10,... | collective-permute-start | bytes 1032200 | tf_op jit(solution)/shard_map/ppermute | solution.py:153
  40.9 10.1 %copy-start = (f32[8,112,384]{2,1,0:T(8,128)S(1)}, f32[8,112,384]{2,1,0:T(8,128)}, u32[]{:S(2)}) copy-start(f32[8,112,384]{2,1,0:T(8,128)} %get-tuple-element.143) | copy-start | bytes 4128772
  43.9 33.6 %collective-permute-start.7 = (f32[4,112,640]{2,1,0:T(8,128)}, f32[4,112,640]{2,1,0:T(8,128)S(1)}, u32[]{:S(2)}, u32[]{:S(2)}) collective-permute-start(f32[4,112,640]{2,1,0:T(8,128)} %get-tuple-element.220), channel_id=1, source_target_pairs={{0,2},{1,3},{2,0},{3,1},{4,6},{5,7},{6,4},{7,5},{8,10},{9,11},{10,... | collective-permute-start | bytes 3440648 | tf_op jit(solution)/shard_map/ppermute | solution.py:153
  48.6 12.6 %collective-permute-start.4 = (f32[2,112,256]{2,1,0:T(8,128)}, f32[2,112,256]{2,1,0:T(8,128)}, u32[]{:S(2)}, u32[]{:S(2)}) collective-permute-start(f32[2,112,256]{2,1,0:T(8,128)} %get-tuple-element.141), channel_id=1, source_target_pairs={{0,8},{1,9},{2,10},{3,11},{4,12},{5,13},{6,14},{7,15},{8,0},{9,1},... | collective-permute-start | bytes 688136 | tf_op jit(solution)/shard_map/ppermute | solution.py:153
  51.0 10.1 %copy-start.7 = (f32[2,112,256]{2,1,0:T(8,128)S(1)}, f32[2,112,256]{2,1,0:T(8,128)}, u32[]{:S(2)}) copy-start(f32[2,112,256]{2,1,0:T(8,128)} %get-tuple-element.146) | copy-start | bytes 688132
  62.1 3.0 %copy-start.4 = (f32[1,112,256]{2,1,0:T(8,128)}, f32[1,112,256]{2,1,0:T(8,128)S(1)}, u32[]{:S(2)}) copy-start(f32[1,112,256]{2,1,0:T(8,128)S(1)} %get-tuple-element.149.mine_ref) | copy-start | bytes 344068
  62.1 3.0 %collective-permute-start.6 = (f32[1,112,256]{2,1,0:T(8,128)S(1)}, f32[1,112,256]{2,1,0:T(8,128)S(1)}, u32[]{:S(2)}, u32[]{:S(2)}) collective-permute-start(f32[1,112,256]{2,1,0:T(8,128)S(1)} %get-tuple-element.149.mine_ref), channel_id=1, source_target_pairs={{0,1},{1,0},{2,3},{3,2},{4,5},{5,4},{6,7},{7,6},{8,9},{9,8},{10,11... | collective-permute-start | bytes 344072 | tf_op jit(solution)/shard_map/ppermute | solution.py:153
  63.8 8.8 %collective-permute-start.8 = (f32[1,112,256]{2,1,0:T(8,128)S(1)}, f32[1,112,256]{2,1,0:T(8,128)S(1)}, u32[]{:S(2)}, u32[]{:S(2)}) collective-permute-start(f32[1,112,256]{2,1,0:T(8,128)S(1)} %get-tuple-element.157), channel_id=1, source_target_pairs={{0,8},{1,9},{2,10},{3,11},{4,12},{5,13},{6,14},{7,15},{8,0},{9,1},... | collective-permute-start | bytes 344072 | tf_op jit(solution)/shard_map/ppermute | solution.py:153
  63.8 23.0 %collective-permute-start.12 = (f32[4,112,384]{2,1,0:T(8,128)}, f32[4,112,384]{2,1,0:T(8,128)}, u32[]{:S(2)}, u32[]{:S(2)}) collective-permute-start(f32[4,112,384]{2,1,0:T(8,128)} %get-tuple-element.222), channel_id=1, source_target_pairs={{0,2},{1,3},{2,0},{3,1},{4,6},{5,7},{6,4},{7,5},{8,10},{9,11},{10,... | collective-permute-start | bytes 2064392 | tf_op jit(solution)/shard_map/ppermute | solution.py:153
  73.9 10.7 %collective-permute-start.9 = (f32[2,112,256]{2,1,0:T(8,128)}, f32[2,112,256]{2,1,0:T(8,128)}, u32[]{:S(2)}, u32[]{:S(2)}) collective-permute-start(f32[2,112,256]{2,1,0:T(8,128)} %constant_dynamic-update-slice_fusion), channel_id=1, source_target_pairs={{0,4},{1,5},{2,6},{3,7},{4,0},{5,1},{6,2},{7,3},{8,12},{9,13},{10,... | collective-permute-start | bytes 688136 | tf_op jit(solution)/shard_map/ppermute | solution.py:153
  78.4 17.0 %collective-permute-start.11 = (f32[2,112,640]{2,1,0:T(8,128)}, f32[2,112,640]{2,1,0:T(8,128)S(1)}, u32[]{:S(2)}, u32[]{:S(2)}) collective-permute-start(f32[2,112,640]{2,1,0:T(8,128)} %get-tuple-element.224), channel_id=1, source_target_pairs={{0,4},{1,5},{2,6},{3,7},{4,0},{5,1},{6,2},{7,3},{8,12},{9,13},{10,... | collective-permute-start | bytes 1720328 | tf_op jit(solution)/shard_map/ppermute | solution.py:153
  86.5 11.2 %collective-permute-start.10 = (f32[4,112,256]{2,1,0:T(8,128)S(1)}, f32[4,112,256]{2,1,0:T(8,128)S(1)}, u32[]{:S(2)}, u32[]{:S(2)}) collective-permute-start(f32[4,112,256]{2,1,0:T(8,128)S(1)} %constant_dynamic-update-slice_fusion.2), channel_id=1, source_target_pairs={{0,2},{1,3},{2,0},{3,1},{4,6},{5,7},{6,4},{7,5},{8,10},{9,11},{10,... | collective-permute-start | bytes 1376264 | tf_op jit(solution)/shard_map/ppermute | solution.py:153
  88.0 14.7 %collective-permute-start.13 = (f32[2,112,384]{2,1,0:T(8,128)S(1)}, f32[2,112,384]{2,1,0:T(8,128)S(1)}, u32[]{:S(2)}, u32[]{:S(2)}) collective-permute-start(f32[2,112,384]{2,1,0:T(8,128)S(1)} %get-tuple-element.226), channel_id=1, source_target_pairs={{0,4},{1,5},{2,6},{3,7},{4,0},{5,1},{6,2},{7,3},{8,12},{9,13},{10,... | collective-permute-start | bytes 1032200 | tf_op jit(solution)/shard_map/ppermute | solution.py:153
  103.4 24.3 %collective-permute-start.14 = (f32[8,112,256]{2,1,0:T(8,128)}, f32[8,112,256]{2,1,0:T(8,128)S(1)}, u32[]{:S(2)}, u32[]{:S(2)}) collective-permute-start(f32[8,112,256]{2,1,0:T(8,128)} %get-tuple-element.193.mine_ref), channel_id=1, source_target_pairs={{0,1},{1,0},{2,3},{3,2},{4,5},{5,4},{6,7},{7,6},{8,9},{9,8},{10,11... | collective-permute-start | bytes 2752520 | tf_op jit(solution)/shard_map/ppermute | solution.py:153
  104.6 19.2 %collective-permute-start.15 = (f32[1,112,640]{2,1,0:T(8,128)S(1)}, f32[1,112,640]{2,1,0:T(8,128)S(1)}, u32[]{:S(2)}, u32[]{:S(2)}) collective-permute-start(f32[1,112,640]{2,1,0:T(8,128)S(1)} %get-tuple-element.228), channel_id=1, source_target_pairs={{0,8},{1,9},{2,10},{3,11},{4,12},{5,13},{6,14},{7,15},{8,0},{9,1},... | collective-permute-start | bytes 860168 | tf_op jit(solution)/shard_map/ppermute | solution.py:153
  105.0 28.0 %collective-permute-start.16 = (f32[1,112,384]{2,1,0:T(8,128)S(1)}, f32[1,112,384]{2,1,0:T(8,128)S(1)}, u32[]{:S(2)}, u32[]{:S(2)}) collective-permute-start(f32[1,112,384]{2,1,0:T(8,128)S(1)} %get-tuple-element.229), channel_id=1, source_target_pairs={{0,8},{1,9},{2,10},{3,11},{4,12},{5,13},{6,14},{7,15},{8,0},{9,1},... | collective-permute-start | bytes 516104 | tf_op jit(solution)/shard_map/ppermute | solution.py:153
  126.4 14.6 %collective-permute-start.17 = (f32[112,112]{1,0:T(8,128)}, f32[112,112]{1,0:T(8,128)S(1)}, u32[]{:S(2)}, u32[]{:S(2)}) collective-permute-start(f32[112,112]{1,0:T(8,128)} %get-tuple-element.188), channel_id=1, source_target_pairs={{0,1},{1,2},{2,3},{3,4},{4,5},{5,6},{6,7},{7,8},{8,9},{9,10},{10,1... | collective-permute-start | bytes 150536 | tf_op jit(solution)/shard_map/ppermute | solution.py:434
  127.7 13.9 %collective-permute-start.18 = (f32[112,112]{1,0:T(8,128)}, f32[112,112]{1,0:T(8,128)S(1)}, u32[]{:S(2)}, u32[]{:S(2)}) collective-permute-start(f32[112,112]{1,0:T(8,128)} %get-tuple-element.189), channel_id=1, source_target_pairs={{0,2},{1,3},{2,4},{3,5},{4,6},{5,7},{6,8},{7,9},{8,10},{9,11},{10,... | collective-permute-start | bytes 150536 | tf_op jit(solution)/shard_map/ppermute | solution.py:434
  127.7 13.9 %collective-permute-start.19 = (f32[112,112]{1,0:T(8,128)}, f32[112,112]{1,0:T(8,128)S(1)}, u32[]{:S(2)}, u32[]{:S(2)}) collective-permute-start(f32[112,112]{1,0:T(8,128)} %get-tuple-element.190), channel_id=1, source_target_pairs={{0,3},{1,4},{2,5},{3,6},{4,7},{5,8},{6,9},{7,10},{8,11},{9,12},{10... | collective-permute-start | bytes 150536 | tf_op jit(solution)/shard_map/ppermute | solution.py:434
  127.7 13.9 %collective-permute-start.20 = (f32[112,112]{1,0:T(8,128)}, f32[112,112]{1,0:T(8,128)S(1)}, u32[]{:S(2)}, u32[]{:S(2)}) collective-permute-start(f32[112,112]{1,0:T(8,128)} %get-tuple-element.191), channel_id=1, source_target_pairs={{0,4},{1,5},{2,6},{3,7},{4,8},{5,9},{6,10},{7,11},{8,12},{9,13},{1... | collective-permute-start | bytes 150536 | tf_op jit(solution)/shard_map/ppermute | solution.py:434
  135.7 6.9 %collective-permute-start.21 = (f32[112,112]{1,0:T(8,128)}, f32[112,112]{1,0:T(8,128)S(1)}, u32[]{:S(2)}, u32[]{:S(2)}) collective-permute-start(f32[112,112]{1,0:T(8,128)} %get-tuple-element.199), channel_id=1, source_target_pairs={{0,5},{1,6},{2,7},{3,8},{4,9},{5,10},{6,11},{7,12},{8,13},{9,14},{... | collective-permute-start | bytes 150536 | tf_op jit(solution)/shard_map/ppermute | solution.py:434
  141.0 8.0 %copy-start.10 = (f32[112,112]{1,0:T(8,128)}, f32[112,112]{1,0:T(8,128)S(1)}, u32[]{:S(2)}) copy-start(f32[112,112]{1,0:T(8,128)S(1)} %collective-permute-done.17.refs_2_) | copy-start | bytes 150532
  141.0 7.0 %collective-permute-start.22 = (f32[112,112]{1,0:T(8,128)}, f32[112,112]{1,0:T(8,128)S(1)}, u32[]{:S(2)}, u32[]{:S(2)}) collective-permute-start(f32[112,112]{1,0:T(8,128)} %get-tuple-element.200), channel_id=1, source_target_pairs={{0,6},{1,7},{2,8},{3,9},{4,10},{5,11},{6,12},{7,13},{8,14},{9,15},... | collective-permute-start | bytes 150536 | tf_op jit(solution)/shard_map/ppermute | solution.py:434
  141.6 7.4 %copy-start.11 = (f32[112,112]{1,0:T(8,128)}, f32[112,112]{1,0:T(8,128)S(1)}, u32[]{:S(2)}) copy-start(f32[112,112]{1,0:T(8,128)S(1)} %collective-permute-done.18.refs_3_) | copy-start | bytes 150532
  141.6 7.4 %collective-permute-start.23 = (f32[112,112]{1,0:T(8,128)}, f32[112,112]{1,0:T(8,128)S(1)}, u32[]{:S(2)}, u32[]{:S(2)}) collective-permute-start(f32[112,112]{1,0:T(8,128)} %get-tuple-element.201), channel_id=1, source_target_pairs={{0,7},{1,8},{2,9},{3,10},{4,11},{5,12},{6,13},{7,14},{8,15},{9,0},... | collective-permute-start | bytes 150536 | tf_op jit(solution)/shard_map/ppermute | solution.py:434
  141.6 7.4 %copy-start.12 = (f32[112,112]{1,0:T(8,128)}, f32[112,112]{1,0:T(8,128)S(1)}, u32[]{:S(2)}) copy-start(f32[112,112]{1,0:T(8,128)S(1)} %collective-permute-done.19.refs_4_) | copy-start | bytes 150532
  141.6 7.4 %copy-start.13 = (f32[112,112]{1,0:T(8,128)}, f32[112,112]{1,0:T(8,128)S(1)}, u32[]{:S(2)}) copy-start(f32[112,112]{1,0:T(8,128)S(1)} %collective-permute-done.20.refs_5_) | copy-start | bytes 150532
  142.5 6.4 %copy-start.14 = (f32[112,112]{1,0:T(8,128)}, f32[112,112]{1,0:T(8,128)S(1)}, u32[]{:S(2)}) copy-start(f32[112,112]{1,0:T(8,128)S(1)} %collective-permute-done.21.refs_6_) | copy-start | bytes 150532
  (10 other events, 9.6 us)

commit v3 on v2

--- a/solution.py
+++ b/solution.py
@@ -47,14 +47,64 @@
     return sum(((m >> (last - k)) & 1) << bit for k, bit in enumerate(order))
 
 
-def front_kernel(order, me_ref, count_ref, offset_ref, resid_ref, feat_ref, sent_ref, kept_ref, jt_ref, r_ref, jp_ref, n21_ref):
+def front_kernel(
+    order, me_ref, count_ref, offset_ref, resid_ref, feat_hbm, sent_hbm, kept_hbm, jt_hbm, r_ref,
+    feat_ref, jp_ref, jt_ref, n21_ref, n11_ref, pack_ref, feat_sems, jt_sems, out_sems,
+):
+    depth, params = feat_ref.shape
+    blocks = params // BLK
+    core = me_ref[0] & 1
+    pan_b = BLK // STRIDE
+    trail_b = BLK - pan_b
+    feat_copies = [
+        pltpu.make_async_copy(feat_hbm.at[:, b * BLK : (b + 1) * BLK], feat_ref.at[:, b * BLK : (b + 1) * BLK], feat_sems.at[b])
+        for b in range(blocks)
+    ]
+    for copy in feat_copies:
+        copy.start()
+    window, pick = window_part(count_ref, offset_ref, resid_ref, depth, jp_ref.shape[1], r_ref)
+    copies = []
+    for b in range(blocks):
+        feat_copies[b].wait()
+        turned = dot_nt(pick, feat_ref[:, b * BLK : (b + 1) * BLK]).astype(jnp.bfloat16)
+        jac = jnp.dot(turned, window, preferred_element_type=jnp.float32).astype(jnp.bfloat16)
+        jp_ref[b * pan_b : (b + 1) * pan_b, :] = jac[:pan_b]
+        rows = slice(b * trail_b, (b + 1) * trail_b)
+        jt_ref[rows, :] = jac[pan_b:]
+        copies.append(pltpu.make_async_copy(jt_ref.at[rows], jt_hbm.at[rows], jt_sems.at[b]))
+        copies[-1].start()
+    jp = jp_ref[...]
+    own, count = sent_hbm.shape[1], sent_hbm.shape[0] - 1
+    ways = ((sent_hbm, 1 - core), (kept_hbm, core))
+    panel = jp.shape[0]
+    half, part = panel // 2, panel // 4
+    n11_ref[...] = dot_nt(jp, jp)
+    grad = dot_nt(r_ref[...], jp)
+    for k, (out, which) in enumerate(ways):
+        for side in range(2):
+            lanes = slice(side * half, (side + 1) * half)
+            at = pl.multiple_of(which * half + side * part, 16)
+            first = n11_ref[pl.ds(at, part), :]
+            pack_ref[k, :part, lanes] = jnp.where(which == 1, first[:, half:], first[:, :half])
+            at = pl.multiple_of(half + which * part + side * (part // 2), 16)
+            pack_ref[k, part : part + part // 2, lanes] = n11_ref[pl.ds(at, part // 2), :half]
+        pack_ref[k, part + part // 2 :, :] = grad[: own - part - part // 2]
+        copies.append(pltpu.make_async_copy(pack_ref.at[k], out.at[count], out_sems.at[k, count]))
+        copies[-1].start()
+    for m in range(count):
+        rows = slice(m * 2 * own, (m + 1) * 2 * own)
+        n21_ref[rows, :] = dot_nt(jt_ref[rows, :], jp)
+        for k, (out, which) in enumerate(ways):
+            source = n21_ref.at[pl.ds(pl.multiple_of(m * 2 * own + which * own, 16), own), :]
+            copies.append(pltpu.make_async_copy(source, out.at[place_of(m, order)], out_sems.at[k, m]))
+            copies[-1].start()
+    for copy in copies:
+        copy.wait()
+
+
+def window_part(count_ref, offset_ref, resid_ref, depth, cap, r_ref):
     tiles, slots = offset_ref.shape
-    depth, params = feat_ref.shape
     samples = depth // tiles
-    cap = jp_ref.shape[1]
-    panel = jp_ref.shape[0]
-    trail = params - panel
-    core = me_ref[0] & 1
     lane = lax.broadcasted_iota(jnp.int32, (8, cap), 1)
     start = jnp.full((8, cap), -depth, jnp.int32)
     resid = jnp.zeros((8, cap), jnp.float32)
@@ -79,42 +129,32 @@
     col = lax.broadcasted_iota(jnp.int32, (BLK, BLK), 1)
     rest = row - pan_b
     source = jnp.where(row < pan_b, row * STRIDE, rest + 1 + ((rest * 9363) >> 16))
-    pick = jnp.where(source == col, 1.0, 0.0).astype(jnp.bfloat16)
-    trail_b = BLK - pan_b
-    for b in range(params // BLK):
-        turned = dot_nt(pick, feat_ref[:, b * BLK : (b + 1) * BLK]).astype(jnp.bfloat16)
-        jac = jnp.dot(turned, window, preferred_element_type=jnp.float32).astype(jnp.bfloat16)
-        jp_ref[b * pan_b : (b + 1) * pan_b, :] = jac[:pan_b]
-        jt_ref[b * trail_b : (b + 1) * trail_b, :] = jac[pan_b:]
-        if trail + (b + 1) * trail_b <= jt_ref.shape[0]:
-            jt_ref[trail + b * trail_b : trail + (b + 1) * trail_b, :] = jac[pan_b:]
-    jp = jp_ref[...]
-    n21_ref[...] = dot_nt(jt_ref[:trail, :], jp)
-    own, count = sent_ref.shape[1], sent_ref.shape[0] - 1
-    for m in range(count):
-        base = owner_of(m, order) * own
-        sent_ref[m] = n21_ref[pl.ds(pl.multiple_of(base + (1 - core) * own, 16), own), :]
-        kept_ref[m] = n21_ref[pl.ds(pl.multiple_of(base + core * own, 16), own), :]
-    half, rows = panel // 2, panel // 4
-    n21_ref[:panel, :] = dot_nt(jp, jp)
-    grad = dot_nt(r_ref[...], jp)
-    for ref, which in ((sent_ref, 1 - core), (kept_ref, core)):
-        for side in range(2):
-            lanes = slice(side * half, (side + 1) * half)
-            at = pl.multiple_of(which * half + side * rows, 16)
-            first = n21_ref[pl.ds(at, rows), :]
-            ref[count, :rows, lanes] = jnp.where(which == 1, first[:, half:], first[:, :half])
-            at = pl.multiple_of(half + which * rows + side * (rows // 2), 16)
-            ref[count, rows : rows + rows // 2, lanes] = n21_ref[pl.ds(at, rows // 2), :half]
-        ref[count, rows + rows // 2 :, :] = grad[: own - rows - rows // 2]
-
-
-def trail_kernel(me_ref, jt_ref, r_ref, sent1_ref, sent2_ref, kept1_ref, kept2_ref, pair_ref):
-    base = pl.program_id(0) * 2 * sent1_ref.shape[1]
+    return window, jnp.where(source == col, 1.0, 0.0).astype(jnp.bfloat16)
+
+
+def trail_kernel(me_ref, jt_hbm, r_ref, *refs):
+    outs, (pair_ref, jt_ref, sems) = refs[:-3], refs[-3:]
+    sent, kept = outs[: len(outs) // 2], outs[len(outs) // 2 :]
+    m = pl.program_id(0)
     core = me_ref[0] & 1
-    own, wide = sent1_ref.shape[1:]
-    end = wide + sent2_ref.shape[2]
-    real = end - r_ref.shape[0]
+    own = sent[0].shape[1]
+    base = m * 2 * own
+    pairs = jt_hbm.shape[0] // (2 * own)
+    ahead = jt_ref.shape[0] // (2 * own) - pairs
+
+    def brought(k):
+        source = jt_hbm.at[pl.ds(pl.multiple_of(lax.rem(k, pairs) * 2 * own, 16), 2 * own), :]
+        return pltpu.make_async_copy(source, jt_ref.at[pl.ds(pl.multiple_of(k * 2 * own, 16), 2 * own), :], sems.at[k])
+
+    @pl.when(m == 0)
+    def _():
+        for k in range(pairs + ahead):
+            brought(jnp.int32(k)).start()
+        for k in range(ahead):
+            brought(jnp.int32(k)).wait()
+
+    brought(m + ahead).wait()
+    real = pair_ref.shape[2] - r_ref.shape[0]
     rows = jt_ref[pl.ds(pl.multiple_of(base, 16), 2 * own), :]
     others = jt_ref[pl.ds(pl.multiple_of(base, 16), real + own), :]
     both = dot_nt(rows, others)
@@ -123,9 +163,11 @@
     pair_ref[0, :, real:] = last[:own]
     pair_ref[1, :, :real] = both[own:, own:]
     pair_ref[1, :, real:] = last[own:]
-    for first, second, which in ((sent1_ref, sent2_ref, 1 - core), (kept1_ref, kept2_ref, core)):
-        first[0] = pair_ref[which, :, :wide]
-        second[0] = pair_ref[which, :, wide:]
+    for group, which in ((sent, 1 - core), (kept, core)):
+        at = 0
+        for ref in group:
+            ref[0] = pair_ref[which, :, at : at + ref.shape[2]]
+            at += ref.shape[2]
 
 
 def place_of(m, order):
@@ -136,16 +178,48 @@
     def spec(order, wide):
         return pl.BlockSpec((1, own, wide), lambda m: (place_of(m, order), 0, 0))
 
+    pairs = half + half // 2
     return pl.pallas_call(
         trail_kernel,
         grid=(half,),
         out_shape=[f32(half, own, wide) for wide in widths] * 2,
-        in_specs=[SMEM_SPEC, pl.BlockSpec(jt.shape, lambda m: (0, 0)), pl.BlockSpec(r.shape, lambda m: (0, 0))],
+        in_specs=[SMEM_SPEC, pl.BlockSpec(memory_space=pl.ANY), pl.BlockSpec(r.shape, lambda m: (0, 0))],
         out_specs=[spec(order, wide) for order, wide in zip(orders, widths)] * 2,
-        scratch_shapes=[pltpu.VMEM((2, own, sum(widths)), jnp.float32)],
+        scratch_shapes=[
+            pltpu.VMEM((2, own, sum(widths)), jnp.float32),
+            pltpu.VMEM((2 * own * pairs, jt.shape[1]), jnp.bfloat16),
+            pltpu.SemaphoreType.DMA((pairs,)),
+        ],
         compiler_params=pltpu.CompilerParams(vmem_limit_bytes=VMEM_LIMIT),
         cost_estimate=pl.CostEstimate(flops=1, bytes_accessed=1, transcendentals=0),
     )(me1, jt, r)
+
+
+def front(order, me1, gauge_count, gauge_offset, gauge_resid, feats, half, own):
+    depth, params = feats.shape
+    cap = gauge_offset.size // 2
+    panel = params // STRIDE
+    trail = params - panel
+    hbm = pl.BlockSpec(memory_space=pl.ANY)
+    return pl.pallas_call(
+        functools.partial(front_kernel, order),
+        out_shape=[f32(half + 1, own, panel)] * 2 + [bf16(trail, cap), bf16(16, cap)],
+        in_specs=[SMEM_SPEC, SMEM_SPEC, VMEM_SPEC, VMEM_SPEC, hbm],
+        out_specs=[hbm, hbm, hbm, VMEM_SPEC],
+        scratch_shapes=[
+            pltpu.VMEM((depth, params), jnp.bfloat16),
+            pltpu.VMEM((panel, cap), jnp.bfloat16),
+            pltpu.VMEM((trail, cap), jnp.bfloat16),
+            pltpu.VMEM((trail, panel), jnp.float32),
+            pltpu.VMEM((panel, panel), jnp.float32),
+            pltpu.VMEM((2, own, panel), jnp.float32),
+            pltpu.SemaphoreType.DMA((params // BLK,)),
+            pltpu.SemaphoreType.DMA((params // BLK,)),
+            pltpu.SemaphoreType.DMA((2, half + 1)),
+        ],
+        compiler_params=pltpu.CompilerParams(vmem_limit_bytes=VMEM_LIMIT),
+        cost_estimate=pl.CostEstimate(flops=1, bytes_accessed=1, transcendentals=0),
+    )(me1, gauge_count, gauge_offset, gauge_resid, feats)
 
 
 def swap(x, axis, bit):
@@ -176,14 +250,14 @@
     return part(1 - mine), part(mine)
 
 
-def mirror(sums, own, ks, row):
+def mirror(sums, own, ks, row, others):
     flat = [x for pair in sums for x in pair]
     widths = [pair[0].shape[-1] for pair in sums]
     new = [len(pair) == 2 for pair in sums]
     total = sum(widths)
 
     def kernel(*refs):
-        ins, outs = list(refs[: len(flat)]), list(refs[len(flat) :])
+        ins, outs = list(refs[: len(flat)]), list(refs[len(flat) + len(others) :])
         turned_ref = outs.pop()
         at = 0
         for wide, pair in zip(widths, new):
@@ -193,14 +267,18 @@
                 outs.pop(0)[...] = x
             turned_ref[at : at + wide, :] = x.T
             at += wide
+        if others:
+            outs.pop(0)[...] = jnp.concatenate([x[...] for x in reversed(refs[len(flat) : len(flat) + len(others)])], axis=1)
         for k in ks:
             outs.pop(0)[...] = turned_ref[k * own : (k + 1) * own, :]
         if row:
             outs.pop(0)[...] = turned_ref[row : row + 8, :]
 
-    shapes = [f32(own, w) for w, pair in zip(widths, new) if pair] + [f32(own, own)] * len(ks) + [f32(8, own)] * bool(row)
-    out = list(call(kernel, flat, shapes, [pltpu.VMEM((total, own), jnp.float32)]))
-    return out[: sum(new)], out[sum(new) : sum(new) + len(ks)], out[-1]
+    shapes = [f32(own, w) for w, pair in zip(widths, new) if pair] + [f32(own, own * len(others))] * bool(others)
+    first = len(shapes)
+    shapes += [f32(own, own)] * len(ks) + [f32(8, own)] * bool(row)
+    out = list(call(kernel, flat + others, shapes, [pltpu.VMEM((total, own), jnp.float32)]))
+    return out[:first], out[first : first + len(ks)], out[-1]
 
 
 def factor_block(a):
@@ -321,7 +399,9 @@
     rhs_ref[...] = (g2_ref[...] - dot_nt(y_ref[...], lower_ref[...], EXACT))[0]
     me = me_ref[0]
     own = schur_ref.shape[0]
-    whole = jnp.concatenate([c[...] for c in chunks], axis=1)[:, : own * (len(mirrors) + 2)]
+    turned = [m[...] for m in reversed(mirrors)]
+    width = schur_ref.shape[1] - sum(x.shape[1] for x in turned)
+    whole = jnp.concatenate([c[...] for c in chunks], axis=1)[:, :width]
     row = lax.broadcasted_iota(jnp.int32, (own, own), 0)
     col = lax.broadcasted_iota(jnp.int32, (own, own), 1)
     nat = own * STRIDE // (STRIDE - 1)
@@ -330,7 +410,7 @@
     pick = target == lax.broadcasted_iota(jnp.int32, (own, nat), 1)
     damp = jnp.sum(jnp.where(pick, damp_ref[pl.ds(me, 1), :], 0.0), axis=1, keepdims=True)
     first = whole[:, :own] + jnp.where(row == col, damp, 0.0)
-    whole = jnp.concatenate([first, whole[:, own:]] + [m[...] for m in reversed(mirrors)], axis=1)
+    whole = jnp.concatenate([first, whole[:, own:]] + turned, axis=1)
     schur_ref[...] = pltpu.roll(whole, me * own, 1) - product_ref[...]
 
 
@@ -344,15 +424,13 @@
     own = trail // n
     if n != 16 or own != 112 or params % BLK:
         return per_device_plain(features, gauge_offset, gauge_count, gauge_resid, damping)
-    cap = tiles_here * slots // 2
     count = n // 2 - 1
     half = n // 2
-    widths = (640, 384)
+    widths = (384, 384, 256)
     me = lax.axis_index(axis)
     me1 = me.astype(jnp.int32).reshape(1)
     order = [1, 2, 3]
-    orders = [order, order]
-    ext = trail + own * half
+    orders = [order] * len(widths)
     last = [()]
 
     def then(*xs):
@@ -363,16 +441,9 @@
         last[0] = x
         return x
 
-    sent, p, jt, r = did(
-        call(
-            functools.partial(front_kernel, order),
-            (me1, gauge_count, gauge_offset, gauge_resid, features.reshape(tiles_here * samples, params)),
-            [f32(half + 1, own, panel)] * 2 + [bf16(ext, cap), bf16(16, cap)],
-            [pltpu.VMEM((panel, cap), jnp.bfloat16), pltpu.VMEM((trail, panel), jnp.float32)],
-        )
-    )
+    feats = features.reshape(tiles_here * samples, params)
+    sent, p, jt, r = did(front(order, me1, gauge_count, gauge_offset, gauge_resid, feats, half, own))
     p_got = swap(sent, axis, 0)
-    t, t_got = [None, None], [None, None]
 
     def panel_fold(p, got, bit):
         shape = f32(p.shape[0] // 2 + 1, *p.shape[1:])
@@ -391,18 +462,26 @@
         trail_fold(q, step)
         trail_send(q, step)
 
+    def trail_sum(q):
+        kept, got = then(t[q], t_got[q])
+        return did(kept[0] + got[0])
+
     def joined(held, got):
         return did(jnp.concatenate(then(held, got), axis=0))
 
-    t_sent = [None, None]
     p, p_got = panel_fold(p, p_got, order[0])
-    *t_sent, t[0], t[1] = did(trailing(*then(me1, jt, r), orders, half, own, widths))
+    out = did(trailing(*then(me1, jt, r), orders, half, own, widths))
+    t_sent, t = out[: len(widths)], list(out[len(widths) :])
     t_sent, p_got = lax.optimization_barrier((t_sent, p_got))
+    t_sent = list(t_sent)
     t_got = [swap(x, axis, 0) for x in t_sent]
     p, p_got = panel_fold(p, p_got, order[1])
-    trail_step(0, 0)
+    trail_fold(0, 0)
     p, p_got = panel_fold(p, p_got, order[2])
+    t_sent[0] = lax.optimization_barrier((t_sent[0], p))[0]
+    trail_send(0, 0)
     trail_step(1, 0)
+    trail_step(2, 0)
     damp_panel, damp_trail = then(damping)[0].reshape(panel, STRIDE), damping.reshape(n, params // n)
     damp_panel = did(damp_panel)
     p, p_got = then(p, p_got)
@@ -413,27 +492,27 @@
     g1, *state = did(
         call(factor_first_kernel, then(me1, n11, n11_got, damp_panel), [f32(8, panel)] + [f32(panel // 2, panel // 2)] * 4)
     )
+    trail_step(0, 1)
     held = joined(held, got)
     got = swap(held, axis, order[1])
-    trail_step(0, 1)
+    trail_step(1, 1)
     factor, inverse = did(call(factor_second_kernel, then(*state), [f32(panel, panel)] * 2))
+    trail_step(0, 2)
     held = joined(held, got)
     got = swap(held, axis, order[0])
-    trail_step(1, 1)
-    trail_step(0, 2)
+    trail_step(2, 1)
+    trail_step(1, 2)
+    first = trail_sum(0)
+    trail_step(2, 2)
     held = joined(held, got)
     mine, lower, y, y0 = did(
         call(lower_kernel, then(inverse, g1, held), [f32(half, own, panel), f32(own, panel), f32(8, panel), f32(panel)])
     )
-    trail_step(1, 2)
-    other = swap(lax.optimization_barrier((mine, t[1]))[0], axis, 0)
-    ks = [range(1, widths[0] // own), range(widths[0] // own, count + 1)]
-    (c0,), blocks, _ = did(mirror([then(t[0], t_got[0])], own, ks[0], 0))
-
-    def mirrored(blocks, ks):
-        return [lax.ppermute(b, axis, [(i, (i + k) % n) for i in range(n)]) for k, b in zip(ks, blocks)]
-
-    mirrors = mirrored(blocks, ks[0])
+    second = trail_sum(1)
+    (third,), blocks, g2 = did(mirror([(first,), (second,), then(t[2], t_got[2])], own, range(1, count + 1), (count + 2) * own, []))
+    chunks = [first, second, third]
+    mirrors = [lax.ppermute(b, axis, [(i, (i + k) % n) for i in range(n)]) for k, b in enumerate(blocks, 1)]
+    other = swap(lax.optimization_barrier((mine, chunks))[0], axis, 0)
     product = did(
         call(
             functools.partial(product_kernel, list(reversed(order))),
@@ -442,11 +521,8 @@
             [pltpu.VMEM((trail, panel), jnp.float32)],
         )
     )
-    (c1,), blocks, g2 = did(mirror([(c0,), then(t[1], t_got[1])], own, ks[1], (count + 2) * own))
-    mirrors += mirrored(blocks, ks[1])
-    chunks = [c0, c1]
     schur, rhs0 = call(
-        functools.partial(last_kernel, 2),
+        functools.partial(last_kernel, len(widths)),
         then(me1, damp_trail, product, g2, y, lower, *chunks, *mirrors),
         [f32(own, trail), f32(own)],
     )

time: 153 us -> 142 us (0.928)
  waiting for transfers between devices: 47.5 us -> 41.1 us
  local copies, waits for them, and re-layouts: 8.48 us -> 6.29 us
    pallas_call x11 -> x9, Pallas kernels: 45.2 us -> 32.3 us  [call(): pl.pallas_call(kernel, out_shape=out_shape, in_specs=[SMEM_SPEC if x.dtyp...]
    pallas_call x0 -> x1, Pallas kernels: none -> 11.6 us  [front(): pl.pallas_call(functools.partial(front_kernel, order), out_shape=[f32(hal...]
    ppermute x17 -> x21, waiting for transfers between devices: 40.1 us -> 36.7 us  [swap(): return lax.ppermute(x, axis, [(i, i ^ 1 << bit) for i in range(n)])]
    ppermute x7, waiting for transfers between devices: 7.35 us -> 4.37 us  [per_device(): lax.ppermute(b, axis, [(i, (i + k) % n) for i in range(n)])]
    add x6 -> x9, other arithmetic: 8.93 us -> 7.22 us  [part(): lax.dynamic_index_in_dim(kept, which, 0, False)]
    concatenate x2, local copies, waits for them, and re-layouts: 1.6 us -> 0.03 us  [joined(): return did(jnp.concatenate(then(held, got), axis=0))]
    unnamed x38 -> x40, local copies, waits for them, and re-layouts: 6.12 us -> 5.49 us
    ppermute x17 -> x21, starting transfers between devices: 20.6 us -> 21.1 us  [swap(): return lax.ppermute(x, axis, [(i, i ^ 1 << bit) for i in range(n)])]
  transfers between devices with their start and end apart: 24 -> 28, of which waited for: 12 -> 12; matrix products, arithmetic and copies ran while one was open for 9% -> 7% of each run, Pallas kernels for 26% -> 26%
where the time goes in v3:
time: 142 us; the launch traced here: 141 us
  Pallas kernels  55.2 us (39%)
  waiting for transfers between devices  41.1 us (29%)
  starting transfers between devices  28.2 us (20%)
  other arithmetic  9.66 us (7%)
  local copies, waits for them, and re-layouts  6.29 us (4%)
    ppermute x21, waiting for transfers between devices, swap(): return lax.ppermute(x, axis, [(i, i ^ 1 << bit) for i in range(n)])  36.7 us
    pallas_call x9, Pallas kernels, call(): pl.pallas_call(kernel, out_shape=out_shape, in_specs=[SMEM_SPEC if x.dtyp...  32.3 us
    ppermute x21, starting transfers between devices, swap(): return lax.ppermute(x, axis, [(i, i ^ 1 << bit) for i in range(n)])  21.1 us
    pallas_call x1, Pallas kernels, front(): pl.pallas_call(functools.partial(front_kernel, order), out_shape=[f32(hal...  11.6 us
    pallas_call x1, Pallas kernels, trailing(): pl.pallas_call(trail_kernel, grid=(half,), out_shape=[f32(half, own, wide...  11.2 us
    add x9, other arithmetic, part(): lax.dynamic_index_in_dim(kept, which, 0, False)  7.22 us
    ppermute x7, starting transfers between devices, per_device(): lax.ppermute(b, axis, [(i, (i + k) % n) for i in range(n)])  7.1 us
    unnamed x40, local copies, waits for them, and re-layouts  5.49 us
  transfers between devices with their start and end apart: 28, of which 12 were waited for; matrix products, arithmetic and copies ran while one was open for 7% of the time, Pallas kernels for 26%

profile of v3, /device:TPU:1, one launch (start us, length us, event | category | flops | bytes accessed | tf_op | source)
XLA Modules:
  0.0 141.3 jit_solution(15484176560687481438)
XLA Ops:
  0.6 11.6 %shard_map.92 = (f32[9,112,256]{2,1,0:T(8,128)}, f32[9,112,256]{2,1,0:T(8,128)}, bf16[1792,768]{1,0:T(8,128)(2,1)}, bf16[16,768]{1,0:T(8,128)(2,1)}) custom-call(s32[1]{0:T(128)} %bitcast.me_ref, s32[4]{0:T(128)} %count_ref.1, s32[4,384]{1,0:T(4,128)} %offset_ref.1, bf16[4,384]{1,0:T(4,128)(2,1)} %resid_ref.1, bf16[1024,2048]{1,0:T(8,128)(2,1)} %bitcast.43), custom_call_target="tpu_custom_call" | custom-call | flops 1 | bytes 1 | tf_op jit(solution)/shard_map/pallas_call | solution.py:204
  12.4 2.8 %collective-permute-done.got_ref = f32[9,112,256]{2,1,0:T(8,128)S(1)} collective-permute-done((f32[9,112,256]{2,1,0:T(8,128)}, f32[9,112,256]{2,1,0:T(8,128)S(1)}, u32[]{:S(2)}, u32[]{:S(2)}) %collective-permute-start) | collective-permute-done | bytes 1032224 | tf_op jit(solution)/shard_map/ppermute | solution.py:227
  16.2 2.6 %shard_map.93 = (f32[5,112,256]{2,1,0:T(8,128)}, f32[5,112,256]{2,1,0:T(8,128)}) custom-call(s32[1]{0:T(128)} %bitcast.me_ref, f32[9,112,256]{2,1,0:T(8,128)} %get-tuple-element.129.kept_ref, f32[9,112,256]{2,1,0:T(8,128)} %copy-done.2), custom_call_target="tpu_custom_call" | custom-call | flops 1 | bytes 1 | tf_op jit(solution)/shard_map/pallas_call | solution.py:34
  18.8 2.4 %collective-permute-start.1 = (f32[5,112,256]{2,1,0:T(8,128)}, f32[5,112,256]{2,1,0:T(8,128)S(1)}, u32[]{:S(2)}, u32[]{:S(2)}) collective-permute-start(f32[5,112,256]{2,1,0:T(8,128)} %get-tuple-element.132), channel_id=1, source_target_pairs={{0,2},{1,3},{2,0},{3,1},{4,6},{5,7},{6,4},{7,5},{8,10},{9,11},{10,... | collective-permute-start | bytes 1720328 | tf_op jit(solution)/shard_map/ppermute | solution.py:227
  21.2 11.2 %shard_map.94 = (f32[8,112,384]{2,1,0:T(8,128)}, f32[8,112,384]{2,1,0:T(8,128)}, f32[8,112,256]{2,1,0:T(8,128)}, f32[8,112,384]{2,1,0:T(8,128)}, f32[8,112,384]{2,1,0:T(8,128)}, /*index=5*/f32[8,112,256]{2,1,0:T(8,128)}) custom-call(s32[1]{0:T(128)} %bitcast.me_ref, bf16[1792,768]{1,0:T(8,128)(2,1)} %get-tuple-element.134.jt_hbm, ...), custom_call_target="tpu_custom_call" | custom-call | flops 1 | bytes 1 | tf_op jit(solution)/shard_map/pallas_call | solution.py:182
  32.4 2.0 %collective-permute-done.1.got_ref = f32[5,112,256]{2,1,0:T(8,128)S(1)} collective-permute-done((f32[5,112,256]{2,1,0:T(8,128)}, f32[5,112,256]{2,1,0:T(8,128)S(1)}, u32[]{:S(2)}, u32[]{:S(2)}) %collective-permute-start.1) | collective-permute-done | bytes 573472 | tf_op jit(solution)/shard_map/ppermute | solution.py:227
  35.8 2.1 %shard_map.95 = (f32[3,112,256]{2,1,0:T(8,128)}, f32[3,112,256]{2,1,0:T(8,128)}) custom-call(s32[1]{0:T(128)} %bitcast.me_ref, f32[5,112,256]{2,1,0:T(8,128)} %get-tuple-element.144.kept_ref, f32[5,112,256]{2,1,0:T(8,128)} %copy-done.5), custom_call_target="tpu_custom_call" | custom-call | flops 1 | bytes 1 | tf_op jit(solution)/shard_map/pallas_call | solution.py:34
  38.0 1.5 %collective-permute-start.2 = (f32[3,112,256]{2,1,0:T(8,128)}, f32[3,112,256]{2,1,0:T(8,128)S(1)}, u32[]{:S(2)}, u32[]{:S(2)}) collective-permute-start(f32[3,112,256]{2,1,0:T(8,128)} %get-tuple-element.147), channel_id=1, source_target_pairs={{0,4},{1,5},{2,6},{3,7},{4,0},{5,1},{6,2},{7,3},{8,12},{9,13},{10,... | collective-permute-start | bytes 1032200 | tf_op jit(solution)/shard_map/ppermute | solution.py:227
  40.6 2.8 %add_bitcast_fusion.2 = (f32[4,112,384]{2,1,0:T(8,128)S(1)}, f32[4,112,384]{2,1,0:T(8,128)}) fusion(f32[2,4,112,384]{3,2,1,0:T(8,128)} %bitcast.50, s32[]{:T(128)S(6)} %select_n.55, f32[2,4,112,384]{3,2,1,0:T(8,128)} %bitcast.49, s32[]{:T(128)S(6)} %select_n.54), kind=kLoop, calls=%fused_computation.3 | loop fusion | flops 344064 | bytes 4128776 | tf_op jit(solution)/shard_map/add | solution.py:248
  43.4 4.3 %collective-permute-done.2.got_ref = f32[3,112,256]{2,1,0:T(8,128)S(1)} collective-permute-done((f32[3,112,256]{2,1,0:T(8,128)}, f32[3,112,256]{2,1,0:T(8,128)S(1)}, u32[]{:S(2)}, u32[]{:S(2)}) %collective-permute-start.2) | collective-permute-done | bytes 344096 | tf_op jit(solution)/shard_map/ppermute | solution.py:227
  48.4 1.9 %shard_map.96 = (f32[2,112,256]{2,1,0:T(8,128)}, f32[2,112,256]{2,1,0:T(8,128)}) custom-call(s32[1]{0:T(128)} %bitcast.me_ref, f32[3,112,256]{2,1,0:T(8,128)} %get-tuple-element.152.kept_ref, f32[3,112,256]{2,1,0:T(8,128)} %copy-done.7), custom_call_target="tpu_custom_call" | custom-call | flops 1 | bytes 1 | tf_op jit(solution)/shard_map/pallas_call | solution.py:34
  50.3 1.3 collective-permute-start.10
  51.6 2.3 %collective-permute-start.4 = (f32[2,112,256]{2,1,0:T(8,128)}, f32[2,112,256]{2,1,0:T(8,128)S(1)}, u32[]{:S(2)}, u32[]{:S(2)}) collective-permute-start(f32[2,112,256]{2,1,0:T(8,128)} %get-tuple-element.155), channel_id=1, source_target_pairs={{0,8},{1,9},{2,10},{3,11},{4,12},{5,13},{6,14},{7,15},{8,0},{9,1},... | collective-permute-start | bytes 688136 | tf_op jit(solution)/shard_map/ppermute | solution.py:227
  55.4 1.3 add_bitcast_fusion.4
  57.5 6.6 %collective-permute-done.4 = f32[2,112,256]{2,1,0:T(8,128)S(1)} collective-permute-done((f32[2,112,256]{2,1,0:T(8,128)}, f32[2,112,256]{2,1,0:T(8,128)S(1)}, u32[]{:S(2)}, u32[]{:S(2)}) %collective-permute-start.4) | collective-permute-done | bytes 229408 | tf_op jit(solution)/shard_map/ppermute | solution.py:227
  64.2 1.6 %collective-permute-start.7 = (f32[1,112,256]{2,1,0:T(8,128)S(1)}, f32[1,112,256]{2,1,0:T(8,128)S(1)}, u32[]{:S(2)}, u32[]{:S(2)}) collective-permute-start(f32[1,112,256]{2,1,0:T(8,128)S(1)} %get-tuple-element.166.mine_ref), channel_id=1, source_target_pairs={{0,1},{1,0},{2,3},{3,2},{4,5},{5,4},{6,7},{7,6},{8,9},{9,8},{10,11... | collective-permute-start | bytes 344072 | tf_op jit(solution)/shard_map/ppermute | solution.py:227
  67.4 6.9 %shard_map.97 = (f32[8,256]{1,0:T(8,128)}, f32[128,128]{1,0:T(8,128)}, f32[128,128]{1,0:T(8,128)}, f32[128,128]{1,0:T(8,128)}, f32[128,128]{1,0:T(8,128)}) custom-call(s32[1]{0:T(128)} %bitcast.me_ref, f32[1,112,256]{2,1,0:T(8,128)} %copy-done.6, f32[1,112,256]{2,1,0:T(8,128)} %copy-done.9, f32[256,8]{1,0:T(8,128)} %reshape.128.damp_ref), custom_call_target="tpu_custom_call" | custom-call | flops 1 | bytes 1 | tf_op jit(solution)/shard_map/pallas_call | solution.py:34
  75.4 2.8 %collective-permute-start.12 = (f32[2,112,384]{2,1,0:T(8,128)S(1)}, f32[2,112,384]{2,1,0:T(8,128)S(1)}, u32[]{:S(2)}, u32[]{:S(2)}) collective-permute-start(f32[2,112,384]{2,1,0:T(8,128)S(1)} %get-tuple-element.252), channel_id=1, source_target_pairs={{0,4},{1,5},{2,6},{3,7},{4,0},{5,1},{6,2},{7,3},{8,12},{9,13},{10,... | collective-permute-start | bytes 1032200 | tf_op jit(solution)/shard_map/ppermute | solution.py:227
  78.4 2.7 %collective-permute-done.8 = f32[4,112,384]{2,1,0:T(8,128)S(1)} collective-permute-done((f32[4,112,384]{2,1,0:T(8,128)}, f32[4,112,384]{2,1,0:T(8,128)S(1)}, u32[]{:S(2)}, u32[]{:S(2)}) %collective-permute-start.8) | collective-permute-done | bytes 688160 | tf_op jit(solution)/shard_map/ppermute | solution.py:227
  81.2 1.4 collective-permute-start.17
  82.6 6.2 %shard_map.98 = (f32[256,256]{1,0:T(8,128)}, f32[256,256]{1,0:T(8,128)}) custom-call(f32[128,128]{1,0:T(8,128)} %get-tuple-element.181.l11_ref, f32[128,128]{1,0:T(8,128)} %get-tuple-element.182.i11_ref, f32[128,128]{1,0:T(8,128)} %get-tuple-element.183.l21_ref, f32[128,128]{1,0:T(8,128)} %get-tuple-element.184.rest_ref), custom_call_target="tpu_custom_call" | custom-call | flops 1 | bytes 1 | tf_op jit(solution)/shard_map/pallas_call | solution.py:34
  88.9 2.4 %collective-permute-start.16 = (f32[1,112,384]{2,1,0:T(8,128)S(1)}, f32[1,112,384]{2,1,0:T(8,128)S(1)}, u32[]{:S(2)}, u32[]{:S(2)}) collective-permute-start(f32[1,112,384]{2,1,0:T(8,128)S(1)} %get-tuple-element.258), channel_id=1, source_target_pairs={{0,8},{1,9},{2,10},{3,11},{4,12},{5,13},{6,14},{7,15},{8,0},{9,1},... | collective-permute-start | bytes 516104 | tf_op jit(solution)/shard_map/ppermute | solution.py:227
  91.3 1.3 collective-permute-start.13
  93.6 8.4 %collective-permute-done.17 = f32[2,112,384]{2,1,0:T(8,128)S(1)} collective-permute-done((f32[2,112,384]{2,1,0:T(8,128)S(1)}, f32[2,112,384]{2,1,0:T(8,128)S(1)}, u32[]{:S(2)}, u32[]{:S(2)}) %collective-permute-start.17) | collective-permute-done | bytes 344096 | tf_op jit(solution)/shard_map/ppermute | solution.py:227
  102.9 6.3 %collective-permute-done.15 = f32[2,112,256]{2,1,0:T(8,128)S(1)} collective-permute-done((f32[2,112,256]{2,1,0:T(8,128)S(1)}, f32[2,112,256]{2,1,0:T(8,128)S(1)}, u32[]{:S(2)}, u32[]{:S(2)}) %collective-permute-start.15) | collective-permute-done | bytes 229408 | tf_op jit(solution)/shard_map/ppermute | solution.py:227
  111.0 3.4 %shard_map.99 = (f32[8,112,256]{2,1,0:T(8,128)}, f32[112,256]{1,0:T(8,128)}, f32[8,256]{1,0:T(8,128)}, f32[256]{0:T(256)}) custom-call(f32[256,256]{1,0:T(8,128)} %get-tuple-element.201.inverse_ref, f32[8,256]{1,0:T(8,128)} %get-tuple-element.202.g1_ref, f32[8,112,256]{2,1,0:T(8,128)} %pad_maximum_fusion.held_ref), custom_call_target="tpu_custom_call" | custom-call | flops 1 | bytes 1 | tf_op jit(solution)/shard_map/pallas_call | solution.py:34
  115.1 2.7 %collective-permute-done.19.refs_3_ = f32[1,112,256]{2,1,0:T(8,128)S(1)} collective-permute-done((f32[1,112,256]{2,1,0:T(8,128)S(1)}, f32[1,112,256]{2,1,0:T(8,128)S(1)}, u32[]{:S(2)}, u32[]{:S(2)}) %collective-permute-start.19) | collective-permute-done | bytes 114720 | tf_op jit(solution)/shard_map/ppermute | solution.py:227
  118.5 2.1 %shard_map.100 = (f32[112,256]{1,0:T(8,128)}, f32[112,112]{1,0:T(8,128)}, f32[112,112]{1,0:T(8,128)}, f32[112,112]{1,0:T(8,128)}, f32[112,112]{1,0:T(8,128)}, /*...) custom-call(f32[112,384]{1,0:T(8,128)} %add_bitcast_fusion.13.refs_0_, ...), custom_call_target="tpu_custom_call" | custom-call | flops 1 | bytes 1 | tf_op jit(solution)/shard_map/pallas_call | solution.py:34
  124.0 3.9 %collective-permute-start.25 = (f32[112,112]{1,0:T(8,128)}, f32[112,112]{1,0:T(8,128)S(1)}, u32[]{:S(2)}, u32[]{:S(2)}) collective-permute-start(f32[112,112]{1,0:T(8,128)} %get-tuple-element.218), channel_id=1, source_target_pairs={{0,5},{1,6},{2,7},{3,8},{4,9},{5,10},{6,11},{7,12},{8,13},{9,14},{... | collective-permute-start | bytes 150536 | tf_op jit(solution)/shard_map/ppermute | solution.py:514
  130.4 4.3 %shard_map.101.product_ref = f32[112,1792]{1,0:T(8,128)} custom-call(s32[1]{0:T(128)} %bitcast.me_ref, f32[8,112,256]{2,1,0:T(8,128)} %get-tuple-element.223.mine_ref, f32[8,112,256]{2,1,0:T(8,128)} %copy-done.4), custom_call_target="tpu_custom_call" | custom-call | flops 1 | bytes 1 | tf_op jit(solution)/shard_map/pallas_call | solution.py:34
  134.8 2.4 %collective-permute-done.26.refs_8_ = f32[112,112]{1,0:T(8,128)S(1)} collective-permute-done((f32[112,112]{1,0:T(8,128)}, f32[112,112]{1,0:T(8,128)S(1)}, u32[]{:S(2)}, u32[]{:S(2)}) %collective-permute-start.26) | collective-permute-done | bytes 50208 | tf_op jit(solution)/shard_map/ppermute | solution.py:514
  138.5 2.8 %shard_map.102 = (f32[112,1792]{1,0:T(8,128)}, f32[112]{0:T(128)}) custom-call(s32[1]{0:T(128)} %bitcast.me_ref, f32[16,128]{1,0:T(8,128)} %bitcast.54, f32[112,1792]{1,0:T(8,128)} %shard_map.101.product_ref, f32[8,112]{1,0:T(8,128)} %get-tuple-element.228.g2_ref, f32[8,256]{1,0:T(8,128)} %get-tuple-element.229.y_ref, ...), custom_call_target="tpu_custom_call" | custom-call | flops 1 | bytes 1 | tf_op jit(solution)/shard_map/pallas_call | solution.py:34
  (92 shorter events, 21.8 us)
Async XLA Ops:
  12.2 2.9 %collective-permute-start = (f32[9,112,256]{2,1,0:T(8,128)}, f32[9,112,256]{2,1,0:T(8,128)S(1)}, u32[]{:S(2)}, u32[]{:S(2)}) collective-permute-start(f32[9,112,256]{2,1,0:T(8,128)} %get-tuple-element.125), channel_id=1, source_target_pairs={{0,1},{1,0},{2,3},{3,2},{4,5},{5,4},{6,7},{7,6},{8,9},{9,8},{10,11... | collective-permute-start | bytes 3096584 | tf_op jit(solution)/shard_map/ppermute | solution.py:227
  18.8 15.6 %collective-permute-start.1 = (f32[5,112,256]{2,1,0:T(8,128)}, f32[5,112,256]{2,1,0:T(8,128)S(1)}, u32[]{:S(2)}, u32[]{:S(2)}) collective-permute-start(f32[5,112,256]{2,1,0:T(8,128)} %get-tuple-element.132), channel_id=1, source_target_pairs={{0,2},{1,3},{2,0},{3,1},{4,6},{5,7},{6,4},{7,5},{8,10},{9,11},{10,... | collective-permute-start | bytes 1720328 | tf_op jit(solution)/shard_map/ppermute | solution.py:227
  34.4 5.1 %collective-permute-start.3 = (f32[8,112,384]{2,1,0:T(8,128)}, f32[8,112,384]{2,1,0:T(8,128)S(1)}, u32[]{:S(2)}, u32[]{:S(2)}) collective-permute-start(f32[8,112,384]{2,1,0:T(8,128)} %get-tuple-element.148), channel_id=1, source_target_pairs={{0,1},{1,0},{2,3},{3,2},{4,5},{5,4},{6,7},{7,6},{8,9},{9,8},{10,11... | collective-permute-start | bytes 4128776 | tf_op jit(solution)/shard_map/ppermute | solution.py:227
  35.3 18.6 %collective-permute-start.6 = (f32[8,112,384]{2,1,0:T(8,128)}, f32[8,112,384]{2,1,0:T(8,128)S(1)}, u32[]{:S(2)}, u32[]{:S(2)}) collective-permute-start(f32[8,112,384]{2,1,0:T(8,128)} %get-tuple-element.157), channel_id=1, source_target_pairs={{0,1},{1,0},{2,3},{3,2},{4,5},{5,4},{6,7},{7,6},{8,9},{9,8},{10,11... | collective-permute-start | bytes 4128776 | tf_op jit(solution)/shard_map/ppermute | solution.py:227
  35.3 19.8 %collective-permute-start.5 = (f32[8,112,256]{2,1,0:T(8,128)}, f32[8,112,256]{2,1,0:T(8,128)}, u32[]{:S(2)}, u32[]{:S(2)}) collective-permute-start(f32[8,112,256]{2,1,0:T(8,128)} %get-tuple-element.156), channel_id=1, source_target_pairs={{0,1},{1,0},{2,3},{3,2},{4,5},{5,4},{6,7},{7,6},{8,9},{9,8},{10,11... | collective-permute-start | bytes 2752520 | tf_op jit(solution)/shard_map/ppermute | solution.py:227
  38.0 9.7 %collective-permute-start.2 = (f32[3,112,256]{2,1,0:T(8,128)}, f32[3,112,256]{2,1,0:T(8,128)S(1)}, u32[]{:S(2)}, u32[]{:S(2)}) collective-permute-start(f32[3,112,256]{2,1,0:T(8,128)} %get-tuple-element.147), channel_id=1, source_target_pairs={{0,4},{1,5},{2,6},{3,7},{4,0},{5,1},{6,2},{7,3},{8,12},{9,13},{10,... | collective-permute-start | bytes 1032200 | tf_op jit(solution)/shard_map/ppermute | solution.py:227
  40.6 13.3 %copy-start = (f32[8,112,384]{2,1,0:T(8,128)S(1)}, f32[8,112,384]{2,1,0:T(8,128)}, u32[]{:S(2)}) copy-start(f32[8,112,384]{2,1,0:T(8,128)} %get-tuple-element.158) | copy-start | bytes 4128772
  50.3 24.0 %collective-permute-start.10 = (f32[4,112,384]{2,1,0:T(8,128)}, f32[4,112,384]{2,1,0:T(8,128)}, u32[]{:S(2)}, u32[]{:S(2)}) collective-permute-start(f32[4,112,384]{2,1,0:T(8,128)} %get-tuple-element.173), channel_id=1, source_target_pairs={{0,2},{1,3},{2,0},{3,1},{4,6},{5,7},{6,4},{7,5},{8,10},{9,11},{10,... | collective-permute-start | bytes 2064392 | tf_op jit(solution)/shard_map/ppermute | solution.py:227
  51.6 12.5 %collective-permute-start.4 = (f32[2,112,256]{2,1,0:T(8,128)}, f32[2,112,256]{2,1,0:T(8,128)S(1)}, u32[]{:S(2)}, u32[]{:S(2)}) collective-permute-start(f32[2,112,256]{2,1,0:T(8,128)} %get-tuple-element.155), channel_id=1, source_target_pairs={{0,8},{1,9},{2,10},{3,11},{4,12},{5,13},{6,14},{7,15},{8,0},{9,1},... | collective-permute-start | bytes 688136 | tf_op jit(solution)/shard_map/ppermute | solution.py:227
  54.9 26.2 %collective-permute-start.8 = (f32[4,112,384]{2,1,0:T(8,128)}, f32[4,112,384]{2,1,0:T(8,128)S(1)}, u32[]{:S(2)}, u32[]{:S(2)}) collective-permute-start(f32[4,112,384]{2,1,0:T(8,128)} %get-tuple-element.244), channel_id=1, source_target_pairs={{0,2},{1,3},{2,0},{3,1},{4,6},{5,7},{6,4},{7,5},{8,10},{9,11},{10,... | collective-permute-start | bytes 2064392 | tf_op jit(solution)/shard_map/ppermute | solution.py:227
  55.4 8.7 %copy-start.8 = (f32[2,112,256]{2,1,0:T(8,128)S(1)}, f32[2,112,256]{2,1,0:T(8,128)}, u32[]{:S(2)}) copy-start(f32[2,112,256]{2,1,0:T(8,128)} %get-tuple-element.163) | copy-start | bytes 688132
  64.2 2.6 %collective-permute-start.7 = (f32[1,112,256]{2,1,0:T(8,128)S(1)}, f32[1,112,256]{2,1,0:T(8,128)S(1)}, u32[]{:S(2)}, u32[]{:S(2)}) collective-permute-start(f32[1,112,256]{2,1,0:T(8,128)S(1)} %get-tuple-element.166.mine_ref), channel_id=1, source_target_pairs={{0,1},{1,0},{2,3},{3,2},{4,5},{5,4},{6,7},{7,6},{8,9},{9,8},{10,11... | collective-permute-start | bytes 344072 | tf_op jit(solution)/shard_map/ppermute | solution.py:227
  65.8 26.8 %collective-permute-start.14 = (f32[4,112,256]{2,1,0:T(8,128)S(1)}, f32[4,112,256]{2,1,0:T(8,128)S(1)}, u32[]{:S(2)}, u32[]{:S(2)}) collective-permute-start(f32[4,112,256]{2,1,0:T(8,128)S(1)} %get-tuple-element.248), channel_id=1, source_target_pairs={{0,2},{1,3},{2,0},{3,1},{4,6},{5,7},{6,4},{7,5},{8,10},{9,11},{10,... | collective-permute-start | bytes 1376264 | tf_op jit(solution)/shard_map/ppermute | solution.py:227
  66.0 12.3 %collective-permute-start.9 = (f32[1,112,256]{2,1,0:T(8,128)S(1)}, f32[1,112,256]{2,1,0:T(8,128)S(1)}, u32[]{:S(2)}, u32[]{:S(2)}) collective-permute-start(f32[1,112,256]{2,1,0:T(8,128)S(1)} %get-tuple-element.177), channel_id=1, source_target_pairs={{0,8},{1,9},{2,10},{3,11},{4,12},{5,13},{6,14},{7,15},{8,0},{9,1},... | collective-permute-start | bytes 344072 | tf_op jit(solution)/shard_map/ppermute | solution.py:227
  75.4 13.4 %collective-permute-start.12 = (f32[2,112,384]{2,1,0:T(8,128)S(1)}, f32[2,112,384]{2,1,0:T(8,128)S(1)}, u32[]{:S(2)}, u32[]{:S(2)}) collective-permute-start(f32[2,112,384]{2,1,0:T(8,128)S(1)} %get-tuple-element.252), channel_id=1, source_target_pairs={{0,4},{1,5},{2,6},{3,7},{4,0},{5,1},{6,2},{7,3},{8,12},{9,13},{10,... | collective-permute-start | bytes 1032200 | tf_op jit(solution)/shard_map/ppermute | solution.py:227
  78.3 12.9 %collective-permute-start.11 = (f32[2,112,256]{2,1,0:T(8,128)S(1)}, f32[2,112,256]{2,1,0:T(8,128)S(1)}, u32[]{:S(2)}, u32[]{:S(2)}) collective-permute-start(f32[2,112,256]{2,1,0:T(8,128)S(1)} %constant_dynamic-update-slice_fusion), channel_id=1, source_target_pairs={{0,4},{1,5},{2,6},{3,7},{4,0},{5,1},{6,2},{7,3},{8,12},{9,13},{10,... | collective-permute-start | bytes 688136 | tf_op jit(solution)/shard_map/ppermute | solution.py:227
  81.2 20.9 %collective-permute-start.17 = (f32[2,112,384]{2,1,0:T(8,128)S(1)}, f32[2,112,384]{2,1,0:T(8,128)S(1)}, u32[]{:S(2)}, u32[]{:S(2)}) collective-permute-start(f32[2,112,384]{2,1,0:T(8,128)S(1)} %get-tuple-element.250), channel_id=1, source_target_pairs={{0,4},{1,5},{2,6},{3,7},{4,0},{5,1},{6,2},{7,3},{8,12},{9,13},{10,... | collective-permute-start | bytes 1032200 | tf_op jit(solution)/shard_map/ppermute | solution.py:227
  88.9 13.4 %collective-permute-start.16 = (f32[1,112,384]{2,1,0:T(8,128)S(1)}, f32[1,112,384]{2,1,0:T(8,128)S(1)}, u32[]{:S(2)}, u32[]{:S(2)}) collective-permute-start(f32[1,112,384]{2,1,0:T(8,128)S(1)} %get-tuple-element.258), channel_id=1, source_target_pairs={{0,8},{1,9},{2,10},{3,11},{4,12},{5,13},{6,14},{7,15},{8,0},{9,1},... | collective-permute-start | bytes 516104 | tf_op jit(solution)/shard_map/ppermute | solution.py:227
  91.3 18.7 %collective-permute-start.13 = (f32[4,112,256]{2,1,0:T(8,128)S(1)}, f32[4,112,256]{2,1,0:T(8,128)S(1)}, u32[]{:S(2)}, u32[]{:S(2)}) collective-permute-start(f32[4,112,256]{2,1,0:T(8,128)S(1)} %constant_dynamic-update-slice_fusion.2), channel_id=1, source_target_pairs={{0,2},{1,3},{2,0},{3,1},{4,6},{5,7},{6,4},{7,5},{8,10},{9,11},{10,... | collective-permute-start | bytes 1376264 | tf_op jit(solution)/shard_map/ppermute | solution.py:227
  92.6 16.6 %collective-permute-start.15 = (f32[2,112,256]{2,1,0:T(8,128)S(1)}, f32[2,112,256]{2,1,0:T(8,128)S(1)}, u32[]{:S(2)}, u32[]{:S(2)}) collective-permute-start(f32[2,112,256]{2,1,0:T(8,128)S(1)} %get-tuple-element.253), channel_id=1, source_target_pairs={{0,4},{1,5},{2,6},{3,7},{4,0},{5,1},{6,2},{7,3},{8,12},{9,13},{10,... | collective-permute-start | bytes 688136 | tf_op jit(solution)/shard_map/ppermute | solution.py:227
  102.1 12.2 %collective-permute-start.18 = (f32[1,112,384]{2,1,0:T(8,128)S(1)}, f32[1,112,384]{2,1,0:T(8,128)S(1)}, u32[]{:S(2)}, u32[]{:S(2)}) collective-permute-start(f32[1,112,384]{2,1,0:T(8,128)S(1)} %get-tuple-element.256), channel_id=1, source_target_pairs={{0,8},{1,9},{2,10},{3,11},{4,12},{5,13},{6,14},{7,15},{8,0},{9,1},... | collective-permute-start | bytes 516104 | tf_op jit(solution)/shard_map/ppermute | solution.py:227
  109.9 7.9 %collective-permute-start.19 = (f32[1,112,256]{2,1,0:T(8,128)S(1)}, f32[1,112,256]{2,1,0:T(8,128)S(1)}, u32[]{:S(2)}, u32[]{:S(2)}) collective-permute-start(f32[1,112,256]{2,1,0:T(8,128)S(1)} %get-tuple-element.260), channel_id=1, source_target_pairs={{0,8},{1,9},{2,10},{3,11},{4,12},{5,13},{6,14},{7,15},{8,0},{9,1},... | collective-permute-start | bytes 344072 | tf_op jit(solution)/shard_map/ppermute | solution.py:227
  120.5 8.9 %collective-permute-start.20 = (f32[8,112,256]{2,1,0:T(8,128)}, f32[8,112,256]{2,1,0:T(8,128)S(1)}, u32[]{:S(2)}, u32[]{:S(2)}) collective-permute-start(f32[8,112,256]{2,1,0:T(8,128)} %get-tuple-element.223.mine_ref), channel_id=1, source_target_pairs={{0,1},{1,0},{2,3},{3,2},{4,5},{5,4},{6,7},{7,6},{8,9},{9,8},{10,11... | collective-permute-start | bytes 2752520 | tf_op jit(solution)/shard_map/ppermute | solution.py:227
  121.5 2.5 %collective-permute-start.21 = (f32[112,112]{1,0:T(8,128)}, f32[112,112]{1,0:T(8,128)S(1)}, u32[]{:S(2)}, u32[]{:S(2)}) collective-permute-start(f32[112,112]{1,0:T(8,128)} %get-tuple-element.214), channel_id=1, source_target_pairs={{0,1},{1,2},{2,3},{3,4},{4,5},{5,6},{6,7},{7,8},{8,9},{9,10},{10,1... | collective-permute-start | bytes 150536 | tf_op jit(solution)/shard_map/ppermute | solution.py:514
  122.4 6.8 %collective-permute-start.22 = (f32[112,112]{1,0:T(8,128)}, f32[112,112]{1,0:T(8,128)S(1)}, u32[]{:S(2)}, u32[]{:S(2)}) collective-permute-start(f32[112,112]{1,0:T(8,128)} %get-tuple-element.215), channel_id=1, source_target_pairs={{0,2},{1,3},{2,4},{3,5},{4,6},{5,7},{6,8},{7,9},{8,10},{9,11},{10,... | collective-permute-start | bytes 150536 | tf_op jit(solution)/shard_map/ppermute | solution.py:514
  123.2 11.5 %collective-permute-start.23 = (f32[112,112]{1,0:T(8,128)}, f32[112,112]{1,0:T(8,128)S(1)}, u32[]{:S(2)}, u32[]{:S(2)}) collective-permute-start(f32[112,112]{1,0:T(8,128)} %get-tuple-element.216), channel_id=1, source_target_pairs={{0,3},{1,4},{2,5},{3,6},{4,7},{5,8},{6,9},{7,10},{8,11},{9,12},{10... | collective-permute-start | bytes 150536 | tf_op jit(solution)/shard_map/ppermute | solution.py:514
  124.0 10.8 %collective-permute-start.24 = (f32[112,112]{1,0:T(8,128)}, f32[112,112]{1,0:T(8,128)S(1)}, u32[]{:S(2)}, u32[]{:S(2)}) collective-permute-start(f32[112,112]{1,0:T(8,128)} %get-tuple-element.217), channel_id=1, source_target_pairs={{0,4},{1,5},{2,6},{3,7},{4,8},{5,9},{6,10},{7,11},{8,12},{9,13},{1... | collective-permute-start | bytes 150536 | tf_op jit(solution)/shard_map/ppermute | solution.py:514
  124.0 13.9 %copy-start.11 = (f32[112,112]{1,0:T(8,128)}, f32[112,112]{1,0:T(8,128)S(1)}, u32[]{:S(2)}) copy-start(f32[112,112]{1,0:T(8,128)S(1)} %collective-permute-done.21.refs_3_) | copy-start | bytes 150532
  124.0 10.8 %collective-permute-start.25 = (f32[112,112]{1,0:T(8,128)}, f32[112,112]{1,0:T(8,128)S(1)}, u32[]{:S(2)}, u32[]{:S(2)}) collective-permute-start(f32[112,112]{1,0:T(8,128)} %get-tuple-element.218), channel_id=1, source_target_pairs={{0,5},{1,6},{2,7},{3,8},{4,9},{5,10},{6,11},{7,12},{8,13},{9,14},{... | collective-permute-start | bytes 150536 | tf_op jit(solution)/shard_map/ppermute | solution.py:514
  129.2 8.7 %copy-start.12 = (f32[112,112]{1,0:T(8,128)}, f32[112,112]{1,0:T(8,128)S(1)}, u32[]{:S(2)}) copy-start(f32[112,112]{1,0:T(8,128)S(1)} %collective-permute-done.22.refs_4_) | copy-start | bytes 150532
  129.2 8.0 %collective-permute-start.26 = (f32[112,112]{1,0:T(8,128)}, f32[112,112]{1,0:T(8,128)S(1)}, u32[]{:S(2)}, u32[]{:S(2)}) collective-permute-start(f32[112,112]{1,0:T(8,128)} %get-tuple-element.219), channel_id=1, source_target_pairs={{0,6},{1,7},{2,8},{3,9},{4,10},{5,11},{6,12},{7,13},{8,14},{9,15},... | collective-permute-start | bytes 150536 | tf_op jit(solution)/shard_map/ppermute | solution.py:514
  129.4 8.4 %collective-permute-start.27 = (f32[112,112]{1,0:T(8,128)}, f32[112,112]{1,0:T(8,128)S(1)}, u32[]{:S(2)}, u32[]{:S(2)}) collective-permute-start(f32[112,112]{1,0:T(8,128)} %get-tuple-element.220), channel_id=1, source_target_pairs={{0,7},{1,8},{2,9},{3,10},{4,11},{5,12},{6,13},{7,14},{8,15},{9,0},... | collective-permute-start | bytes 150536 | tf_op jit(solution)/shard_map/ppermute | solution.py:514
  (15 other events, 22.6 us)

commit v4 on v3

--- a/solution.py
+++ b/solution.py
@@ -64,15 +64,19 @@
         copy.start()
     window, pick = window_part(count_ref, offset_ref, resid_ref, depth, jp_ref.shape[1], r_ref)
     copies = []
+    group = blocks // 2
     for b in range(blocks):
-        feat_copies[b].wait()
+        if b % group == 0:
+            for copy in feat_copies[b : b + group]:
+                copy.wait()
         turned = dot_nt(pick, feat_ref[:, b * BLK : (b + 1) * BLK]).astype(jnp.bfloat16)
         jac = jnp.dot(turned, window, preferred_element_type=jnp.float32).astype(jnp.bfloat16)
         jp_ref[b * pan_b : (b + 1) * pan_b, :] = jac[:pan_b]
-        rows = slice(b * trail_b, (b + 1) * trail_b)
-        jt_ref[rows, :] = jac[pan_b:]
-        copies.append(pltpu.make_async_copy(jt_ref.at[rows], jt_hbm.at[rows], jt_sems.at[b]))
-        copies[-1].start()
+        jt_ref[b * trail_b : (b + 1) * trail_b, :] = jac[pan_b:]
+        if b % group == group - 1:
+            rows = slice((b + 1 - group) * trail_b, (b + 1) * trail_b)
+            copies.append(pltpu.make_async_copy(jt_ref.at[rows], jt_hbm.at[rows], jt_sems.at[b // group]))
+            copies[-1].start()
     jp = jp_ref[...]
     own, count = sent_hbm.shape[1], sent_hbm.shape[0] - 1
     ways = ((sent_hbm, 1 - core), (kept_hbm, core))
@@ -91,13 +95,14 @@
         pack_ref[k, part + part // 2 :, :] = grad[: own - part - part // 2]
         copies.append(pltpu.make_async_copy(pack_ref.at[k], out.at[count], out_sems.at[k, count]))
         copies[-1].start()
-    for m in range(count):
-        rows = slice(m * 2 * own, (m + 1) * 2 * own)
+    for first in range(0, count, count // 4):
+        rows = slice(first * 2 * own, (first + count // 4) * 2 * own)
         n21_ref[rows, :] = dot_nt(jt_ref[rows, :], jp)
-        for k, (out, which) in enumerate(ways):
-            source = n21_ref.at[pl.ds(pl.multiple_of(m * 2 * own + which * own, 16), own), :]
-            copies.append(pltpu.make_async_copy(source, out.at[place_of(m, order)], out_sems.at[k, m]))
-            copies[-1].start()
+        for m in range(first, first + count // 4):
+            for k, (out, which) in enumerate(ways):
+                source = n21_ref.at[pl.ds(pl.multiple_of(m * 2 * own + which * own, 16), own), :]
+                copies.append(pltpu.make_async_copy(source, out.at[place_of(m, order)], out_sems.at[k, m]))
+                copies[-1].start()
     for copy in copies:
         copy.wait()
 
@@ -106,23 +111,20 @@
     tiles, slots = offset_ref.shape
     samples = depth // tiles
     lane = lax.broadcasted_iota(jnp.int32, (8, cap), 1)
-    start = jnp.full((8, cap), -depth, jnp.int32)
-    resid = jnp.zeros((8, cap), jnp.float32)
+    row = lax.broadcasted_iota(jnp.int32, (8, slots), 0)
+    merged = jnp.where(lax.broadcasted_iota(jnp.int32, (8, cap), 0) == 0, -1.0 * depth, 0.0)
     before = jnp.int32(0)
     for t in range(tiles):
         count = count_ref[t]
         live = (lane >= before) & (lane < before + count)
-        offs = jnp.concatenate([offset_ref[t : t + 1, :], jnp.zeros((1, cap - slots), jnp.int32)], axis=1)
-        offs = pltpu.roll(jnp.broadcast_to(offs, (8, cap)), before, 1)
-        res = jnp.concatenate([resid_ref[t : t + 1, :].astype(jnp.float32), jnp.zeros((1, cap - slots), jnp.float32)], axis=1)
-        res = pltpu.roll(jnp.broadcast_to(res, (8, cap)), before, 1)
-        start = jnp.where(live, offs + t * samples, start)
-        resid = jnp.where(live, res, resid)
+        offs = (offset_ref[t : t + 1, :] + t * samples).astype(jnp.float32)
+        both = jnp.where(row == 0, offs, jnp.where(row == 1, resid_ref[t : t + 1, :].astype(jnp.float32), 0.0))
+        both = jnp.concatenate([both, jnp.zeros((8, cap - slots), jnp.float32)], axis=1)
+        merged = jnp.where(live, pltpu.roll(both, before, 1), merged)
         before = before + count
-    first = lax.broadcasted_iota(jnp.int32, (8, cap), 0) == 0
-    resid = jnp.where(first, resid, 0.0).astype(jnp.bfloat16)
-    r_ref[...] = jnp.concatenate([resid, jnp.zeros((8, cap), jnp.bfloat16)], axis=0)
-    after = lax.broadcasted_iota(jnp.int32, (depth, cap), 0) - start[0:1, :]
+    start = merged[0:1].astype(jnp.int32)
+    r_ref[...] = jnp.concatenate([merged[1:], jnp.zeros((9, cap), jnp.float32)], axis=0).astype(jnp.bfloat16)
+    after = lax.broadcasted_iota(jnp.int32, (depth, cap), 0) - start
     window = jnp.where((after >= 0) & (after < LWIN), 1.0 / LWIN, 0.0).astype(jnp.bfloat16)
     pan_b = BLK // STRIDE
     row = lax.broadcasted_iota(jnp.int32, (BLK, BLK), 0)
@@ -214,7 +216,7 @@
             pltpu.VMEM((panel, panel), jnp.float32),
             pltpu.VMEM((2, own, panel), jnp.float32),
             pltpu.SemaphoreType.DMA((params // BLK,)),
-            pltpu.SemaphoreType.DMA((params // BLK,)),
+            pltpu.SemaphoreType.DMA((2,)),
             pltpu.SemaphoreType.DMA((2, half + 1)),
         ],
         compiler_params=pltpu.CompilerParams(vmem_limit_bytes=VMEM_LIMIT),
@@ -399,7 +401,7 @@
     rhs_ref[...] = (g2_ref[...] - dot_nt(y_ref[...], lower_ref[...], EXACT))[0]
     me = me_ref[0]
     own = schur_ref.shape[0]
-    turned = [m[...] for m in reversed(mirrors)]
+    turned = [m[...] for m in reversed(mirrors[1:])] + [mirrors[0][...]]
     width = schur_ref.shape[1] - sum(x.shape[1] for x in turned)
     whole = jnp.concatenate([c[...] for c in chunks], axis=1)[:, :width]
     row = lax.broadcasted_iota(jnp.int32, (own, own), 0)
@@ -476,10 +478,8 @@
     t_sent = list(t_sent)
     t_got = [swap(x, axis, 0) for x in t_sent]
     p, p_got = panel_fold(p, p_got, order[1])
-    trail_fold(0, 0)
+    trail_step(0, 0)
     p, p_got = panel_fold(p, p_got, order[2])
-    t_sent[0] = lax.optimization_barrier((t_sent[0], p))[0]
-    trail_send(0, 0)
     trail_step(1, 0)
     trail_step(2, 0)
     damp_panel, damp_trail = then(damping)[0].reshape(panel, STRIDE), damping.reshape(n, params // n)
@@ -489,29 +489,38 @@
     held, n11 = p[:1], p[1:]
     n11_got = swap(n11, axis, 0)
     got = swap(held, axis, order[2])
+    trail_step(0, 1)
     g1, *state = did(
         call(factor_first_kernel, then(me1, n11, n11_got, damp_panel), [f32(8, panel)] + [f32(panel // 2, panel // 2)] * 4)
     )
-    trail_step(0, 1)
     held = joined(held, got)
     got = swap(held, axis, order[1])
+    trail_step(0, 2)
     trail_step(1, 1)
     factor, inverse = did(call(factor_second_kernel, then(*state), [f32(panel, panel)] * 2))
-    trail_step(0, 2)
     held = joined(held, got)
     got = swap(held, axis, order[0])
     trail_step(2, 1)
     trail_step(1, 2)
     first = trail_sum(0)
+    near = widths[0] // own
+    _, blocks, _ = did(mirror([then(first)], own, range(1, near), 0, []))
+
+    def mirrored(blocks, ks):
+        return [lax.ppermute(b, axis, [(i, (i + k) % n) for i in range(n)]) for k, b in zip(ks, blocks)]
+
+    near_mirrors = mirrored(blocks, range(1, near))
     trail_step(2, 2)
     held = joined(held, got)
     mine, lower, y, y0 = did(
         call(lower_kernel, then(inverse, g1, held), [f32(half, own, panel), f32(own, panel), f32(8, panel), f32(panel)])
     )
     second = trail_sum(1)
-    (third,), blocks, g2 = did(mirror([(first,), (second,), then(t[2], t_got[2])], own, range(1, count + 1), (count + 2) * own, []))
+    (third, right), blocks, g2 = did(
+        mirror([(first,), (second,), then(t[2], t_got[2])], own, range(near, count + 1), (count + 2) * own, near_mirrors)
+    )
     chunks = [first, second, third]
-    mirrors = [lax.ppermute(b, axis, [(i, (i + k) % n) for i in range(n)]) for k, b in enumerate(blocks, 1)]
+    mirrors = mirrored(blocks, range(near, count + 1))
     other = swap(lax.optimization_barrier((mine, chunks))[0], axis, 0)
     product = did(
         call(
@@ -523,7 +532,7 @@
     )
     schur, rhs0 = call(
         functools.partial(last_kernel, len(widths)),
-        then(me1, damp_trail, product, g2, y, lower, *chunks, *mirrors),
+        then(me1, damp_trail, product, g2, y, lower, *chunks, right, *mirrors),
         [f32(own, trail), f32(own)],
     )
     return (factor, lower, schur, y0, rhs0)

time: 142 us -> 134 us (0.944)
  waiting for transfers between devices: 41.1 us -> 21.7 us
  starting transfers between devices: 28.2 us -> 35.1 us
  other arithmetic: 9.66 us -> 12.8 us
    ppermute x21, waiting for transfers between devices: 36.7 us -> 19.5 us  [swap(): return lax.ppermute(x, axis, [(i, i ^ 1 << bit) for i in range(n)])]
    ppermute x7, starting transfers between devices: 7.1 us -> 10.8 us  [mirrored(): lax.ppermute(b, axis, [(i, (i + k) % n) for i in range(n)])]
    ppermute x21, starting transfers between devices: 21.1 us -> 24.4 us  [swap(): return lax.ppermute(x, axis, [(i, i ^ 1 << bit) for i in range(n)])]
    add x9, other arithmetic: 7.22 us -> 10.3 us  [part(): lax.dynamic_index_in_dim(kept, which, 0, False)]
    ppermute x7, waiting for transfers between devices: 4.37 us -> 2.18 us  [mirrored(): lax.ppermute(b, axis, [(i, (i + k) % n) for i in range(n)])]
    pallas_call x9 -> x10, Pallas kernels: 32.3 us -> 34.1 us  [call(): pl.pallas_call(kernel, out_shape=out_shape, in_specs=[SMEM_SPEC if x.dtyp...]
    unnamed x40 -> x38, local copies, waits for them, and re-layouts: 5.49 us -> 5.72 us
  transfers between devices with their start and end apart: 28 -> 28, of which waited for: 12 -> 11; matrix products, arithmetic and copies ran while one was open for 7% -> 11% of each run, Pallas kernels for 26% -> 28%
where the time goes in v4:
time: 134 us
  Pallas kernels  55.8 us (42%)
  starting transfers between devices  35.1 us (26%)
  waiting for transfers between devices  21.7 us (16%)
  other arithmetic  12.8 us (10%)
  local copies, waits for them, and re-layouts  7.41 us (6%)
    pallas_call x10, Pallas kernels, call(): pl.pallas_call(kernel, out_shape=out_shape, in_specs=[SMEM_SPEC if x.dtyp...  34.1 us
    ppermute x21, starting transfers between devices, swap(): return lax.ppermute(x, axis, [(i, i ^ 1 << bit) for i in range(n)])  24.4 us
    ppermute x21, waiting for transfers between devices, swap(): return lax.ppermute(x, axis, [(i, i ^ 1 << bit) for i in range(n)])  19.5 us
    pallas_call x1, Pallas kernels, trailing(): pl.pallas_call(trail_kernel, grid=(half,), out_shape=[f32(half, own, wide...  11.2 us
    ppermute x7, starting transfers between devices, mirrored(): lax.ppermute(b, axis, [(i, (i + k) % n) for i in range(n)])  10.8 us
    pallas_call x1, Pallas kernels, front(): pl.pallas_call(functools.partial(front_kernel, order), out_shape=[f32(hal...  10.5 us
    add x9, other arithmetic, part(): lax.dynamic_index_in_dim(kept, which, 0, False)  10.3 us
    unnamed x38, local copies, waits for them, and re-layouts  5.72 us
  transfers between devices with their start and end apart: 28, of which 11 were waited for; matrix products, arithmetic and copies ran while one was open for 11% of the time, Pallas kernels for 28%

profile of v4, /device:TPU:1, one launch (start us, length us, event | category | flops | bytes accessed | tf_op | source)
XLA Modules:
  0.0 133.7 jit_solution(15024577617744616225)
XLA Ops:
  0.6 10.5 %shard_map.92 = (f32[9,112,256]{2,1,0:T(8,128)}, f32[9,112,256]{2,1,0:T(8,128)}, bf16[1792,768]{1,0:T(8,128)(2,1)}, bf16[16,768]{1,0:T(8,128)(2,1)}) custom-call(s32[1]{0:T(128)} %bitcast.me_ref, s32[4]{0:T(128)} %count_ref.1, s32[4,384]{1,0:T(4,128)} %offset_ref.1, bf16[4,384]{1,0:T(4,128)(2,1)} %resid_ref.1, bf16[1024,2048]{1,0:T(8,128)(2,1)} %bitcast.43), custom_call_target="tpu_custom_call" | custom-call | flops 1 | bytes 1 | tf_op jit(solution)/shard_map/pallas_call | solution.py:206
  11.3 2.8 %collective-permute-done.got_ref = f32[9,112,256]{2,1,0:T(8,128)S(1)} collective-permute-done((f32[9,112,256]{2,1,0:T(8,128)}, f32[9,112,256]{2,1,0:T(8,128)S(1)}, u32[]{:S(2)}, u32[]{:S(2)}) %collective-permute-start) | collective-permute-done | bytes 1032224 | tf_op jit(solution)/shard_map/ppermute | solution.py:229
  15.1 2.6 %shard_map.93 = (f32[5,112,256]{2,1,0:T(8,128)}, f32[5,112,256]{2,1,0:T(8,128)}) custom-call(s32[1]{0:T(128)} %bitcast.me_ref, f32[9,112,256]{2,1,0:T(8,128)} %get-tuple-element.129.kept_ref, f32[9,112,256]{2,1,0:T(8,128)} %copy-done.2), custom_call_target="tpu_custom_call" | custom-call | flops 1 | bytes 1 | tf_op jit(solution)/shard_map/pallas_call | solution.py:34
  17.7 2.4 %collective-permute-start.1 = (f32[5,112,256]{2,1,0:T(8,128)}, f32[5,112,256]{2,1,0:T(8,128)S(1)}, u32[]{:S(2)}, u32[]{:S(2)}) collective-permute-start(f32[5,112,256]{2,1,0:T(8,128)} %get-tuple-element.132), channel_id=1, source_target_pairs={{0,2},{1,3},{2,0},{3,1},{4,6},{5,7},{6,4},{7,5},{8,10},{9,11},{10,... | collective-permute-start | bytes 1720328 | tf_op jit(solution)/shard_map/ppermute | solution.py:229
  20.1 11.2 %shard_map.94 = (f32[8,112,384]{2,1,0:T(8,128)}, f32[8,112,384]{2,1,0:T(8,128)}, f32[8,112,256]{2,1,0:T(8,128)}, f32[8,112,384]{2,1,0:T(8,128)}, f32[8,112,384]{2,1,0:T(8,128)}, /*index=5*/f32[8,112,256]{2,1,0:T(8,128)}) custom-call(s32[1]{0:T(128)} %bitcast.me_ref, bf16[1792,768]{1,0:T(8,128)(2,1)} %get-tuple-element.134.jt_hbm, ...), custom_call_target="tpu_custom_call" | custom-call | flops 1 | bytes 1 | tf_op jit(solution)/shard_map/pallas_call | solution.py:184
  31.3 2.0 %collective-permute-done.1.got_ref = f32[5,112,256]{2,1,0:T(8,128)S(1)} collective-permute-done((f32[5,112,256]{2,1,0:T(8,128)}, f32[5,112,256]{2,1,0:T(8,128)S(1)}, u32[]{:S(2)}, u32[]{:S(2)}) %collective-permute-start.1) | collective-permute-done | bytes 573472 | tf_op jit(solution)/shard_map/ppermute | solution.py:229
  34.7 2.2 %shard_map.95 = (f32[3,112,256]{2,1,0:T(8,128)}, f32[3,112,256]{2,1,0:T(8,128)}) custom-call(s32[1]{0:T(128)} %bitcast.me_ref, f32[5,112,256]{2,1,0:T(8,128)} %get-tuple-element.144.kept_ref, f32[5,112,256]{2,1,0:T(8,128)} %copy-done.5), custom_call_target="tpu_custom_call" | custom-call | flops 1 | bytes 1 | tf_op jit(solution)/shard_map/pallas_call | solution.py:34
  36.9 1.5 %collective-permute-start.2 = (f32[3,112,256]{2,1,0:T(8,128)}, f32[3,112,256]{2,1,0:T(8,128)S(1)}, u32[]{:S(2)}, u32[]{:S(2)}) collective-permute-start(f32[3,112,256]{2,1,0:T(8,128)} %get-tuple-element.147), channel_id=1, source_target_pairs={{0,4},{1,5},{2,6},{3,7},{4,0},{5,1},{6,2},{7,3},{8,12},{9,13},{10,... | collective-permute-start | bytes 1032200 | tf_op jit(solution)/shard_map/ppermute | solution.py:229
  39.9 2.8 %add_bitcast_fusion.2 = (f32[4,112,384]{2,1,0:T(8,128)S(1)}, f32[4,112,384]{2,1,0:T(8,128)}) fusion(f32[2,4,112,384]{3,2,1,0:T(8,128)} %bitcast.49, s32[]{:T(128)S(6)} %select_n.55, f32[2,4,112,384]{3,2,1,0:T(8,128)} %bitcast.48, s32[]{:T(128)S(6)} %select_n.54), kind=kLoop, calls=%fused_computation.3 | loop fusion | flops 344064 | bytes 4128776 | tf_op jit(solution)/shard_map/add | solution.py:250
  42.7 1.5 %collective-permute-start.8 = (f32[4,112,384]{2,1,0:T(8,128)}, f32[4,112,384]{2,1,0:T(8,128)}, u32[]{:S(2)}, u32[]{:S(2)}) collective-permute-start(f32[4,112,384]{2,1,0:T(8,128)} %get-tuple-element.246), channel_id=1, source_target_pairs={{0,2},{1,3},{2,0},{3,1},{4,6},{5,7},{6,4},{7,5},{8,10},{9,11},{10,... | collective-permute-start | bytes 2064392 | tf_op jit(solution)/shard_map/ppermute | solution.py:229
  44.2 2.5 %collective-permute-done.2.got_ref = f32[3,112,256]{2,1,0:T(8,128)S(1)} collective-permute-done((f32[3,112,256]{2,1,0:T(8,128)}, f32[3,112,256]{2,1,0:T(8,128)S(1)}, u32[]{:S(2)}, u32[]{:S(2)}) %collective-permute-start.2) | collective-permute-done | bytes 344096 | tf_op jit(solution)/shard_map/ppermute | solution.py:229
  47.4 1.9 %shard_map.96 = (f32[2,112,256]{2,1,0:T(8,128)}, f32[2,112,256]{2,1,0:T(8,128)}) custom-call(s32[1]{0:T(128)} %bitcast.me_ref, f32[3,112,256]{2,1,0:T(8,128)} %get-tuple-element.152.kept_ref, f32[3,112,256]{2,1,0:T(8,128)} %copy-done.7), custom_call_target="tpu_custom_call" | custom-call | flops 1 | bytes 1 | tf_op jit(solution)/shard_map/pallas_call | solution.py:34
  49.3 2.4 %collective-permute-start.4 = (f32[2,112,256]{2,1,0:T(8,128)}, f32[2,112,256]{2,1,0:T(8,128)S(1)}, u32[]{:S(2)}, u32[]{:S(2)}) collective-permute-start(f32[2,112,256]{2,1,0:T(8,128)} %get-tuple-element.155), channel_id=1, source_target_pairs={{0,8},{1,9},{2,10},{3,11},{4,12},{5,13},{6,14},{7,15},{8,0},{9,1},... | collective-permute-start | bytes 688136 | tf_op jit(solution)/shard_map/ppermute | solution.py:229
  51.7 2.4 %add_bitcast_fusion = (f32[4,112,384]{2,1,0:T(8,128)S(1)}, f32[4,112,384]{2,1,0:T(8,128)}) fusion(f32[2,4,112,384]{3,2,1,0:T(8,128)} %bitcast.7, s32[]{:T(128)S(6)} %select_n.55, f32[2,4,112,384]{3,2,1,0:T(8,128)S(1)} %bitcast.47, s32[]{:T(128)S(6)} %select_n.54), kind=kLoop, calls=%fused_computation.1 | loop fusion | flops 344064 | bytes 4128776 | tf_op jit(solution)/shard_map/add | solution.py:250
  57.5 4.3 %collective-permute-done.4 = f32[2,112,256]{2,1,0:T(8,128)S(1)} collective-permute-done((f32[2,112,256]{2,1,0:T(8,128)}, f32[2,112,256]{2,1,0:T(8,128)S(1)}, u32[]{:S(2)}, u32[]{:S(2)}) %collective-permute-start.4) | collective-permute-done | bytes 229408 | tf_op jit(solution)/shard_map/ppermute | solution.py:229
  61.9 1.7 %collective-permute-start.7 = (f32[1,112,256]{2,1,0:T(8,128)S(1)}, f32[1,112,256]{2,1,0:T(8,128)}, u32[]{:S(2)}, u32[]{:S(2)}) collective-permute-start(f32[1,112,256]{2,1,0:T(8,128)S(1)} %get-tuple-element.168.mine_ref), channel_id=1, source_target_pairs={{0,1},{1,0},{2,3},{3,2},{4,5},{5,4},{6,7},{7,6},{8,9},{9,8},{10,11... | collective-permute-start | bytes 344072 | tf_op jit(solution)/shard_map/ppermute | solution.py:229
  63.6 1.9 %add_bitcast_fusion.8 = (f32[2,112,384]{2,1,0:T(8,128)S(1)}, f32[2,112,384]{2,1,0:T(8,128)}) fusion(f32[2,2,112,384]{3,2,1,0:T(8,128)} %bitcast.15, s32[]{:T(128)S(6)} %select_n.57, f32[2,2,112,384]{3,2,1,0:T(8,128)S(1)} %bitcast.45, s32[]{:T(128)S(6)} %select_n.56), kind=kLoop, calls=%fused_computation.9 | loop fusion | flops 172032 | bytes 2064392 | tf_op jit(solution)/shard_map/add | solution.py:250
  65.4 3.6 %collective-permute-start.10 = (f32[2,112,384]{2,1,0:T(8,128)}, f32[2,112,384]{2,1,0:T(8,128)}, u32[]{:S(2)}, u32[]{:S(2)}) collective-permute-start(f32[2,112,384]{2,1,0:T(8,128)} %get-tuple-element.252), channel_id=1, source_target_pairs={{0,4},{1,5},{2,6},{3,7},{4,0},{5,1},{6,2},{7,3},{8,12},{9,13},{10,... | collective-permute-start | bytes 1032200 | tf_op jit(solution)/shard_map/ppermute | solution.py:229
  70.2 6.9 %shard_map.97 = (f32[8,256]{1,0:T(8,128)}, f32[128,128]{1,0:T(8,128)}, f32[128,128]{1,0:T(8,128)}, f32[128,128]{1,0:T(8,128)}, f32[128,128]{1,0:T(8,128)}) custom-call(s32[1]{0:T(128)} %bitcast.me_ref, f32[1,112,256]{2,1,0:T(8,128)} %copy-done.6, f32[1,112,256]{2,1,0:T(8,128)} %collective-permute-done.7.other_ref, f32[256,8]{1,0:T(8,128)} %reshape.128.damp_ref), custom_call_target="tpu_custom_call" | custom-call | flops 1 | bytes 1 | tf_op jit(solution)/shard_map/pallas_call | solution.py:34
  80.3 1.6 %collective-permute-start.17 = (f32[2,112,384]{2,1,0:T(8,128)S(1)}, f32[2,112,384]{2,1,0:T(8,128)S(1)}, u32[]{:S(2)}, u32[]{:S(2)}) collective-permute-start(f32[2,112,384]{2,1,0:T(8,128)S(1)} %get-tuple-element.250), channel_id=1, source_target_pairs={{0,4},{1,5},{2,6},{3,7},{4,0},{5,1},{6,2},{7,3},{8,12},{9,13},{10,... | collective-permute-start | bytes 1032200 | tf_op jit(solution)/shard_map/ppermute | solution.py:229
  81.9 6.2 %shard_map.98 = (f32[256,256]{1,0:T(8,128)}, f32[256,256]{1,0:T(8,128)}) custom-call(f32[128,128]{1,0:T(8,128)} %get-tuple-element.182.l11_ref, f32[128,128]{1,0:T(8,128)} %get-tuple-element.183.i11_ref, f32[128,128]{1,0:T(8,128)} %get-tuple-element.184.l21_ref, f32[128,128]{1,0:T(8,128)} %get-tuple-element.185.rest_ref), custom_call_target="tpu_custom_call" | custom-call | flops 1 | bytes 1 | tf_op jit(solution)/shard_map/pallas_call | solution.py:34
  89.7 5.6 %collective-permute-done.17 = f32[2,112,384]{2,1,0:T(8,128)S(1)} collective-permute-done((f32[2,112,384]{2,1,0:T(8,128)S(1)}, f32[2,112,384]{2,1,0:T(8,128)S(1)}, u32[]{:S(2)}, u32[]{:S(2)}) %collective-permute-start.17) | collective-permute-done | bytes 344096 | tf_op jit(solution)/shard_map/ppermute | solution.py:229
  96.5 1.7 %shard_map.99 = (f32[112,112]{1,0:T(8,128)}, f32[112,112]{1,0:T(8,128)}) custom-call(f32[112,384]{1,0:T(8,128)} %add_bitcast_fusion.13.refs_0_), custom_call_target="tpu_custom_call" | custom-call | flops 1 | bytes 1 | tf_op jit(solution)/shard_map/pallas_call | solution.py:34
  98.2 3.0 %collective-permute-start.20 = (f32[112,112]{1,0:T(8,128)}, f32[112,112]{1,0:T(8,128)S(1)}, u32[]{:S(2)}, u32[]{:S(2)}) collective-permute-start(f32[112,112]{1,0:T(8,128)} %get-tuple-element.197), channel_id=1, source_target_pairs={{0,1},{1,2},{2,3},{3,4},{4,5},{5,6},{6,7},{7,8},{8,9},{9,10},{10,1... | collective-permute-start | bytes 150536 | tf_op jit(solution)/shard_map/ppermute | solution.py:510
  102.8 2.4 %collective-permute-start.19 = (f32[1,112,256]{2,1,0:T(8,128)S(1)}, f32[1,112,256]{2,1,0:T(8,128)S(1)}, u32[]{:S(2)}, u32[]{:S(2)}) collective-permute-start(f32[1,112,256]{2,1,0:T(8,128)S(1)} %get-tuple-element.260), channel_id=1, source_target_pairs={{0,8},{1,9},{2,10},{3,11},{4,12},{5,13},{6,14},{7,15},{8,0},{9,1},... | collective-permute-start | bytes 344072 | tf_op jit(solution)/shard_map/ppermute | solution.py:229
  106.2 3.4 %shard_map.100 = (f32[8,112,256]{2,1,0:T(8,128)}, f32[112,256]{1,0:T(8,128)}, f32[8,256]{1,0:T(8,128)}, f32[256]{0:T(256)}) custom-call(f32[256,256]{1,0:T(8,128)} %get-tuple-element.203.inverse_ref, f32[8,256]{1,0:T(8,128)} %get-tuple-element.204.g1_ref, f32[8,112,256]{2,1,0:T(8,128)} %pad_maximum_fusion.held_ref), custom_call_target="tpu_custom_call" | custom-call | flops 1 | bytes 1 | tf_op jit(solution)/shard_map/pallas_call | solution.py:34
  112.2 2.1 %shard_map.101 = (f32[112,256]{1,0:T(8,128)}, f32[112,224]{1,0:T(8,128)}, f32[112,112]{1,0:T(8,128)}, f32[112,112]{1,0:T(8,128)}, f32[112,112]{1,0:T(8,128)}, /*...) custom-call(f32[112,384]{1,0:T(8,128)} %add_bitcast_fusion.13.refs_0_, ...), custom_call_target="tpu_custom_call" | custom-call | flops 1 | bytes 1 | tf_op jit(solution)/shard_map/pallas_call | solution.py:34
  116.1 4.3 %collective-permute-start.25 = (f32[112,112]{1,0:T(8,128)}, f32[112,112]{1,0:T(8,128)S(1)}, u32[]{:S(2)}, u32[]{:S(2)}) collective-permute-start(f32[112,112]{1,0:T(8,128)} %get-tuple-element.219), channel_id=1, source_target_pairs={{0,5},{1,6},{2,7},{3,8},{4,9},{5,10},{6,11},{7,12},{8,13},{9,14},{... | collective-permute-start | bytes 150536 | tf_op jit(solution)/shard_map/ppermute | solution.py:510
  120.4 2.3 %collective-permute-start.26 = (f32[112,112]{1,0:T(8,128)}, f32[112,112]{1,0:T(8,128)S(1)}, u32[]{:S(2)}, u32[]{:S(2)}) collective-permute-start(f32[112,112]{1,0:T(8,128)} %get-tuple-element.220), channel_id=1, source_target_pairs={{0,6},{1,7},{2,8},{3,9},{4,10},{5,11},{6,12},{7,13},{8,14},{9,15},... | collective-permute-start | bytes 150536 | tf_op jit(solution)/shard_map/ppermute | solution.py:510
  123.7 4.3 %shard_map.102.product_ref = f32[112,1792]{1,0:T(8,128)} custom-call(s32[1]{0:T(128)} %bitcast.me_ref, f32[8,112,256]{2,1,0:T(8,128)} %get-tuple-element.224.mine_ref, f32[8,112,256]{2,1,0:T(8,128)} %copy-done.4), custom_call_target="tpu_custom_call" | custom-call | flops 1 | bytes 1 | tf_op jit(solution)/shard_map/pallas_call | solution.py:34
  128.1 2.0 %collective-permute-done.26.refs_7_ = f32[112,112]{1,0:T(8,128)S(1)} collective-permute-done((f32[112,112]{1,0:T(8,128)}, f32[112,112]{1,0:T(8,128)S(1)}, u32[]{:S(2)}, u32[]{:S(2)}) %collective-permute-start.26) | collective-permute-done | bytes 50208 | tf_op jit(solution)/shard_map/ppermute | solution.py:510
  130.9 2.8 %shard_map.103 = (f32[112,1792]{1,0:T(8,128)}, f32[112]{0:T(128)}) custom-call(s32[1]{0:T(128)} %bitcast.me_ref, f32[16,128]{1,0:T(8,128)} %bitcast.53, f32[112,1792]{1,0:T(8,128)} %shard_map.102.product_ref, f32[8,112]{1,0:T(8,128)} %get-tuple-element.229.g2_ref, f32[8,256]{1,0:T(8,128)} %get-tuple-element.230.y_ref, ...), custom_call_target="tpu_custom_call" | custom-call | flops 1 | bytes 1 | tf_op jit(solution)/shard_map/pallas_call | solution.py:34
  (91 shorter events, 24.0 us)
Async XLA Ops:
  11.2 2.9 %collective-permute-start = (f32[9,112,256]{2,1,0:T(8,128)}, f32[9,112,256]{2,1,0:T(8,128)S(1)}, u32[]{:S(2)}, u32[]{:S(2)}) collective-permute-start(f32[9,112,256]{2,1,0:T(8,128)} %get-tuple-element.125), channel_id=1, source_target_pairs={{0,1},{1,0},{2,3},{3,2},{4,5},{5,4},{6,7},{7,6},{8,9},{9,8},{10,11... | collective-permute-start | bytes 3096584 | tf_op jit(solution)/shard_map/ppermute | solution.py:229
  17.7 15.6 %collective-permute-start.1 = (f32[5,112,256]{2,1,0:T(8,128)}, f32[5,112,256]{2,1,0:T(8,128)S(1)}, u32[]{:S(2)}, u32[]{:S(2)}) collective-permute-start(f32[5,112,256]{2,1,0:T(8,128)} %get-tuple-element.132), channel_id=1, source_target_pairs={{0,2},{1,3},{2,0},{3,1},{4,6},{5,7},{6,4},{7,5},{8,10},{9,11},{10,... | collective-permute-start | bytes 1720328 | tf_op jit(solution)/shard_map/ppermute | solution.py:229
  33.3 5.4 %collective-permute-start.3 = (f32[8,112,384]{2,1,0:T(8,128)}, f32[8,112,384]{2,1,0:T(8,128)S(1)}, u32[]{:S(2)}, u32[]{:S(2)}) collective-permute-start(f32[8,112,384]{2,1,0:T(8,128)} %get-tuple-element.148), channel_id=1, source_target_pairs={{0,1},{1,0},{2,3},{3,2},{4,5},{5,4},{6,7},{7,6},{8,9},{9,8},{10,11... | collective-permute-start | bytes 4128776 | tf_op jit(solution)/shard_map/ppermute | solution.py:229
  34.2 17.5 %collective-permute-start.6 = (f32[8,112,384]{2,1,0:T(8,128)}, f32[8,112,384]{2,1,0:T(8,128)}, u32[]{:S(2)}, u32[]{:S(2)}) collective-permute-start(f32[8,112,384]{2,1,0:T(8,128)} %get-tuple-element.157), channel_id=1, source_target_pairs={{0,1},{1,0},{2,3},{3,2},{4,5},{5,4},{6,7},{7,6},{8,9},{9,8},{10,11... | collective-permute-start | bytes 4128776 | tf_op jit(solution)/shard_map/ppermute | solution.py:229
  34.2 21.1 %collective-permute-start.5 = (f32[8,112,256]{2,1,0:T(8,128)}, f32[8,112,256]{2,1,0:T(8,128)}, u32[]{:S(2)}, u32[]{:S(2)}) collective-permute-start(f32[8,112,256]{2,1,0:T(8,128)} %get-tuple-element.156), channel_id=1, source_target_pairs={{0,1},{1,0},{2,3},{3,2},{4,5},{5,4},{6,7},{7,6},{8,9},{9,8},{10,11... | collective-permute-start | bytes 2752520 | tf_op jit(solution)/shard_map/ppermute | solution.py:229
  36.9 9.8 %collective-permute-start.2 = (f32[3,112,256]{2,1,0:T(8,128)}, f32[3,112,256]{2,1,0:T(8,128)S(1)}, u32[]{:S(2)}, u32[]{:S(2)}) collective-permute-start(f32[3,112,256]{2,1,0:T(8,128)} %get-tuple-element.147), channel_id=1, source_target_pairs={{0,4},{1,5},{2,6},{3,7},{4,0},{5,1},{6,2},{7,3},{8,12},{9,13},{10,... | collective-permute-start | bytes 1032200 | tf_op jit(solution)/shard_map/ppermute | solution.py:229
  39.9 11.8 %copy-start = (f32[8,112,384]{2,1,0:T(8,128)S(1)}, f32[8,112,384]{2,1,0:T(8,128)}, u32[]{:S(2)}) copy-start(f32[8,112,384]{2,1,0:T(8,128)} %get-tuple-element.158) | copy-start | bytes 4128772
  42.7 20.8 %collective-permute-start.8 = (f32[4,112,384]{2,1,0:T(8,128)}, f32[4,112,384]{2,1,0:T(8,128)}, u32[]{:S(2)}, u32[]{:S(2)}) collective-permute-start(f32[4,112,384]{2,1,0:T(8,128)} %get-tuple-element.246), channel_id=1, source_target_pairs={{0,2},{1,3},{2,0},{3,1},{4,6},{5,7},{6,4},{7,5},{8,10},{9,11},{10,... | collective-permute-start | bytes 2064392 | tf_op jit(solution)/shard_map/ppermute | solution.py:229
  49.3 12.5 %collective-permute-start.4 = (f32[2,112,256]{2,1,0:T(8,128)}, f32[2,112,256]{2,1,0:T(8,128)S(1)}, u32[]{:S(2)}, u32[]{:S(2)}) collective-permute-start(f32[2,112,256]{2,1,0:T(8,128)} %get-tuple-element.155), channel_id=1, source_target_pairs={{0,8},{1,9},{2,10},{3,11},{4,12},{5,13},{6,14},{7,15},{8,0},{9,1},... | collective-permute-start | bytes 688136 | tf_op jit(solution)/shard_map/ppermute | solution.py:229
  51.7 3.6 %copy-start.3 = (f32[8,112,256]{2,1,0:T(8,128)S(1)}, f32[8,112,256]{2,1,0:T(8,128)}, u32[]{:S(2)}) copy-start(f32[8,112,256]{2,1,0:T(8,128)} %get-tuple-element.160) | copy-start | bytes 2752516
  54.1 26.1 %collective-permute-start.9 = (f32[4,112,384]{2,1,0:T(8,128)}, f32[4,112,384]{2,1,0:T(8,128)S(1)}, u32[]{:S(2)}, u32[]{:S(2)}) collective-permute-start(f32[4,112,384]{2,1,0:T(8,128)} %get-tuple-element.244), channel_id=1, source_target_pairs={{0,2},{1,3},{2,0},{3,1},{4,6},{5,7},{6,4},{7,5},{8,10},{9,11},{10,... | collective-permute-start | bytes 2064392 | tf_op jit(solution)/shard_map/ppermute | solution.py:229
  55.4 6.4 %copy-start.8 = (f32[2,112,256]{2,1,0:T(8,128)S(1)}, f32[2,112,256]{2,1,0:T(8,128)}, u32[]{:S(2)}) copy-start(f32[2,112,256]{2,1,0:T(8,128)} %get-tuple-element.163) | copy-start | bytes 688132
  61.9 8.4 %copy-start.6 = (f32[1,112,256]{2,1,0:T(8,128)}, f32[1,112,256]{2,1,0:T(8,128)S(1)}, u32[]{:S(2)}) copy-start(f32[1,112,256]{2,1,0:T(8,128)S(1)} %get-tuple-element.168.mine_ref) | copy-start | bytes 344068
  61.9 8.4 %collective-permute-start.7 = (f32[1,112,256]{2,1,0:T(8,128)S(1)}, f32[1,112,256]{2,1,0:T(8,128)}, u32[]{:S(2)}, u32[]{:S(2)}) collective-permute-start(f32[1,112,256]{2,1,0:T(8,128)S(1)} %get-tuple-element.168.mine_ref), channel_id=1, source_target_pairs={{0,1},{1,0},{2,3},{3,2},{4,5},{5,4},{6,7},{7,6},{8,9},{9,8},{10,11... | collective-permute-start | bytes 344072 | tf_op jit(solution)/shard_map/ppermute | solution.py:229
  63.5 13.5 %collective-permute-start.11 = (f32[1,112,256]{2,1,0:T(8,128)S(1)}, f32[1,112,256]{2,1,0:T(8,128)}, u32[]{:S(2)}, u32[]{:S(2)}) collective-permute-start(f32[1,112,256]{2,1,0:T(8,128)S(1)} %get-tuple-element.176), channel_id=1, source_target_pairs={{0,8},{1,9},{2,10},{3,11},{4,12},{5,13},{6,14},{7,15},{8,0},{9,1},... | collective-permute-start | bytes 344072 | tf_op jit(solution)/shard_map/ppermute | solution.py:229
  65.4 13.7 %collective-permute-start.10 = (f32[2,112,384]{2,1,0:T(8,128)}, f32[2,112,384]{2,1,0:T(8,128)}, u32[]{:S(2)}, u32[]{:S(2)}) collective-permute-start(f32[2,112,384]{2,1,0:T(8,128)} %get-tuple-element.252), channel_id=1, source_target_pairs={{0,4},{1,5},{2,6},{3,7},{4,0},{5,1},{6,2},{7,3},{8,12},{9,13},{10,... | collective-permute-start | bytes 1032200 | tf_op jit(solution)/shard_map/ppermute | solution.py:229
  69.0 20.6 %collective-permute-start.14 = (f32[4,112,256]{2,1,0:T(8,128)S(1)}, f32[4,112,256]{2,1,0:T(8,128)S(1)}, u32[]{:S(2)}, u32[]{:S(2)}) collective-permute-start(f32[4,112,256]{2,1,0:T(8,128)S(1)} %get-tuple-element.248), channel_id=1, source_target_pairs={{0,2},{1,3},{2,0},{3,1},{4,6},{5,7},{6,4},{7,5},{8,10},{9,11},{10,... | collective-permute-start | bytes 1376264 | tf_op jit(solution)/shard_map/ppermute | solution.py:229
  78.0 10.1 %collective-permute-start.12 = (f32[2,112,256]{2,1,0:T(8,128)S(1)}, f32[2,112,256]{2,1,0:T(8,128)S(1)}, u32[]{:S(2)}, u32[]{:S(2)}) collective-permute-start(f32[2,112,256]{2,1,0:T(8,128)S(1)} %constant_dynamic-update-slice_fusion), channel_id=1, source_target_pairs={{0,4},{1,5},{2,6},{3,7},{4,0},{5,1},{6,2},{7,3},{8,12},{9,13},{10,... | collective-permute-start | bytes 688136 | tf_op jit(solution)/shard_map/ppermute | solution.py:229
  80.2 15.6 %collective-permute-start.16 = (f32[1,112,384]{2,1,0:T(8,128)S(1)}, f32[1,112,384]{2,1,0:T(8,128)S(1)}, u32[]{:S(2)}, u32[]{:S(2)}) collective-permute-start(f32[1,112,384]{2,1,0:T(8,128)S(1)} %get-tuple-element.258), channel_id=1, source_target_pairs={{0,8},{1,9},{2,10},{3,11},{4,12},{5,13},{6,14},{7,15},{8,0},{9,1},... | collective-permute-start | bytes 516104 | tf_op jit(solution)/shard_map/ppermute | solution.py:229
  80.3 15.0 %collective-permute-start.17 = (f32[2,112,384]{2,1,0:T(8,128)S(1)}, f32[2,112,384]{2,1,0:T(8,128)S(1)}, u32[]{:S(2)}, u32[]{:S(2)}) collective-permute-start(f32[2,112,384]{2,1,0:T(8,128)S(1)} %get-tuple-element.250), channel_id=1, source_target_pairs={{0,4},{1,5},{2,6},{3,7},{4,0},{5,1},{6,2},{7,3},{8,12},{9,13},{10,... | collective-permute-start | bytes 1032200 | tf_op jit(solution)/shard_map/ppermute | solution.py:229
  88.2 17.0 %collective-permute-start.13 = (f32[4,112,256]{2,1,0:T(8,128)S(1)}, f32[4,112,256]{2,1,0:T(8,128)S(1)}, u32[]{:S(2)}, u32[]{:S(2)}) collective-permute-start(f32[4,112,256]{2,1,0:T(8,128)S(1)} %constant_dynamic-update-slice_fusion.2), channel_id=1, source_target_pairs={{0,2},{1,3},{2,0},{3,1},{4,6},{5,7},{6,4},{7,5},{8,10},{9,11},{10,... | collective-permute-start | bytes 1376264 | tf_op jit(solution)/shard_map/ppermute | solution.py:229
  89.6 12.5 %collective-permute-start.15 = (f32[2,112,256]{2,1,0:T(8,128)S(1)}, f32[2,112,256]{2,1,0:T(8,128)S(1)}, u32[]{:S(2)}, u32[]{:S(2)}) collective-permute-start(f32[2,112,256]{2,1,0:T(8,128)S(1)} %get-tuple-element.253), channel_id=1, source_target_pairs={{0,4},{1,5},{2,6},{3,7},{4,0},{5,1},{6,2},{7,3},{8,12},{9,13},{10,... | collective-permute-start | bytes 688136 | tf_op jit(solution)/shard_map/ppermute | solution.py:229
  95.4 14.3 %collective-permute-start.18 = (f32[1,112,384]{2,1,0:T(8,128)S(1)}, f32[1,112,384]{2,1,0:T(8,128)S(1)}, u32[]{:S(2)}, u32[]{:S(2)}) collective-permute-start(f32[1,112,384]{2,1,0:T(8,128)S(1)} %get-tuple-element.256), channel_id=1, source_target_pairs={{0,8},{1,9},{2,10},{3,11},{4,12},{5,13},{6,14},{7,15},{8,0},{9,1},... | collective-permute-start | bytes 516104 | tf_op jit(solution)/shard_map/ppermute | solution.py:229
  98.2 12.8 %collective-permute-start.20 = (f32[112,112]{1,0:T(8,128)}, f32[112,112]{1,0:T(8,128)S(1)}, u32[]{:S(2)}, u32[]{:S(2)}) collective-permute-start(f32[112,112]{1,0:T(8,128)} %get-tuple-element.197), channel_id=1, source_target_pairs={{0,1},{1,2},{2,3},{3,4},{4,5},{5,6},{6,7},{7,8},{8,9},{9,10},{10,1... | collective-permute-start | bytes 150536 | tf_op jit(solution)/shard_map/ppermute | solution.py:510
  101.2 9.8 %collective-permute-start.21 = (f32[112,112]{1,0:T(8,128)}, f32[112,112]{1,0:T(8,128)S(1)}, u32[]{:S(2)}, u32[]{:S(2)}) collective-permute-start(f32[112,112]{1,0:T(8,128)} %get-tuple-element.198), channel_id=1, source_target_pairs={{0,2},{1,3},{2,4},{3,5},{4,6},{5,7},{6,8},{7,9},{8,10},{9,11},{10,... | collective-permute-start | bytes 150536 | tf_op jit(solution)/shard_map/ppermute | solution.py:510
  102.8 8.2 %collective-permute-start.19 = (f32[1,112,256]{2,1,0:T(8,128)S(1)}, f32[1,112,256]{2,1,0:T(8,128)S(1)}, u32[]{:S(2)}, u32[]{:S(2)}) collective-permute-start(f32[1,112,256]{2,1,0:T(8,128)S(1)} %get-tuple-element.260), channel_id=1, source_target_pairs={{0,8},{1,9},{2,10},{3,11},{4,12},{5,13},{6,14},{7,15},{8,0},{9,1},... | collective-permute-start | bytes 344072 | tf_op jit(solution)/shard_map/ppermute | solution.py:229
  114.3 8.4 %collective-permute-start.22 = (f32[8,112,256]{2,1,0:T(8,128)}, f32[8,112,256]{2,1,0:T(8,128)S(1)}, u32[]{:S(2)}, u32[]{:S(2)}) collective-permute-start(f32[8,112,256]{2,1,0:T(8,128)} %get-tuple-element.224.mine_ref), channel_id=1, source_target_pairs={{0,1},{1,0},{2,3},{3,2},{4,5},{5,4},{6,7},{7,6},{8,9},{9,8},{10,11... | collective-permute-start | bytes 2752520 | tf_op jit(solution)/shard_map/ppermute | solution.py:229
  115.7 12.4 %collective-permute-start.23 = (f32[112,112]{1,0:T(8,128)}, f32[112,112]{1,0:T(8,128)S(1)}, u32[]{:S(2)}, u32[]{:S(2)}) collective-permute-start(f32[112,112]{1,0:T(8,128)} %get-tuple-element.217), channel_id=1, source_target_pairs={{0,3},{1,4},{2,5},{3,6},{4,7},{5,8},{6,9},{7,10},{8,11},{9,12},{10... | collective-permute-start | bytes 150536 | tf_op jit(solution)/shard_map/ppermute | solution.py:510
  115.7 12.4 %collective-permute-start.24 = (f32[112,112]{1,0:T(8,128)}, f32[112,112]{1,0:T(8,128)S(1)}, u32[]{:S(2)}, u32[]{:S(2)}) collective-permute-start(f32[112,112]{1,0:T(8,128)} %get-tuple-element.218), channel_id=1, source_target_pairs={{0,4},{1,5},{2,6},{3,7},{4,8},{5,9},{6,10},{7,11},{8,12},{9,13},{1... | collective-permute-start | bytes 150536 | tf_op jit(solution)/shard_map/ppermute | solution.py:510
  116.1 12.0 %collective-permute-start.25 = (f32[112,112]{1,0:T(8,128)}, f32[112,112]{1,0:T(8,128)S(1)}, u32[]{:S(2)}, u32[]{:S(2)}) collective-permute-start(f32[112,112]{1,0:T(8,128)} %get-tuple-element.219), channel_id=1, source_target_pairs={{0,5},{1,6},{2,7},{3,8},{4,9},{5,10},{6,11},{7,12},{8,13},{9,14},{... | collective-permute-start | bytes 150536 | tf_op jit(solution)/shard_map/ppermute | solution.py:510
  120.4 9.6 %collective-permute-start.26 = (f32[112,112]{1,0:T(8,128)}, f32[112,112]{1,0:T(8,128)S(1)}, u32[]{:S(2)}, u32[]{:S(2)}) collective-permute-start(f32[112,112]{1,0:T(8,128)} %get-tuple-element.220), channel_id=1, source_target_pairs={{0,6},{1,7},{2,8},{3,9},{4,10},{5,11},{6,12},{7,13},{8,14},{9,15},... | collective-permute-start | bytes 150536 | tf_op jit(solution)/shard_map/ppermute | solution.py:510
  122.7 7.5 %collective-permute-start.27 = (f32[112,112]{1,0:T(8,128)}, f32[112,112]{1,0:T(8,128)S(1)}, u32[]{:S(2)}, u32[]{:S(2)}) collective-permute-start(f32[112,112]{1,0:T(8,128)} %get-tuple-element.221), channel_id=1, source_target_pairs={{0,7},{1,8},{2,9},{3,10},{4,11},{5,12},{6,13},{7,14},{8,15},{9,0},... | collective-permute-start | bytes 150536 | tf_op jit(solution)/shard_map/ppermute | solution.py:510
  (14 other events, 16.3 us)

commit v5 on v4

--- a/solution.py
+++ b/solution.py
@@ -475,9 +475,10 @@
     out = did(trailing(*then(me1, jt, r), orders, half, own, widths))
     t_sent, t = out[: len(widths)], list(out[len(widths) :])
     t_sent, p_got = lax.optimization_barrier((t_sent, p_got))
-    t_sent = list(t_sent)
-    t_got = [swap(x, axis, 0) for x in t_sent]
+    t_got = [swap(t_sent[0], axis, 0)]
     p, p_got = panel_fold(p, p_got, order[1])
+    t_sent = list(lax.optimization_barrier((t_sent, p))[0])
+    t_got += [swap(x, axis, 0) for x in t_sent[1:]]
     trail_step(0, 0)
     p, p_got = panel_fold(p, p_got, order[2])
     trail_step(1, 0)
@@ -497,10 +498,10 @@
     got = swap(held, axis, order[1])
     trail_step(0, 2)
     trail_step(1, 1)
-    factor, inverse = did(call(factor_second_kernel, then(*state), [f32(panel, panel)] * 2))
     held = joined(held, got)
     got = swap(held, axis, order[0])
     trail_step(2, 1)
+    factor, inverse = did(call(factor_second_kernel, then(*state), [f32(panel, panel)] * 2))
     trail_step(1, 2)
     first = trail_sum(0)
     near = widths[0] // own

time: 134 us -> 134 us (level)
  no operation moved by 1% of the time
where the time goes in v5:
time: 134 us
  Pallas kernels  55.8 us (42%)
  starting transfers between devices  34 us (25%)
  waiting for transfers between devices  22.9 us (17%)
  other arithmetic  12.8 us (10%)
  local copies, waits for them, and re-layouts  7.39 us (6%)
    pallas_call x10, Pallas kernels, call(): pl.pallas_call(kernel, out_shape=out_shape, in_specs=[SMEM_SPEC if x.dtyp...  34.1 us
    ppermute x21, starting transfers between devices, swap(): return lax.ppermute(x, axis, [(i, i ^ 1 << bit) for i in range(n)])  23.2 us
    ppermute x21, waiting for transfers between devices, swap(): return lax.ppermute(x, axis, [(i, i ^ 1 << bit) for i in range(n)])  20.7 us
    pallas_call x1, Pallas kernels, trailing(): pl.pallas_call(trail_kernel, grid=(half,), out_shape=[f32(half, own, wide...  11.2 us
    ppermute x7, starting transfers between devices, mirrored(): lax.ppermute(b, axis, [(i, (i + k) % n) for i in range(n)])  10.8 us
    pallas_call x1, Pallas kernels, front(): pl.pallas_call(functools.partial(front_kernel, order), out_shape=[f32(hal...  10.5 us
    add x9, other arithmetic, part(): lax.dynamic_index_in_dim(kept, which, 0, False)  10.3 us
    unnamed x38, local copies, waits for them, and re-layouts  5.69 us
  transfers between devices with their start and end apart: 28, of which 11 were waited for; matrix products, arithmetic and copies ran while one was open for 11% of the time, Pallas kernels for 28%

profile of v5, /device:TPU:1, one launch (start us, length us, event | category | flops | bytes accessed | tf_op | source)
XLA Modules:
  0.0 133.7 jit_solution(18004464738502870521)
XLA Ops:
  0.6 10.5 %shard_map.92 = (f32[9,112,256]{2,1,0:T(8,128)}, f32[9,112,256]{2,1,0:T(8,128)}, bf16[1792,768]{1,0:T(8,128)(2,1)}, bf16[16,768]{1,0:T(8,128)(2,1)}) custom-call(s32[1]{0:T(128)} %bitcast.me_ref, s32[4]{0:T(128)} %count_ref.1, s32[4,384]{1,0:T(4,128)} %offset_ref.1, bf16[4,384]{1,0:T(4,128)(2,1)} %resid_ref.1, bf16[1024,2048]{1,0:T(8,128)(2,1)} %bitcast.43), custom_call_target="tpu_custom_call" | custom-call | flops 1 | bytes 1 | tf_op jit(solution)/shard_map/pallas_call | solution.py:206
  11.3 2.8 %collective-permute-done.got_ref = f32[9,112,256]{2,1,0:T(8,128)S(1)} collective-permute-done((f32[9,112,256]{2,1,0:T(8,128)}, f32[9,112,256]{2,1,0:T(8,128)S(1)}, u32[]{:S(2)}, u32[]{:S(2)}) %collective-permute-start) | collective-permute-done | bytes 1032224 | tf_op jit(solution)/shard_map/ppermute | solution.py:229
  15.0 2.6 %shard_map.93 = (f32[5,112,256]{2,1,0:T(8,128)}, f32[5,112,256]{2,1,0:T(8,128)}) custom-call(s32[1]{0:T(128)} %bitcast.me_ref, f32[9,112,256]{2,1,0:T(8,128)} %get-tuple-element.131.kept_ref, f32[9,112,256]{2,1,0:T(8,128)} %copy-done.2), custom_call_target="tpu_custom_call" | custom-call | flops 1 | bytes 1 | tf_op jit(solution)/shard_map/pallas_call | solution.py:34
  17.7 2.4 %collective-permute-start.1 = (f32[5,112,256]{2,1,0:T(8,128)}, f32[5,112,256]{2,1,0:T(8,128)S(1)}, u32[]{:S(2)}, u32[]{:S(2)}) collective-permute-start(f32[5,112,256]{2,1,0:T(8,128)} %get-tuple-element.134), channel_id=1, source_target_pairs={{0,2},{1,3},{2,0},{3,1},{4,6},{5,7},{6,4},{7,5},{8,10},{9,11},{10,... | collective-permute-start | bytes 1720328 | tf_op jit(solution)/shard_map/ppermute | solution.py:229
  20.0 11.2 %shard_map.94 = (f32[8,112,384]{2,1,0:T(8,128)}, f32[8,112,384]{2,1,0:T(8,128)}, f32[8,112,256]{2,1,0:T(8,128)}, f32[8,112,384]{2,1,0:T(8,128)}, f32[8,112,384]{2,1,0:T(8,128)}, /*index=5*/f32[8,112,256]{2,1,0:T(8,128)}) custom-call(s32[1]{0:T(128)} %bitcast.me_ref, bf16[1792,768]{1,0:T(8,128)(2,1)} %get-tuple-element.136.jt_hbm, ...), custom_call_target="tpu_custom_call" | custom-call | flops 1 | bytes 1 | tf_op jit(solution)/shard_map/pallas_call | solution.py:184
  31.2 2.0 %collective-permute-done.1.got_ref = f32[5,112,256]{2,1,0:T(8,128)S(1)} collective-permute-done((f32[5,112,256]{2,1,0:T(8,128)}, f32[5,112,256]{2,1,0:T(8,128)S(1)}, u32[]{:S(2)}, u32[]{:S(2)}) %collective-permute-start.1) | collective-permute-done | bytes 573472 | tf_op jit(solution)/shard_map/ppermute | solution.py:229
  34.2 2.2 %shard_map.95 = (f32[3,112,256]{2,1,0:T(8,128)}, f32[3,112,256]{2,1,0:T(8,128)}) custom-call(s32[1]{0:T(128)} %bitcast.me_ref, f32[5,112,256]{2,1,0:T(8,128)} %get-tuple-element.146.kept_ref, f32[5,112,256]{2,1,0:T(8,128)} %copy-done.5), custom_call_target="tpu_custom_call" | custom-call | flops 1 | bytes 1 | tf_op jit(solution)/shard_map/pallas_call | solution.py:34
  37.2 1.5 %collective-permute-start.2 = (f32[3,112,256]{2,1,0:T(8,128)}, f32[3,112,256]{2,1,0:T(8,128)S(1)}, u32[]{:S(2)}, u32[]{:S(2)}) collective-permute-start(f32[3,112,256]{2,1,0:T(8,128)} %get-tuple-element.149), channel_id=1, source_target_pairs={{0,4},{1,5},{2,6},{3,7},{4,0},{5,1},{6,2},{7,3},{8,12},{9,13},{10,... | collective-permute-start | bytes 1032200 | tf_op jit(solution)/shard_map/ppermute | solution.py:229
  39.8 2.8 %add_bitcast_fusion.2 = (f32[4,112,384]{2,1,0:T(8,128)S(1)}, f32[4,112,384]{2,1,0:T(8,128)}) fusion(f32[2,4,112,384]{3,2,1,0:T(8,128)} %bitcast.49, s32[]{:T(128)S(6)} %select_n.55, f32[2,4,112,384]{3,2,1,0:T(8,128)} %bitcast.48, s32[]{:T(128)S(6)} %select_n.54), kind=kLoop, calls=%fused_computation.3 | loop fusion | flops 344064 | bytes 4128776 | tf_op jit(solution)/shard_map/add | solution.py:250
  43.8 2.8 %collective-permute-done.2.got_ref = f32[3,112,256]{2,1,0:T(8,128)S(1)} collective-permute-done((f32[3,112,256]{2,1,0:T(8,128)}, f32[3,112,256]{2,1,0:T(8,128)S(1)}, u32[]{:S(2)}, u32[]{:S(2)}) %collective-permute-start.2) | collective-permute-done | bytes 344096 | tf_op jit(solution)/shard_map/ppermute | solution.py:229
  47.4 1.9 %shard_map.96 = (f32[2,112,256]{2,1,0:T(8,128)}, f32[2,112,256]{2,1,0:T(8,128)}) custom-call(s32[1]{0:T(128)} %bitcast.me_ref, f32[3,112,256]{2,1,0:T(8,128)} %get-tuple-element.154.kept_ref, f32[3,112,256]{2,1,0:T(8,128)} %copy-done.7), custom_call_target="tpu_custom_call" | custom-call | flops 1 | bytes 1 | tf_op jit(solution)/shard_map/pallas_call | solution.py:34
  49.3 2.4 %collective-permute-start.4 = (f32[2,112,256]{2,1,0:T(8,128)}, f32[2,112,256]{2,1,0:T(8,128)S(1)}, u32[]{:S(2)}, u32[]{:S(2)}) collective-permute-start(f32[2,112,256]{2,1,0:T(8,128)} %get-tuple-element.157), channel_id=1, source_target_pairs={{0,8},{1,9},{2,10},{3,11},{4,12},{5,13},{6,14},{7,15},{8,0},{9,1},... | collective-permute-start | bytes 688136 | tf_op jit(solution)/shard_map/ppermute | solution.py:229
  51.7 2.4 %add_bitcast_fusion = (f32[4,112,384]{2,1,0:T(8,128)S(1)}, f32[4,112,384]{2,1,0:T(8,128)}) fusion(f32[2,4,112,384]{3,2,1,0:T(8,128)} %bitcast.7, s32[]{:T(128)S(6)} %select_n.55, f32[2,4,112,384]{3,2,1,0:T(8,128)S(1)} %bitcast.47, s32[]{:T(128)S(6)} %select_n.54), kind=kLoop, calls=%fused_computation.1 | loop fusion | flops 344064 | bytes 4128776 | tf_op jit(solution)/shard_map/add | solution.py:250
  57.4 4.2 %collective-permute-done.4 = f32[2,112,256]{2,1,0:T(8,128)S(1)} collective-permute-done((f32[2,112,256]{2,1,0:T(8,128)}, f32[2,112,256]{2,1,0:T(8,128)S(1)}, u32[]{:S(2)}, u32[]{:S(2)}) %collective-permute-start.4) | collective-permute-done | bytes 229408 | tf_op jit(solution)/shard_map/ppermute | solution.py:229
  61.7 1.8 %collective-permute-start.7 = (f32[1,112,256]{2,1,0:T(8,128)S(1)}, f32[1,112,256]{2,1,0:T(8,128)}, u32[]{:S(2)}, u32[]{:S(2)}) collective-permute-start(f32[1,112,256]{2,1,0:T(8,128)S(1)} %get-tuple-element.172.mine_ref), channel_id=1, source_target_pairs={{0,1},{1,0},{2,3},{3,2},{4,5},{5,4},{6,7},{7,6},{8,9},{9,8},{10,11... | collective-permute-start | bytes 344072 | tf_op jit(solution)/shard_map/ppermute | solution.py:229
  63.5 1.9 %add_bitcast_fusion.8 = (f32[2,112,384]{2,1,0:T(8,128)S(1)}, f32[2,112,384]{2,1,0:T(8,128)}) fusion(f32[2,2,112,384]{3,2,1,0:T(8,128)} %bitcast.15, s32[]{:T(128)S(6)} %select_n.57, f32[2,2,112,384]{3,2,1,0:T(8,128)S(1)} %bitcast.45, s32[]{:T(128)S(6)} %select_n.56), kind=kLoop, calls=%fused_computation.9 | loop fusion | flops 172032 | bytes 2064392 | tf_op jit(solution)/shard_map/add | solution.py:250
  65.4 3.6 %collective-permute-start.13 = (f32[2,112,384]{2,1,0:T(8,128)}, f32[2,112,384]{2,1,0:T(8,128)}, u32[]{:S(2)}, u32[]{:S(2)}) collective-permute-start(f32[2,112,384]{2,1,0:T(8,128)} %get-tuple-element.256), channel_id=1, source_target_pairs={{0,4},{1,5},{2,6},{3,7},{4,0},{5,1},{6,2},{7,3},{8,12},{9,13},{10,... | collective-permute-start | bytes 1032200 | tf_op jit(solution)/shard_map/ppermute | solution.py:229
  70.2 6.9 %shard_map.97 = (f32[8,256]{1,0:T(8,128)}, f32[128,128]{1,0:T(8,128)}, f32[128,128]{1,0:T(8,128)}, f32[128,128]{1,0:T(8,128)}, f32[128,128]{1,0:T(8,128)}) custom-call(s32[1]{0:T(128)} %bitcast.me_ref, f32[1,112,256]{2,1,0:T(8,128)} %copy-done.6, f32[1,112,256]{2,1,0:T(8,128)} %collective-permute-done.7.other_ref, f32[256,8]{1,0:T(8,128)} %reshape.128.damp_ref), custom_call_target="tpu_custom_call" | custom-call | flops 1 | bytes 1 | tf_op jit(solution)/shard_map/pallas_call | solution.py:34
  80.3 1.6 %collective-permute-start.17 = (f32[2,112,384]{2,1,0:T(8,128)S(1)}, f32[2,112,384]{2,1,0:T(8,128)S(1)}, u32[]{:S(2)}, u32[]{:S(2)}) collective-permute-start(f32[2,112,384]{2,1,0:T(8,128)S(1)} %get-tuple-element.254), channel_id=1, source_target_pairs={{0,4},{1,5},{2,6},{3,7},{4,0},{5,1},{6,2},{7,3},{8,12},{9,13},{10,... | collective-permute-start | bytes 1032200 | tf_op jit(solution)/shard_map/ppermute | solution.py:229
  81.9 3.3 %collective-permute-done.11 = f32[2,112,256]{2,1,0:T(8,128)S(1)} collective-permute-done((f32[2,112,256]{2,1,0:T(8,128)S(1)}, f32[2,112,256]{2,1,0:T(8,128)S(1)}, u32[]{:S(2)}, u32[]{:S(2)}) %collective-permute-start.11) | collective-permute-done | bytes 229408 | tf_op jit(solution)/shard_map/ppermute | solution.py:229
  85.5 6.2 %shard_map.98 = (f32[256,256]{1,0:T(8,128)}, f32[256,256]{1,0:T(8,128)}) custom-call(f32[128,128]{1,0:T(8,128)} %get-tuple-element.190.l11_ref, f32[128,128]{1,0:T(8,128)} %get-tuple-element.191.i11_ref, f32[128,128]{1,0:T(8,128)} %get-tuple-element.192.l21_ref, f32[128,128]{1,0:T(8,128)} %get-tuple-element.193.rest_ref), custom_call_target="tpu_custom_call" | custom-call | flops 1 | bytes 1 | tf_op jit(solution)/shard_map/pallas_call | solution.py:34
  91.7 3.6 %collective-permute-done.17 = f32[2,112,384]{2,1,0:T(8,128)S(1)} collective-permute-done((f32[2,112,384]{2,1,0:T(8,128)S(1)}, f32[2,112,384]{2,1,0:T(8,128)S(1)}, u32[]{:S(2)}, u32[]{:S(2)}) %collective-permute-start.17) | collective-permute-done | bytes 344096 | tf_op jit(solution)/shard_map/ppermute | solution.py:229
  96.5 1.7 %shard_map.99 = (f32[112,112]{1,0:T(8,128)}, f32[112,112]{1,0:T(8,128)}) custom-call(f32[112,384]{1,0:T(8,128)} %add_bitcast_fusion.13.refs_0_), custom_call_target="tpu_custom_call" | custom-call | flops 1 | bytes 1 | tf_op jit(solution)/shard_map/pallas_call | solution.py:34
  98.2 3.0 %collective-permute-start.20 = (f32[112,112]{1,0:T(8,128)}, f32[112,112]{1,0:T(8,128)S(1)}, u32[]{:S(2)}, u32[]{:S(2)}) collective-permute-start(f32[112,112]{1,0:T(8,128)} %get-tuple-element.201), channel_id=1, source_target_pairs={{0,1},{1,2},{2,3},{3,4},{4,5},{5,6},{6,7},{7,8},{8,9},{9,10},{10,1... | collective-permute-start | bytes 150536 | tf_op jit(solution)/shard_map/ppermute | solution.py:511
  102.8 2.4 %collective-permute-start.19 = (f32[1,112,256]{2,1,0:T(8,128)S(1)}, f32[1,112,256]{2,1,0:T(8,128)S(1)}, u32[]{:S(2)}, u32[]{:S(2)}) collective-permute-start(f32[1,112,256]{2,1,0:T(8,128)S(1)} %get-tuple-element.264), channel_id=1, source_target_pairs={{0,8},{1,9},{2,10},{3,11},{4,12},{5,13},{6,14},{7,15},{8,0},{9,1},... | collective-permute-start | bytes 344072 | tf_op jit(solution)/shard_map/ppermute | solution.py:229
  106.2 3.4 %shard_map.100 = (f32[8,112,256]{2,1,0:T(8,128)}, f32[112,256]{1,0:T(8,128)}, f32[8,256]{1,0:T(8,128)}, f32[256]{0:T(256)}) custom-call(f32[256,256]{1,0:T(8,128)} %get-tuple-element.207.inverse_ref, f32[8,256]{1,0:T(8,128)} %get-tuple-element.208.g1_ref, f32[8,112,256]{2,1,0:T(8,128)} %pad_maximum_fusion.held_ref), custom_call_target="tpu_custom_call" | custom-call | flops 1 | bytes 1 | tf_op jit(solution)/shard_map/pallas_call | solution.py:34
  112.2 2.1 %shard_map.101 = (f32[112,256]{1,0:T(8,128)}, f32[112,224]{1,0:T(8,128)}, f32[112,112]{1,0:T(8,128)}, f32[112,112]{1,0:T(8,128)}, f32[112,112]{1,0:T(8,128)}, /*...) custom-call(f32[112,384]{1,0:T(8,128)} %add_bitcast_fusion.13.refs_0_, ...), custom_call_target="tpu_custom_call" | custom-call | flops 1 | bytes 1 | tf_op jit(solution)/shard_map/pallas_call | solution.py:34
  116.0 4.4 %collective-permute-start.25 = (f32[112,112]{1,0:T(8,128)}, f32[112,112]{1,0:T(8,128)S(1)}, u32[]{:S(2)}, u32[]{:S(2)}) collective-permute-start(f32[112,112]{1,0:T(8,128)} %get-tuple-element.223), channel_id=1, source_target_pairs={{0,5},{1,6},{2,7},{3,8},{4,9},{5,10},{6,11},{7,12},{8,13},{9,14},{... | collective-permute-start | bytes 150536 | tf_op jit(solution)/shard_map/ppermute | solution.py:511
  120.4 2.3 %collective-permute-start.26 = (f32[112,112]{1,0:T(8,128)}, f32[112,112]{1,0:T(8,128)S(1)}, u32[]{:S(2)}, u32[]{:S(2)}) collective-permute-start(f32[112,112]{1,0:T(8,128)} %get-tuple-element.224), channel_id=1, source_target_pairs={{0,6},{1,7},{2,8},{3,9},{4,10},{5,11},{6,12},{7,13},{8,14},{9,15},... | collective-permute-start | bytes 150536 | tf_op jit(solution)/shard_map/ppermute | solution.py:511
  123.6 4.3 %shard_map.102.product_ref = f32[112,1792]{1,0:T(8,128)} custom-call(s32[1]{0:T(128)} %bitcast.me_ref, f32[8,112,256]{2,1,0:T(8,128)} %get-tuple-element.228.mine_ref, f32[8,112,256]{2,1,0:T(8,128)} %copy-done.4), custom_call_target="tpu_custom_call" | custom-call | flops 1 | bytes 1 | tf_op jit(solution)/shard_map/pallas_call | solution.py:34
  128.0 2.0 %collective-permute-done.26.refs_7_ = f32[112,112]{1,0:T(8,128)S(1)} collective-permute-done((f32[112,112]{1,0:T(8,128)}, f32[112,112]{1,0:T(8,128)S(1)}, u32[]{:S(2)}, u32[]{:S(2)}) %collective-permute-start.26) | collective-permute-done | bytes 50208 | tf_op jit(solution)/shard_map/ppermute | solution.py:511
  130.9 2.8 %shard_map.103 = (f32[112,1792]{1,0:T(8,128)}, f32[112]{0:T(128)}) custom-call(s32[1]{0:T(128)} %bitcast.me_ref, f32[16,128]{1,0:T(8,128)} %bitcast.53, f32[112,1792]{1,0:T(8,128)} %shard_map.102.product_ref, f32[8,112]{1,0:T(8,128)} %get-tuple-element.233.g2_ref, f32[8,256]{1,0:T(8,128)} %get-tuple-element.234.y_ref, ...), custom_call_target="tpu_custom_call" | custom-call | flops 1 | bytes 1 | tf_op jit(solution)/shard_map/pallas_call | solution.py:34
  (91 shorter events, 23.8 us)
Async XLA Ops:
  11.1 2.9 %collective-permute-start = (f32[9,112,256]{2,1,0:T(8,128)}, f32[9,112,256]{2,1,0:T(8,128)S(1)}, u32[]{:S(2)}, u32[]{:S(2)}) collective-permute-start(f32[9,112,256]{2,1,0:T(8,128)} %get-tuple-element.127), channel_id=1, source_target_pairs={{0,1},{1,0},{2,3},{3,2},{4,5},{5,4},{6,7},{7,6},{8,9},{9,8},{10,11... | collective-permute-start | bytes 3096584 | tf_op jit(solution)/shard_map/ppermute | solution.py:229
  17.7 15.6 %collective-permute-start.1 = (f32[5,112,256]{2,1,0:T(8,128)}, f32[5,112,256]{2,1,0:T(8,128)S(1)}, u32[]{:S(2)}, u32[]{:S(2)}) collective-permute-start(f32[5,112,256]{2,1,0:T(8,128)} %get-tuple-element.134), channel_id=1, source_target_pairs={{0,2},{1,3},{2,0},{3,1},{4,6},{5,7},{6,4},{7,5},{8,10},{9,11},{10,... | collective-permute-start | bytes 1720328 | tf_op jit(solution)/shard_map/ppermute | solution.py:229
  33.3 5.4 %collective-permute-start.3 = (f32[8,112,384]{2,1,0:T(8,128)}, f32[8,112,384]{2,1,0:T(8,128)S(1)}, u32[]{:S(2)}, u32[]{:S(2)}) collective-permute-start(f32[8,112,384]{2,1,0:T(8,128)} %get-tuple-element.150), channel_id=1, source_target_pairs={{0,1},{1,0},{2,3},{3,2},{4,5},{5,4},{6,7},{7,6},{8,9},{9,8},{10,11... | collective-permute-start | bytes 4128776 | tf_op jit(solution)/shard_map/ppermute | solution.py:229
  36.4 15.3 %collective-permute-start.6 = (f32[8,112,384]{2,1,0:T(8,128)}, f32[8,112,384]{2,1,0:T(8,128)}, u32[]{:S(2)}, u32[]{:S(2)}) collective-permute-start(f32[8,112,384]{2,1,0:T(8,128)} %get-tuple-element.161), channel_id=1, source_target_pairs={{0,1},{1,0},{2,3},{3,2},{4,5},{5,4},{6,7},{7,6},{8,9},{9,8},{10,11... | collective-permute-start | bytes 4128776 | tf_op jit(solution)/shard_map/ppermute | solution.py:229
  37.2 18.2 %collective-permute-start.5 = (f32[8,112,256]{2,1,0:T(8,128)}, f32[8,112,256]{2,1,0:T(8,128)}, u32[]{:S(2)}, u32[]{:S(2)}) collective-permute-start(f32[8,112,256]{2,1,0:T(8,128)} %get-tuple-element.160), channel_id=1, source_target_pairs={{0,1},{1,0},{2,3},{3,2},{4,5},{5,4},{6,7},{7,6},{8,9},{9,8},{10,11... | collective-permute-start | bytes 2752520 | tf_op jit(solution)/shard_map/ppermute | solution.py:229
  37.2 9.5 %collective-permute-start.2 = (f32[3,112,256]{2,1,0:T(8,128)}, f32[3,112,256]{2,1,0:T(8,128)S(1)}, u32[]{:S(2)}, u32[]{:S(2)}) collective-permute-start(f32[3,112,256]{2,1,0:T(8,128)} %get-tuple-element.149), channel_id=1, source_target_pairs={{0,4},{1,5},{2,6},{3,7},{4,0},{5,1},{6,2},{7,3},{8,12},{9,13},{10,... | collective-permute-start | bytes 1032200 | tf_op jit(solution)/shard_map/ppermute | solution.py:229
  39.8 11.9 %copy-start = (f32[8,112,384]{2,1,0:T(8,128)S(1)}, f32[8,112,384]{2,1,0:T(8,128)}, u32[]{:S(2)}) copy-start(f32[8,112,384]{2,1,0:T(8,128)} %get-tuple-element.162) | copy-start | bytes 4128772
  42.6 20.9 %collective-permute-start.8 = (f32[4,112,384]{2,1,0:T(8,128)}, f32[4,112,384]{2,1,0:T(8,128)}, u32[]{:S(2)}, u32[]{:S(2)}) collective-permute-start(f32[4,112,384]{2,1,0:T(8,128)} %get-tuple-element.250), channel_id=1, source_target_pairs={{0,2},{1,3},{2,0},{3,1},{4,6},{5,7},{6,4},{7,5},{8,10},{9,11},{10,... | collective-permute-start | bytes 2064392 | tf_op jit(solution)/shard_map/ppermute | solution.py:229
  49.3 12.4 %collective-permute-start.4 = (f32[2,112,256]{2,1,0:T(8,128)}, f32[2,112,256]{2,1,0:T(8,128)S(1)}, u32[]{:S(2)}, u32[]{:S(2)}) collective-permute-start(f32[2,112,256]{2,1,0:T(8,128)} %get-tuple-element.157), channel_id=1, source_target_pairs={{0,8},{1,9},{2,10},{3,11},{4,12},{5,13},{6,14},{7,15},{8,0},{9,1},... | collective-permute-start | bytes 688136 | tf_op jit(solution)/shard_map/ppermute | solution.py:229
  51.7 3.6 %copy-start.3 = (f32[8,112,256]{2,1,0:T(8,128)S(1)}, f32[8,112,256]{2,1,0:T(8,128)}, u32[]{:S(2)}) copy-start(f32[8,112,256]{2,1,0:T(8,128)} %get-tuple-element.164) | copy-start | bytes 2752516
  54.1 26.1 %collective-permute-start.12 = (f32[4,112,384]{2,1,0:T(8,128)}, f32[4,112,384]{2,1,0:T(8,128)S(1)}, u32[]{:S(2)}, u32[]{:S(2)}) collective-permute-start(f32[4,112,384]{2,1,0:T(8,128)} %get-tuple-element.248), channel_id=1, source_target_pairs={{0,2},{1,3},{2,0},{3,1},{4,6},{5,7},{6,4},{7,5},{8,10},{9,11},{10,... | collective-permute-start | bytes 2064392 | tf_op jit(solution)/shard_map/ppermute | solution.py:229
  55.3 6.3 %copy-start.8 = (f32[2,112,256]{2,1,0:T(8,128)S(1)}, f32[2,112,256]{2,1,0:T(8,128)}, u32[]{:S(2)}) copy-start(f32[2,112,256]{2,1,0:T(8,128)} %get-tuple-element.167) | copy-start | bytes 688132
  61.7 8.5 %copy-start.6 = (f32[1,112,256]{2,1,0:T(8,128)}, f32[1,112,256]{2,1,0:T(8,128)S(1)}, u32[]{:S(2)}) copy-start(f32[1,112,256]{2,1,0:T(8,128)S(1)} %get-tuple-element.172.mine_ref) | copy-start | bytes 344068
  61.7 8.5 %collective-permute-start.7 = (f32[1,112,256]{2,1,0:T(8,128)S(1)}, f32[1,112,256]{2,1,0:T(8,128)}, u32[]{:S(2)}, u32[]{:S(2)}) collective-permute-start(f32[1,112,256]{2,1,0:T(8,128)S(1)} %get-tuple-element.172.mine_ref), channel_id=1, source_target_pairs={{0,1},{1,0},{2,3},{3,2},{4,5},{5,4},{6,7},{7,6},{8,9},{9,8},{10,11... | collective-permute-start | bytes 344072 | tf_op jit(solution)/shard_map/ppermute | solution.py:229
  63.5 13.6 %collective-permute-start.10 = (f32[1,112,256]{2,1,0:T(8,128)S(1)}, f32[1,112,256]{2,1,0:T(8,128)}, u32[]{:S(2)}, u32[]{:S(2)}) collective-permute-start(f32[1,112,256]{2,1,0:T(8,128)S(1)} %get-tuple-element.180), channel_id=1, source_target_pairs={{0,8},{1,9},{2,10},{3,11},{4,12},{5,13},{6,14},{7,15},{8,0},{9,1},... | collective-permute-start | bytes 344072 | tf_op jit(solution)/shard_map/ppermute | solution.py:229
  65.4 13.7 %collective-permute-start.13 = (f32[2,112,384]{2,1,0:T(8,128)}, f32[2,112,384]{2,1,0:T(8,128)}, u32[]{:S(2)}, u32[]{:S(2)}) collective-permute-start(f32[2,112,384]{2,1,0:T(8,128)} %get-tuple-element.256), channel_id=1, source_target_pairs={{0,4},{1,5},{2,6},{3,7},{4,0},{5,1},{6,2},{7,3},{8,12},{9,13},{10,... | collective-permute-start | bytes 1032200 | tf_op jit(solution)/shard_map/ppermute | solution.py:229
  69.0 16.3 %collective-permute-start.9 = (f32[4,112,256]{2,1,0:T(8,128)S(1)}, f32[4,112,256]{2,1,0:T(8,128)S(1)}, u32[]{:S(2)}, u32[]{:S(2)}) collective-permute-start(f32[4,112,256]{2,1,0:T(8,128)S(1)} %get-tuple-element.252), channel_id=1, source_target_pairs={{0,2},{1,3},{2,0},{3,1},{4,6},{5,7},{6,4},{7,5},{8,10},{9,11},{10,... | collective-permute-start | bytes 1376264 | tf_op jit(solution)/shard_map/ppermute | solution.py:229
  78.0 7.2 %collective-permute-start.11 = (f32[2,112,256]{2,1,0:T(8,128)S(1)}, f32[2,112,256]{2,1,0:T(8,128)S(1)}, u32[]{:S(2)}, u32[]{:S(2)}) collective-permute-start(f32[2,112,256]{2,1,0:T(8,128)S(1)} %constant_dynamic-update-slice_fusion), channel_id=1, source_target_pairs={{0,4},{1,5},{2,6},{3,7},{4,0},{5,1},{6,2},{7,3},{8,12},{9,13},{10,... | collective-permute-start | bytes 688136 | tf_op jit(solution)/shard_map/ppermute | solution.py:229
  80.1 15.7 %collective-permute-start.16 = (f32[1,112,384]{2,1,0:T(8,128)S(1)}, f32[1,112,384]{2,1,0:T(8,128)S(1)}, u32[]{:S(2)}, u32[]{:S(2)}) collective-permute-start(f32[1,112,384]{2,1,0:T(8,128)S(1)} %get-tuple-element.262), channel_id=1, source_target_pairs={{0,8},{1,9},{2,10},{3,11},{4,12},{5,13},{6,14},{7,15},{8,0},{9,1},... | collective-permute-start | bytes 516104 | tf_op jit(solution)/shard_map/ppermute | solution.py:229
  80.3 15.0 %collective-permute-start.17 = (f32[2,112,384]{2,1,0:T(8,128)S(1)}, f32[2,112,384]{2,1,0:T(8,128)S(1)}, u32[]{:S(2)}, u32[]{:S(2)}) collective-permute-start(f32[2,112,384]{2,1,0:T(8,128)S(1)} %get-tuple-element.254), channel_id=1, source_target_pairs={{0,4},{1,5},{2,6},{3,7},{4,0},{5,1},{6,2},{7,3},{8,12},{9,13},{10,... | collective-permute-start | bytes 1032200 | tf_op jit(solution)/shard_map/ppermute | solution.py:229
  85.2 20.0 %collective-permute-start.14 = (f32[4,112,256]{2,1,0:T(8,128)S(1)}, f32[4,112,256]{2,1,0:T(8,128)S(1)}, u32[]{:S(2)}, u32[]{:S(2)}) collective-permute-start(f32[4,112,256]{2,1,0:T(8,128)S(1)} %constant_dynamic-update-slice_fusion.2), channel_id=1, source_target_pairs={{0,2},{1,3},{2,0},{3,1},{4,6},{5,7},{6,4},{7,5},{8,10},{9,11},{10,... | collective-permute-start | bytes 1376264 | tf_op jit(solution)/shard_map/ppermute | solution.py:229
  85.4 16.7 %collective-permute-start.15 = (f32[2,112,256]{2,1,0:T(8,128)S(1)}, f32[2,112,256]{2,1,0:T(8,128)S(1)}, u32[]{:S(2)}, u32[]{:S(2)}) collective-permute-start(f32[2,112,256]{2,1,0:T(8,128)S(1)} %get-tuple-element.258), channel_id=1, source_target_pairs={{0,4},{1,5},{2,6},{3,7},{4,0},{5,1},{6,2},{7,3},{8,12},{9,13},{10,... | collective-permute-start | bytes 688136 | tf_op jit(solution)/shard_map/ppermute | solution.py:229
  95.4 14.2 %collective-permute-start.18 = (f32[1,112,384]{2,1,0:T(8,128)S(1)}, f32[1,112,384]{2,1,0:T(8,128)S(1)}, u32[]{:S(2)}, u32[]{:S(2)}) collective-permute-start(f32[1,112,384]{2,1,0:T(8,128)S(1)} %get-tuple-element.260), channel_id=1, source_target_pairs={{0,8},{1,9},{2,10},{3,11},{4,12},{5,13},{6,14},{7,15},{8,0},{9,1},... | collective-permute-start | bytes 516104 | tf_op jit(solution)/shard_map/ppermute | solution.py:229
  98.2 12.7 %collective-permute-start.20 = (f32[112,112]{1,0:T(8,128)}, f32[112,112]{1,0:T(8,128)S(1)}, u32[]{:S(2)}, u32[]{:S(2)}) collective-permute-start(f32[112,112]{1,0:T(8,128)} %get-tuple-element.201), channel_id=1, source_target_pairs={{0,1},{1,2},{2,3},{3,4},{4,5},{5,6},{6,7},{7,8},{8,9},{9,10},{10,1... | collective-permute-start | bytes 150536 | tf_op jit(solution)/shard_map/ppermute | solution.py:511
  101.2 9.7 %collective-permute-start.21 = (f32[112,112]{1,0:T(8,128)}, f32[112,112]{1,0:T(8,128)S(1)}, u32[]{:S(2)}, u32[]{:S(2)}) collective-permute-start(f32[112,112]{1,0:T(8,128)} %get-tuple-element.202), channel_id=1, source_target_pairs={{0,2},{1,3},{2,4},{3,5},{4,6},{5,7},{6,8},{7,9},{8,10},{9,11},{10,... | collective-permute-start | bytes 150536 | tf_op jit(solution)/shard_map/ppermute | solution.py:511
  102.8 8.2 %collective-permute-start.19 = (f32[1,112,256]{2,1,0:T(8,128)S(1)}, f32[1,112,256]{2,1,0:T(8,128)S(1)}, u32[]{:S(2)}, u32[]{:S(2)}) collective-permute-start(f32[1,112,256]{2,1,0:T(8,128)S(1)} %get-tuple-element.264), channel_id=1, source_target_pairs={{0,8},{1,9},{2,10},{3,11},{4,12},{5,13},{6,14},{7,15},{8,0},{9,1},... | collective-permute-start | bytes 344072 | tf_op jit(solution)/shard_map/ppermute | solution.py:229
  114.3 8.4 %collective-permute-start.22 = (f32[8,112,256]{2,1,0:T(8,128)}, f32[8,112,256]{2,1,0:T(8,128)S(1)}, u32[]{:S(2)}, u32[]{:S(2)}) collective-permute-start(f32[8,112,256]{2,1,0:T(8,128)} %get-tuple-element.228.mine_ref), channel_id=1, source_target_pairs={{0,1},{1,0},{2,3},{3,2},{4,5},{5,4},{6,7},{7,6},{8,9},{9,8},{10,11... | collective-permute-start | bytes 2752520 | tf_op jit(solution)/shard_map/ppermute | solution.py:229
  115.6 12.3 %collective-permute-start.23 = (f32[112,112]{1,0:T(8,128)}, f32[112,112]{1,0:T(8,128)S(1)}, u32[]{:S(2)}, u32[]{:S(2)}) collective-permute-start(f32[112,112]{1,0:T(8,128)} %get-tuple-element.221), channel_id=1, source_target_pairs={{0,3},{1,4},{2,5},{3,6},{4,7},{5,8},{6,9},{7,10},{8,11},{9,12},{10... | collective-permute-start | bytes 150536 | tf_op jit(solution)/shard_map/ppermute | solution.py:511
  115.6 12.3 %collective-permute-start.24 = (f32[112,112]{1,0:T(8,128)}, f32[112,112]{1,0:T(8,128)S(1)}, u32[]{:S(2)}, u32[]{:S(2)}) collective-permute-start(f32[112,112]{1,0:T(8,128)} %get-tuple-element.222), channel_id=1, source_target_pairs={{0,4},{1,5},{2,6},{3,7},{4,8},{5,9},{6,10},{7,11},{8,12},{9,13},{1... | collective-permute-start | bytes 150536 | tf_op jit(solution)/shard_map/ppermute | solution.py:511
  116.0 12.0 %collective-permute-start.25 = (f32[112,112]{1,0:T(8,128)}, f32[112,112]{1,0:T(8,128)S(1)}, u32[]{:S(2)}, u32[]{:S(2)}) collective-permute-start(f32[112,112]{1,0:T(8,128)} %get-tuple-element.223), channel_id=1, source_target_pairs={{0,5},{1,6},{2,7},{3,8},{4,9},{5,10},{6,11},{7,12},{8,13},{9,14},{... | collective-permute-start | bytes 150536 | tf_op jit(solution)/shard_map/ppermute | solution.py:511
  120.4 9.6 %collective-permute-start.26 = (f32[112,112]{1,0:T(8,128)}, f32[112,112]{1,0:T(8,128)S(1)}, u32[]{:S(2)}, u32[]{:S(2)}) collective-permute-start(f32[112,112]{1,0:T(8,128)} %get-tuple-element.224), channel_id=1, source_target_pairs={{0,6},{1,7},{2,8},{3,9},{4,10},{5,11},{6,12},{7,13},{8,14},{9,15},... | collective-permute-start | bytes 150536 | tf_op jit(solution)/shard_map/ppermute | solution.py:511
  122.7 7.5 %collective-permute-start.27 = (f32[112,112]{1,0:T(8,128)}, f32[112,112]{1,0:T(8,128)S(1)}, u32[]{:S(2)}, u32[]{:S(2)}) collective-permute-start(f32[112,112]{1,0:T(8,128)} %get-tuple-element.225), channel_id=1, source_target_pairs={{0,7},{1,8},{2,9},{3,10},{4,11},{5,12},{6,13},{7,14},{8,15},{9,0},... | collective-permute-start | bytes 150536 | tf_op jit(solution)/shard_map/ppermute | solution.py:511
  (14 other events, 15.9 us)
